TPU v7x, 256 devices: a whole 4x4x8 slice. The times are simulated.
256 devices in a mesh: comm: 8 (over z), stn: 16 (over y, x), tm: 2 (over core).
Axes of the slice: x: 4, y: 4, z: 8, core: 2. Of those that a mesh axis runs over, the one named last changes fastest.
Arguments:
- tiles: float32 [16, 512, 3, 128, 128], P('comm', ('stn', 'tm')), may hold values from -0.21875 to 0.21875
- cap_tiles: float32 [16, 512, 128, 128], P('comm', ('stn', 'tm')), may hold values from -0.125 to 0.125
- row_index: int32 [16, 512, 3], P('comm', ('stn', 'tm')), may hold values from 0 to 255, as said below
- cap_index: int32 [16, 512], P('comm', ('stn', 'tm')), may hold values from 0 to 15
- arc_scale: float32 [16, 512, 128], P('comm', ('stn', 'tm')), may hold values from 0.1 to 10
- rows_rhs: float32 [16, 256, 128], P('comm', ('stn', 'tm')), may hold values from -6 to 6
- cap_rhs: float32 [512, 128], P(('stn', 'tm')), may hold values from -6 to 6
- precond: float32 [16, 256, 128, 128], P('comm', ('stn', 'tm')), as said below
- cap_precond: float32 [512, 128, 128], P(('stn', 'tm')), as said below
Outputs:
- solution: float32 [16, 256, 128], P('comm', ('stn', 'tm'))
- cap_solution: float32 [512, 128], P(('stn', 'tm'))
- residual: float32 [16, 256, 128], P('comm', ('stn', 'tm'))
- cap_residual: float32 [512, 128], P(('stn', 'tm'))
Inputs may be any that keep to these rules, and one draw needn't show every extreme that they name: For arc column block j, row_index[c, j, 0] and row_index[c, j, 1] differ and lie among the 8 row blocks from (j // 16) * 8 on; row_index[c, j, 2] lies outside them. Of the third row blocks of the 16 arc blocks from (j // 16) * 16 on of one commodity, at most 1 lie in any one other range of 8 row blocks, and exactly 1 in some. `precond`: every block is symmetric positive definite. `cap_precond`: every block is symmetric positive definite.
All inputs are finite; a program needn't handle non-finite values.
Results may differ from a plain program's by a relative error of at most 0.0003.
Values sent between devices are 32-bit elements; how exact they have to be, the bound alone decides.
No kernel may reach another device: no remote copies, remote signals or barrier semaphores. Data moves between devices by JAX's collectives and lax.ppermute only.
A program may use at most 64 MiB of HBM per device.

v0:
```python
import jax
import jax.numpy as jnp
from jax import lax
from jax.sharding import PartitionSpec as P

ITERS = 3


ridge_weight = 1.0


def inner_total(row_local, cap_local):
    first = lax.psum(row_local, ("comm", "stn", "tm"))
    second = lax.psum(cap_local, ("stn", "tm"))
    return first + second


def body(
    tiles, cap_tiles, row_index, cap_index, arc_scale, rows_rhs, cap_rhs, precond, cap_precond
):
    high = lax.Precision.HIGHEST
    comm_dev, arc_blocks, touched = row_index.shape
    row_blocks = rows_rhs.shape[1]
    width = rows_rhs.shape[2]
    cap_blocks = cap_rhs.shape[0]
    group = lax.axis_size("stn") * lax.axis_size("tm")
    total_rows = row_blocks * group
    cap_onehot = (
        cap_index[:, :, None] == jnp.arange(cap_blocks, dtype=jnp.int32)[None, None, :]
    ).astype(jnp.float32)
    flat_index = row_index.reshape(comm_dev, arc_blocks * touched)
    row_onehot = (
        flat_index[:, :, None] == jnp.arange(total_rows, dtype=jnp.int32)[None, None, :]
    ).astype(jnp.float32)

    def condition(resid, cap_resid):
        zed = jnp.einsum("cqrs,cqs->cqr", precond, resid, precision=high)
        cap_zed = jnp.einsum("qrs,qs->qr", cap_precond, cap_resid, precision=high)
        return (zed, cap_zed)

    solution = jnp.zeros_like(rows_rhs)
    cap_solution = jnp.zeros_like(cap_rhs)
    residual, cap_residual = (rows_rhs, cap_rhs)
    zed, cap_zed = condition(residual, cap_residual)
    dirs_own, cap_dirs = (zed, cap_zed)
    rz_now = inner_total(jnp.sum(residual * zed), jnp.sum(cap_residual * cap_zed))
    for step in range(ITERS):
        dirs_full = lax.all_gather(dirs_own, ("stn", "tm"), axis=1, tiled=True)
        chosen = jax.vmap(lambda table, idx: table[idx])(dirs_full, row_index)
        upward = jnp.einsum("cjkra,cjkr->cja", tiles, chosen, precision=high)
        upward = upward + jnp.einsum(
            "cjra,cjr->cja", cap_tiles, cap_dirs[cap_index], precision=high
        )
        scaled = arc_scale * upward
        parts = jnp.einsum("cjkra,cja->cjkr", tiles, scaled, precision=high)
        placed = jnp.einsum(
            "cnq,cnr->cqr",
            row_onehot,
            parts.reshape(comm_dev, arc_blocks * touched, width),
            precision=high,
        )
        image = (
            lax.psum_scatter(placed, ("stn", "tm"), scatter_dimension=1, tiled=True)
            + ridge_weight * dirs_own
        )
        cap_parts = jnp.einsum("cjra,cja->cjr", cap_tiles, scaled, precision=high)
        cap_placed = jnp.einsum("cjq,cjr->qr", cap_onehot, cap_parts, precision=high)
        cap_image = lax.psum(cap_placed, "comm") + ridge_weight * cap_dirs
        image, cap_image = (image, cap_image)
        alpha = rz_now / inner_total(jnp.sum(dirs_own * image), jnp.sum(cap_dirs * cap_image))
        solution = solution + alpha * dirs_own
        cap_solution = cap_solution + alpha * cap_dirs
        residual = residual - alpha * image
        cap_residual = cap_residual - alpha * cap_image
        if step + 1 < ITERS:
            zed, cap_zed = condition(residual, cap_residual)
            rz_next = inner_total(jnp.sum(residual * zed), jnp.sum(cap_residual * cap_zed))
            ratio = rz_next / rz_now
            dirs_own = zed + ratio * dirs_own
            cap_dirs = cap_zed + ratio * cap_dirs
            rz_now = rz_next
    return (solution, cap_solution, residual, cap_residual)


def solution(mesh):
    placed = (
        P("comm", ("stn", "tm"), None, None, None),
        P("comm", ("stn", "tm"), None, None),
        P("comm", ("stn", "tm"), None),
        P("comm", ("stn", "tm")),
        P("comm", ("stn", "tm"), None),
        P("comm", ("stn", "tm"), None),
        P(("stn", "tm"), None),
        P("comm", ("stn", "tm"), None, None),
        P(("stn", "tm"), None, None),
    )
    return jax.shard_map(
        body,
        mesh=mesh,
        in_specs=placed,
        out_specs=(
            P("comm", ("stn", "tm"), None),
            P(("stn", "tm"), None),
            P("comm", ("stn", "tm"), None),
            P(("stn", "tm"), None),
        ),
        check_vma=False,
    )
```

profile of v0, /device:TPU:1, one launch (start us, length us, event | category | flops | bytes accessed | tf_op | source)
XLA Modules:
  0.0 920.8 jit_solution(11091948533044873107)
XLA Ops:
  8.8 2.9 fusion.16
  11.8 26.3 %all_gather.9 = f32[2,256,128]{2,1,0:T(8,128)S(1)} all-gather(f32[2,8,128]{2,1,0:T(8,128)S(1)} %bitcast.156), channel_id=1, replica_groups=mesh['comm'=8,'stn'=16,'tm'=2] {'stn','tm'}, dimensions={1}, use_global_device_ids=true | all-gather | bytes 270336 | tf_op jit(solution)/shard_map/all_gather | solution.py:48
  40.5 5.8 fusion.18
  48.6 1.9 fusion.19
  50.5 8.6 fusion.20
  60.7 3.4 fusion.21
  64.3 16.5 %psum.108 = f32[16,128]{1,0:T(8,128)S(1)} all-reduce(f32[16,128]{1,0:T(8,128)S(1)} %convolution_bitcast_fusion.2), channel_id=1, replica_groups=mesh['comm'=8,'stn'=16,'tm'=2] {'comm'}, use_global_device_ids=true, to_apply=%region_7.0 | all-reduce | flops 2048 | bytes 16384 | tf_op jit(solution)/shard_map/psum | solution.py:68
  81.4 66.6 %all-reduce.1 = (f32[]{:T(128)}, f32[]{:T(128)}) all-reduce(f32[]{:T(128)} %get-tuple-element.5, f32[]{:T(128)} %get-tuple-element.4), channel_id=1, replica_groups=mesh['comm'=8,'stn'=16,'tm'=2] {'stn','tm'}, use_global_device_ids=true, to_apply=%region_3.0 | all-reduce | flops 2 | bytes 16 | tf_op jit(solution)/shard_map/psum | solution.py:14
  149.3 72.6 %all-reduce = (f32[]{:T(128)}, f32[]{:T(128)}) all-reduce(f32[]{:T(128)} %get-tuple-element.7, f32[]{:T(128)} %get-tuple-element.6), channel_id=1, replica_groups=mesh['comm'=8,'stn'=16,'tm'=2] {'comm','stn','tm'}, use_global_device_ids=true, to_apply=%region_1.0 | all-reduce | flops 2 | bytes 16 | tf_op jit(solution)/shard_map/psum | solution.py:13
  224.6 1.7 fusion.22
  226.9 2.9 fusion.23
  230.5 73.5 %psum.110 = f32[]{:T(128)} all-reduce(f32[]{:T(128)} %multiply_reduce_fusion.7), channel_id=1, replica_groups=mesh['comm'=8,'stn'=16,'tm'=2] {'comm','stn','tm'}, use_global_device_ids=true, to_apply=%region_11.0 | all-reduce | flops 1 | bytes 8 | tf_op jit(solution)/shard_map/psum | solution.py:13
  304.0 63.3 %psum.111 = f32[]{:T(128)} all-reduce(f32[]{:T(128)} %multiply_reduce_fusion.6), channel_id=1, replica_groups=mesh['comm'=8,'stn'=16,'tm'=2] {'stn','tm'}, use_global_device_ids=true, to_apply=%region_13.0 | all-reduce | flops 1 | bytes 8 | tf_op jit(solution)/shard_map/psum | solution.py:14
  368.7 22.8 %all_gather.10 = f32[2,256,128]{2,1,0:T(8,128)S(1)} all-gather(f32[2,8,128]{2,1,0:T(8,128)S(1)} %multiply_add_fusion.5), channel_id=1, replica_groups=mesh['comm'=8,'stn'=16,'tm'=2] {'stn','tm'}, dimensions={1}, use_global_device_ids=true | all-gather | bytes 270336 | tf_op jit(solution)/shard_map/all_gather | solution.py:48
  392.8 5.7 fusion.24
  399.1 1.9 fusion.25
  401.0 8.6 fusion.26
  410.9 3.4 fusion.27
  414.5 11.8 %psum.113 = f32[16,128]{1,0:T(8,128)S(1)} all-reduce(f32[16,128]{1,0:T(8,128)S(1)} %convolution_bitcast_fusion.1), channel_id=1, replica_groups=mesh['comm'=8,'stn'=16,'tm'=2] {'comm'}, use_global_device_ids=true, to_apply=%region_17.0 | all-reduce | flops 2048 | bytes 16384 | tf_op jit(solution)/shard_map/psum | solution.py:68
  426.9 66.7 %psum.114 = f32[]{:T(128)} all-reduce(f32[]{:T(128)} %get-tuple-element.16), channel_id=1, replica_groups=mesh['comm'=8,'stn'=16,'tm'=2] {'stn','tm'}, use_global_device_ids=true, to_apply=%region_19.0 | all-reduce | flops 1 | bytes 8 | tf_op jit(solution)/shard_map/psum | solution.py:14
  494.9 72.4 %psum.112 = f32[]{:T(128)} all-reduce(f32[]{:T(128)} %get-tuple-element.18), channel_id=1, replica_groups=mesh['comm'=8,'stn'=16,'tm'=2] {'comm','stn','tm'}, use_global_device_ids=true, to_apply=%region_16.0 | all-reduce | flops 1 | bytes 8 | tf_op jit(solution)/shard_map/psum | solution.py:13
  571.1 2.9 fusion.29
  574.6 73.5 %psum.115 = f32[]{:T(128)} all-reduce(f32[]{:T(128)} %multiply_reduce_fusion.3), channel_id=1, replica_groups=mesh['comm'=8,'stn'=16,'tm'=2] {'comm','stn','tm'}, use_global_device_ids=true, to_apply=%region_21.0 | all-reduce | flops 1 | bytes 8 | tf_op jit(solution)/shard_map/psum | solution.py:13
  648.1 63.3 %psum.116 = f32[]{:T(128)} all-reduce(f32[]{:T(128)} %multiply_reduce_fusion.2), channel_id=1, replica_groups=mesh['comm'=8,'stn'=16,'tm'=2] {'stn','tm'}, use_global_device_ids=true, to_apply=%region_23.0 | all-reduce | flops 1 | bytes 8 | tf_op jit(solution)/shard_map/psum | solution.py:14
  712.8 22.8 %all_gather.11 = f32[2,256,128]{2,1,0:T(8,128)S(1)} all-gather(f32[2,8,128]{2,1,0:T(8,128)S(1)} %multiply_add_fusion.3), channel_id=1, replica_groups=mesh['comm'=8,'stn'=16,'tm'=2] {'stn','tm'}, dimensions={1}, use_global_device_ids=true | all-gather | bytes 270336 | tf_op jit(solution)/shard_map/all_gather | solution.py:48
  736.9 5.7 fusion.30
  743.2 1.9 fusion.31
  745.1 8.6 fusion.32
  754.9 3.4 fusion.33
  758.5 11.8 %psum.118 = f32[16,128]{1,0:T(8,128)S(1)} all-reduce(f32[16,128]{1,0:T(8,128)S(1)} %convolution_bitcast_fusion), channel_id=1, replica_groups=mesh['comm'=8,'stn'=16,'tm'=2] {'comm'}, use_global_device_ids=true, to_apply=%region_27.0 | all-reduce | flops 2048 | bytes 16384 | tf_op jit(solution)/shard_map/psum | solution.py:68
  771.0 66.7 %psum.119 = f32[]{:T(128)} all-reduce(f32[]{:T(128)} %get-tuple-element.12), channel_id=1, replica_groups=mesh['comm'=8,'stn'=16,'tm'=2] {'stn','tm'}, use_global_device_ids=true, to_apply=%region_29.0 | all-reduce | flops 1 | bytes 8 | tf_op jit(solution)/shard_map/psum | solution.py:14
  839.0 72.6 %psum.117 = f32[]{:T(128)} all-reduce(f32[]{:T(128)} %get-tuple-element.14), channel_id=1, replica_groups=mesh['comm'=8,'stn'=16,'tm'=2] {'comm','stn','tm'}, use_global_device_ids=true, to_apply=%region_26.0 | all-reduce | flops 1 | bytes 8 | tf_op jit(solution)/shard_map/psum | solution.py:13
  (71 shorter events, 26.1 us)
Async XLA Ops:
  7.2 41.4 %copy-start = (f32[2,16,128,128]{3,2,1,0:T(8,128)S(1)}, f32[2,16,128,128]{3,2,1,0:T(8,128)}, u32[]{:S(2)}) copy-start(f32[2,16,128,128]{3,2,1,0:T(8,128)} %param.10) | copy-start | bytes 6291460
  7.2 39.1 %copy-start.5 = (f32[16,128]{1,0:T(8,128)S(1)}, f32[16,128]{1,0:T(8,128)}, u32[]{:S(2)}) copy-start(f32[16,128]{1,0:T(8,128)} %param.15) | copy-start | bytes 24580
  7.2 43.3 %copy-start.3 = (f32[2,16,128]{2,1,0:T(8,128)S(1)}, f32[2,16,128]{2,1,0:T(8,128)}, u32[]{:S(2)}) copy-start(f32[2,16,128]{2,1,0:T(8,128)} %param.13) | copy-start | bytes 49156
  7.2 140.8 %reduce-scatter.4.cloned.1.call-start = ((), (), s32[]{:S(2)}) async-start(), calls=%async_computation.3 | async-start | bytes 270336 | tf_op jit(solution)/shard_map/reduce_scatter | solution.py:63
  40.4 5.8 copy-start.2
  46.3 17.8 %copy-start.6 = (s32[2,16]{1,0:T(2,128)S(1)}, s32[2,16]{1,0:T(2,128)}, u32[]{:S(2)}) copy-start(s32[2,16]{1,0:T(2,128)} %param.12) | copy-start | bytes 388
  46.3 101.7 %copy-start.4 = (f32[2,8,128]{2,1,0:T(8,128)S(1)}, f32[2,8,128]{2,1,0:T(8,128)}, u32[]{:S(2)}) copy-start(f32[2,8,128]{2,1,0:T(8,128)} %param.14) | copy-start | bytes 24580
  46.3 178.3 %copy-start.1 = (f32[2,8,128,128]{3,2,1,0:T(8,128)S(1)}, f32[2,8,128,128]{3,2,1,0:T(8,128)}, u32[]{:S(2)}) copy-start(f32[2,8,128,128]{3,2,1,0:T(8,128)} %param.16) | copy-start | bytes 3145732
  60.5 433.2 %reduce-scatter.6.cloned.1.call-start = ((), (), s32[]{:S(2)}) async-start(), calls=%async_computation.4 | async-start | bytes 270336 | tf_op jit(solution)/shard_map/reduce_scatter | solution.py:63
  410.8 426.9 %reduce-scatter.8.cloned.1.call-start = ((), (), s32[]{:S(2)}) async-start(), calls=%async_computation.5 | async-start | bytes 270336 | tf_op jit(solution)/shard_map/reduce_scatter | solution.py:63
Sparse Core Ops, SparseCore 0:
  60.6 79.6 reduce-scatter.3
  411.0 76.2 reduce-scatter.5
  755.1 76.2 reduce-scatter.7
where the time goes:
time: 930 us; the launch traced here: 921 us
  blocking collectives  803 us (86%)
  matrix products  76.8 us (8%)
  between operations  22.2 us (2%)
  other arithmetic  11 us (1%)
    psum x5, blocking collectives, inner_total(): first = lax.psum(row_local, ('comm', 'stn', 'tm'))  365 us
    psum x5, blocking collectives, inner_total(): second = lax.psum(cap_local, ('stn', 'tm'))  327 us
    all_gather x3, blocking collectives, body(): dirs_full = lax.all_gather(dirs_own, ('stn', 'tm'), axis=1, tiled=True)  71.8 us
    psum x3, blocking collectives, body(): cap_image = lax.psum(cap_placed, 'comm') + ridge_weight * cap_dirs  40.2 us
    dot_general x3, matrix products, body(): parts = jnp.einsum('cjkra,cja->cjkr', tiles, scaled, precision=high)  25.9 us
  transfers between devices with their start and end apart: 3, of which 0 were waited for; matrix products, arithmetic and copies ran while one was open for 1% of the time, Pallas kernels for 0%

commit v1 on v0

v1 whole, which is shorter than its diff:
```python
import functools

import jax
import jax.numpy as jnp
from jax import lax
from jax.experimental import pallas as pl
from jax.experimental.pallas import tpu as pltpu
from jax.sharding import PartitionSpec as P

GROUP = ("stn", "tm")
F32 = jnp.float32
SLOT = 4
NOTE = 8
VMEM = pl.BlockSpec(memory_space=pltpu.VMEM)
SMEM = pl.BlockSpec(memory_space=pltpu.SMEM)


def kept(x):
    return pltpu.with_memory_space_constraint(x, pltpu.VMEM)


def call(kernel, outs, args, scalars=0, scratch=(), aliases=None, flops=0):
    outs = [o if not isinstance(o, tuple) else jax.ShapeDtypeStruct(o, F32) for o in outs]
    return pl.pallas_call(
        kernel,
        out_shape=outs,
        in_specs=[SMEM] * scalars + [VMEM] * (len(args) - scalars),
        out_specs=[VMEM] * len(outs),
        scratch_shapes=list(scratch),
        input_output_aliases=aliases or {},
        compiler_params=pltpu.CompilerParams(vmem_limit_bytes=16 * 1024 * 1024),
        cost_estimate=pl.CostEstimate(flops=flops, bytes_accessed=4 * 1024 * 1024, transcendentals=0),
    )(*args)


def down(block, column):
    return jnp.sum(block * jnp.broadcast_to(column, block.shape), axis=0, keepdims=True)


def fold(x):
    return jnp.sum(x, axis=0, keepdims=True)


def precondition(blocks_ref, x, out_ref):
    xt = x.T
    for i in range(x.shape[0]):
        out_ref[i : i + 1] = down(blocks_ref[i], xt[:, i : i + 1])


def turn_kernel(tiles_ref, cap_tiles_ref, turned_ref):
    touched = tiles_ref.shape[1]

    def one(i, _):
        for k in range(touched):
            turned_ref[i, k] = tiles_ref[i, k].T
        turned_ref[i, touched] = cap_tiles_ref[i].T
        return 0

    lax.fori_loop(0, tiles_ref.shape[0], one, 0)


def first_kernel(rhs_ref, precond_ref, v_ref, send_ref):
    precondition(precond_ref, rhs_ref[...], v_ref)
    send_ref[...] = jnp.broadcast_to(v_ref[...][None], send_ref.shape)


def near_kernel(comms, index_ref, v_ref, tiles_ref, up_ref, wide_ref):
    rows = v_ref.shape[0]
    blocks = rows // comms
    arcs = tiles_ref.shape[0] // comms
    vt = v_ref[...].T
    for i in range(rows):
        wide_ref[i] = jnp.broadcast_to(vt[:, i : i + 1], wide_ref.shape[1:])

    def one(i, _):
        c = i // arcs
        total = jnp.zeros(wide_ref.shape[1:], F32)
        for k in range(2):
            b = c * blocks + lax.rem(index_ref[i * 3 + k], blocks)
            total = total + tiles_ref[i, k] * wide_ref[b]
        up_ref[pl.ds(i, 1)] = fold(total)
        return 0

    lax.fori_loop(0, tiles_ref.shape[0], one, 0, unroll=4)


def cap_up(cap_index_ref, q_ref, cap_tiles_ref, up_ref, out_ref, wide_ref):
    qt = q_ref[...].T
    for i in range(q_ref.shape[0]):
        wide_ref[i] = jnp.broadcast_to(qt[:, i : i + 1], wide_ref.shape[1:])

    def one(i, _):
        out_ref[pl.ds(i, 1)] = up_ref[pl.ds(i, 1)] + fold(
            cap_tiles_ref[i] * wide_ref[cap_index_ref[i]]
        )
        return 0

    lax.fori_loop(0, cap_tiles_ref.shape[0], one, 0, unroll=4)


def cap_first_kernel(
    cap_index_ref, cap_rhs_ref, up_ref, cap_precond_ref, cap_tiles_ref, q_ref, out_ref, wide_ref
):
    precondition(cap_precond_ref, cap_rhs_ref[...], q_ref)
    cap_up(cap_index_ref, q_ref, cap_tiles_ref, up_ref, out_ref, wide_ref)


def cap_second_kernel(
    cap_index_ref, cap_rhs_ref, q0_ref, half_ref, other_ref, up_ref, cap_precond_ref, cap_tiles_ref,
    yq_ref, q_ref, sums_ref, out_ref, wide_ref,
):
    caps = q0_ref.shape[0]
    note = half_ref[...] + other_ref[...]
    q0 = q0_ref[...]
    yq_ref[...] = q0 + note[:caps]
    sums_ref[...] = note[caps:]
    sums_ref[0:1] += fold(cap_rhs_ref[...] * q0)
    sums_ref[1:2] += fold(q0 * q0)
    precondition(cap_precond_ref, yq_ref[...], q_ref)
    cap_up(cap_index_ref, q_ref, cap_tiles_ref, up_ref, out_ref, wide_ref)


def cap_third_kernel(
    cap_index_ref, alpha_ref, cap_rhs_ref, q0_ref, yq0_ref, q1_ref, half_ref, other_ref, up_ref,
    cap_precond_ref, cap_tiles_ref, zq_ref, yzq_ref, rq_ref, q_ref, sums_ref, out_ref, wide_ref,
):
    caps = q0_ref.shape[0]
    alpha = alpha_ref[0:1]
    yq0, q1 = yq0_ref[...], q1_ref[...]
    yq1 = q1 + half_ref[:caps] + other_ref[:caps]
    zq = q0_ref[...] - alpha * q1
    yzq = yq0 - alpha * yq1
    rq = cap_rhs_ref[...] - alpha * yq0
    zq_ref[...] = zq
    yzq_ref[...] = yzq
    rq_ref[...] = rq
    precondition(cap_precond_ref, alpha * yzq, q_ref)
    q = q_ref[...]
    pairs = ((zq, yq0), (zq, yzq), (q, yq0), (q, yzq), (q, q), (zq, rq), (q, rq))
    for n, (one, other) in enumerate(pairs):
        sums_ref[n : n + 1] = fold(one * other)
    sums_ref[7:8] = jnp.zeros_like(sums_ref[7:8])
    cap_up(cap_index_ref, q_ref, cap_tiles_ref, up_ref, out_ref, wide_ref)


def arcs_up(comms, index_ref, blocks, up_ref, got_ref, scale_ref, tiles_ref, far_ref, scaled_ref):
    count = up_ref.shape[0]
    arcs = count // comms
    for i in range(count):
        c = i // arcs
        far = index_ref[i * 3 + 2]
        row = c if got_ref.shape[1] == comms else c * blocks + lax.rem(far, blocks)
        far_ref[i : i + 1] = got_ref[lax.div(far, blocks), pl.ds(row, 1)]
    ft = far_ref[...].T
    for i in range(count):
        far_ref[i : i + 1] = up_ref[i : i + 1] + down(tiles_ref[i, 2], ft[:, i : i + 1])
    upward = far_ref[...]
    scaled = scale_ref[...] * upward
    scaled_ref[...] = scaled
    return fold(upward * scaled)


def arcs_down(comms, index_ref, cap_index_ref, blocks, scaled_ref, turned_ref, note_ref, local_ref,
              back_ref, first):
    count = scaled_ref.shape[0]
    arcs = count // comms
    st = scaled_ref[...].T
    if back_ref is not None:
        local_ref[...] = jnp.zeros_like(local_ref)
        if first:
            back_ref[...] = jnp.full(back_ref.shape, -1.0, F32)
    for i in range(count):
        c = i // arcs
        wide = jnp.broadcast_to(st[:, i : i + 1], turned_ref.shape[2:])
        if note_ref is not None:
            cap = cap_index_ref[i]
            note_ref[pl.ds(cap, 1)] += fold(turned_ref[i, 3] * wide)
        if back_ref is None:
            continue
        for k in range(2):
            b = c * blocks + lax.rem(index_ref[i * 3 + k], blocks)
            local_ref[pl.ds(b, 1)] += fold(turned_ref[i, k] * wide)
        far = index_ref[i * 3 + 2]
        to = lax.div(far, blocks)
        back_ref[to, c : c + 1] = fold(turned_ref[i, 2] * wide)
        if first:
            local = lax.rem(far, blocks).astype(F32)
            back_ref[to, comms + c : comms + c + 1] = jnp.full((1, back_ref.shape[2]), local, F32)


def both_kernel(comms, blocks, caps, first, index_ref, cap_index_ref, rhs_ref, v_ref, sums_ref, up_ref,
                got_ref, scale_ref, tiles_ref, turned_ref, note_ref, local_ref, back_ref, far_ref,
                scaled_ref):
    energy = arcs_up(comms, index_ref, blocks, up_ref, got_ref, scale_ref, tiles_ref, far_ref, scaled_ref)
    note_ref[...] = jnp.zeros_like(note_ref)
    arcs_down(comms, index_ref, cap_index_ref, blocks, scaled_ref, turned_ref, note_ref, local_ref,
              back_ref, first)
    if first:
        v = v_ref[...]
        note_ref[caps : caps + 1] = fold(rhs_ref[...] * v)
        note_ref[caps + 1 : caps + 2] = fold(v * v) + energy
    else:
        shape = (back_ref.shape[0], 2, back_ref.shape[2])
        back_ref[:, comms : comms + 2] = jnp.broadcast_to(sums_ref[0:2][None], shape)


def last_up_kernel(comms, blocks, caps, index_ref, cap_index_ref, z_ref, yz_ref, r_ref, y0_ref, v_ref,
                   up_ref, got_ref, scale_ref, tiles_ref, turned_ref, notes_ref, scaled_ref, far_ref,
                   note_ref):
    energy = arcs_up(comms, index_ref, blocks, up_ref, got_ref, scale_ref, tiles_ref, far_ref, scaled_ref)
    note_ref[...] = jnp.zeros_like(note_ref)
    arcs_down(comms, index_ref, cap_index_ref, blocks, scaled_ref, turned_ref, note_ref, None, None, False)
    z, yz, r, y0, v = z_ref[...], yz_ref[...], r_ref[...], y0_ref[...], v_ref[...]
    pairs = ((z, y0), (z, yz), (v, y0), (v, yz), (v, v), (z, r), (v, r))
    for n, (one, other) in enumerate(pairs):
        note_ref[caps + n : caps + n + 1] = fold(one * other)
    note_ref[caps + 4 : caps + 5] += energy
    notes_ref[...] = jnp.broadcast_to(note_ref[...][None], notes_ref.shape)


def last_down_kernel(comms, blocks, index_ref, scaled_ref, turned_ref, local_ref, back_ref):
    arcs_down(comms, index_ref, None, blocks, scaled_ref, turned_ref, None, local_ref, back_ref, False)


def insert_kernel(comms, caps, notes_ref, sums_ref, back_ref, cap_ref, out_ref):
    del back_ref
    total = jnp.sum(notes_ref[...], axis=0)
    cap_ref[...] = total[:caps]
    sums = jnp.sum(total[caps:] + sums_ref[...], axis=1, keepdims=True)
    width = out_ref.shape[2]
    pick = lax.broadcasted_iota(jnp.int32, (NOTE, width), 0) == lax.broadcasted_iota(
        jnp.int32, (NOTE, width), 1
    )
    row = fold(jnp.where(pick, jnp.broadcast_to(sums, (NOTE, width)), 0.0))
    out_ref[:, comms : comms + 1] = jnp.broadcast_to(row[None], (out_ref.shape[0], 1, width))


def collect(comms, v_ref, local_ref, back_ref, asked, y_ref):
    blocks = v_ref.shape[0] // comms
    for c in range(comms):
        part = back_ref[:, c]
        for b in range(blocks):
            n = c * blocks + b
            came = fold(jnp.where(asked[c] == b, part, 0.0))
            y_ref[n : n + 1] = v_ref[n : n + 1] + local_ref[n : n + 1] + came


def pack(comms, v_ref, asked, send_ref):
    blocks = v_ref.shape[0] // comms
    for c in range(comms):
        row = jnp.zeros_like(asked[c])
        for b in range(blocks):
            n = c * blocks + b
            row = jnp.where(asked[c] == b, v_ref[n : n + 1], row)
        send_ref[:, c] = row


def rows_second_kernel(comms, v0_ref, local_ref, back_ref, precond_ref, y_ref, v_ref, send_ref, asked_ref):
    asked = [back_ref[:, comms + c] for c in range(comms)]
    for c in range(comms):
        asked_ref[c] = asked[c]
    collect(comms, v0_ref, local_ref, back_ref, asked, y_ref)
    precondition(precond_ref, y_ref[...], v_ref)
    pack(comms, v_ref, asked, send_ref)


def rows_third_kernel(comms, rhs_ref, v0_ref, y0_ref, v1_ref, local_ref, back_ref, asked_ref, precond_ref,
                      alpha_ref, z_ref, yz_ref, r_ref, v_ref, send_ref):
    asked = [asked_ref[c] for c in range(comms)]
    collect(comms, v1_ref, local_ref, back_ref, asked, yz_ref)
    first = jnp.sum(fold(back_ref[:, comms]), axis=1, keepdims=True)
    second = jnp.sum(fold(back_ref[:, comms + 1]), axis=1, keepdims=True)
    alpha = jnp.broadcast_to(first / second, (1, alpha_ref.shape[1]))
    alpha_ref[...] = jnp.broadcast_to(alpha, alpha_ref.shape)
    alpha_ref[1:2] = jnp.broadcast_to(second, (1, alpha_ref.shape[1]))
    y0 = y0_ref[...]
    z_ref[...] = v0_ref[...] - alpha * v1_ref[...]
    yz = y0 - alpha * yz_ref[...]
    yz_ref[...] = yz
    r_ref[...] = rhs_ref[...] - alpha * y0
    precondition(precond_ref, alpha * yz, v_ref)
    pack(comms, v_ref, asked, send_ref)


def last_kernel(comms, alpha_ref, v0_ref, y0_ref, z_ref, yz_ref, r_ref, v2_ref, local_ref, back_ref,
                asked_ref, q0_ref, yq0_ref, zq_ref, yzq_ref, rq_ref, q2_ref, cap_ref,
                sol_ref, cap_sol_ref, res_ref, cap_res_ref, y_ref):
    asked = [asked_ref[c] for c in range(comms)]
    collect(comms, v2_ref, local_ref, back_ref, asked, y_ref)
    row = fold(back_ref[:, comms])
    width = row.shape[1]
    lane = lax.broadcasted_iota(jnp.int32, row.shape, 1)
    s = [
        jnp.broadcast_to(
            jnp.sum(jnp.where(lane == n, row, 0.0), axis=1, keepdims=True), (1, width)
        )
        for n in range(7)
    ]
    alpha, h00 = alpha_ref[0:1], alpha_ref[1:2]
    h1, h2 = s[0] / h00, s[2] / h00
    a11 = s[1] - h1 * s[0]
    a12 = s[3] - h1 * s[2]
    a22 = s[4] - h2 * s[2]
    lower = a12 / a11
    c2 = (s[6] - lower * s[5]) / (a22 - lower * a12)
    c1 = s[5] / a11 - lower * c2
    c0 = c1 * h1 + c2 * h2
    sol_ref[...] = (alpha - c0) * v0_ref[...] + c1 * z_ref[...] + c2 * v2_ref[...]
    cap_sol_ref[...] = (alpha - c0) * q0_ref[...] + c1 * zq_ref[...] + c2 * q2_ref[...]
    res_ref[...] = r_ref[...] + c0 * y0_ref[...] - c1 * yz_ref[...] - c2 * y_ref[...]
    yq2 = q2_ref[...] + cap_ref[...]
    cap_res_ref[...] = rq_ref[...] + c0 * yq0_ref[...] - c1 * yzq_ref[...] - c2 * yq2


def body(
    tiles, cap_tiles, row_index, cap_index, arc_scale, rows_rhs, cap_rhs, precond, cap_precond
):
    comms, arcs, touched = row_index.shape
    blocks, width = rows_rhs.shape[1:]
    caps = cap_rhs.shape[0]
    groups = lax.axis_size("stn") * lax.axis_size("tm")
    peers = lax.axis_size("comm")
    rows, count = comms * blocks, comms * arcs
    flat = (width, width)
    tiles = kept(tiles.reshape(count, touched, *flat))
    cap_tiles = kept(cap_tiles.reshape(count, *flat))
    precond = kept(precond.reshape(rows, *flat))
    cap_precond = kept(cap_precond)
    index = row_index.reshape(-1)
    cap_index = cap_index.reshape(-1)
    scale = arc_scale.reshape(count, width)
    rhs = rows_rhs.reshape(rows, width)
    row_shape, cap_shape, arc_shape = (rows, width), (caps, width), (count, width)
    wide_rows = pltpu.VMEM((rows, *flat), F32)
    wide_caps = pltpu.VMEM((caps, *flat), F32)
    arc_scratch = pltpu.VMEM(arc_shape, F32)
    small = (NOTE, width)
    note_shape = (caps + NOTE, width)
    send_shape = (groups, comms, width)
    back_shape = (groups, SLOT, width)
    near_flops, far_flops = 2 * count * width * width, 10 * count * width * width

    def exchange(x):
        return lax.all_to_all(x, GROUP, 0, 0)

    def near(v):
        (up,) = call(
            functools.partial(near_kernel, comms), [arc_shape], (index, v, tiles), 1, [wide_rows],
            flops=near_flops,
        )
        return up

    def across(x, step):
        return lax.ppermute(x, "comm", [(i, i ^ step) for i in range(peers)])

    v0, send = call(first_kernel, [row_shape, (groups, rows, width)], (rhs, precond))
    got = exchange(send)
    (turned,) = call(
        turn_kernel, [pltpu.VMEM((count, touched + 1, *flat), F32)], (tiles, cap_tiles), flops=far_flops
    )
    turned = kept(turned)
    up = near(v0)
    q0, up = call(
        cap_first_kernel, [cap_shape, arc_shape], (cap_index, cap_rhs, up, cap_precond, cap_tiles), 1,
        [wide_caps], flops=near_flops,
    )

    def both(first, v, sums, up, got):
        return call(
            functools.partial(both_kernel, comms, blocks, caps, first),
            [note_shape, row_shape, back_shape],
            (index, cap_index, rhs, v, sums, up, got, scale, tiles, turned),
            2,
            [arc_scratch, arc_scratch],
            flops=far_flops,
        )

    note, local, back = both(True, v0, rhs, up, got)
    back = exchange(back)
    note = note + across(note, 1)
    note = note + across(note, 2)
    y0, v1, send, asked = call(
        functools.partial(rows_second_kernel, comms),
        [row_shape, row_shape, send_shape, (comms, groups, width)],
        (v0, local, back, precond),
    )
    got = exchange(send)
    other = across(note, 4)
    up = near(v1)
    yq0, q1, sums, up = call(
        cap_second_kernel, [cap_shape, cap_shape, small, arc_shape],
        (cap_index, cap_rhs, q0, note, other, up, cap_precond, cap_tiles), 1, [wide_caps],
        flops=near_flops,
    )
    note, local, back = both(False, v1, sums, up, got)
    back = exchange(back)
    note = note + across(note, 1)
    note = note + across(note, 2)
    alpha, z1, yz, r1, v2, send = call(
        functools.partial(rows_third_kernel, comms),
        [small, row_shape, row_shape, row_shape, row_shape, send_shape],
        (rhs, v0, y0, v1, local, back, asked, precond),
    )
    got = exchange(send)
    other = across(note, 4)
    up = near(v2)
    zq1, yzq, rq1, q2, sums, up = call(
        cap_third_kernel, [cap_shape] * 4 + [small, arc_shape],
        (cap_index, alpha, cap_rhs, q0, yq0, q1, note, other, up, cap_precond, cap_tiles), 1, [wide_caps],
        flops=near_flops,
    )
    notes, scaled = call(
        functools.partial(last_up_kernel, comms, blocks, caps),
        [(peers, *note_shape), arc_shape],
        (index, cap_index, z1, yz, r1, y0, v2, up, got, scale, tiles, turned), 2,
        [arc_scratch, pltpu.VMEM(note_shape, F32)],
        flops=near_flops,
    )
    notes = lax.all_to_all(notes, "comm", 0, 0)
    local, back = call(
        functools.partial(last_down_kernel, comms, blocks), [row_shape, back_shape],
        (index, scaled, turned), 1, flops=far_flops,
    )
    cap_sum, back = call(
        functools.partial(insert_kernel, comms, caps), [cap_shape, back_shape], (notes, sums, back),
        aliases={2: 1},
    )
    back = exchange(back)
    sol, cap_sol, res, cap_res = call(
        functools.partial(last_kernel, comms), [row_shape, cap_shape, row_shape, cap_shape],
        (alpha, v0, y0, z1, yz, r1, v2, local, back, asked, q0, yq0, zq1, yzq, rq1, q2, cap_sum), 0,
        [pltpu.VMEM(row_shape, F32)],
    )
    return sol.reshape(rows_rhs.shape), cap_sol, res.reshape(rows_rhs.shape), cap_res


def solution(mesh):
    placed = (
        P("comm", GROUP, None, None, None),
        P("comm", GROUP, None, None),
        P("comm", GROUP, None),
        P("comm", GROUP),
        P("comm", GROUP, None),
        P("comm", GROUP, None),
        P(GROUP, None),
        P("comm", GROUP, None, None),
        P(GROUP, None, None),
    )
    return jax.shard_map(
        body,
        mesh=mesh,
        in_specs=placed,
        out_specs=(
            P("comm", GROUP, None),
            P(GROUP, None),
            P("comm", GROUP, None),
            P(GROUP, None),
        ),
        check_vma=False,
    )
```

time: 930 us -> 159 us (0.17)
  blocking collectives: 803 us -> 17.2 us
  matrix products: 76.8 us -> 0 us
  starting transfers between devices: 0.33 us -> 52.3 us
  local copies, waits for them, and re-layouts: 7.19 us -> 38.7 us
  Pallas kernels: 0 us -> 30.1 us
  between operations: 22.2 us -> 0.92 us
  waiting for transfers between devices: 0.05 us -> 19 us
  other arithmetic: 11 us -> 0.02 us
    psum x13 -> x0, blocking collectives: 731 us -> none  [the longest x5 365 us: inner_total(): first = lax.psum(row_local, ('comm', 'stn', 'tm'))]
    dot_general x24 -> x0, matrix products: 76.8 us -> none  [the longest x3 25.9 us: body(): parts = jnp.einsum('cjkra,cja->cjkr', tiles, scaled, precision=high)]
    all_gather x3 -> x0, blocking collectives: 71.8 us -> none  [body(): dirs_full = lax.all_gather(dirs_own, ('stn', 'tm'), axis=1, tiled=True)]
    unnamed x15 -> x47, local copies, waits for them, and re-layouts: 0.81 us -> 37.9 us
    all_to_all x0 -> x6, starting transfers between devices: none -> 36.3 us  [the longest x5 32.4 us: exchange(): return lax.all_to_all(x, GROUP, 0, 0)]
    pallas_call x0 -> x16, Pallas kernels: none -> 30.1 us  [call(): pl.pallas_call(kernel, out_shape=outs, in_specs=[SMEM] * scalars + [VMEM]...]
    all_to_all x0 -> x1, blocking collectives: none -> 17.2 us  [exchange(): return lax.all_to_all(x, GROUP, 0, 0)]
    ppermute x0 -> x6, starting transfers between devices: none -> 16 us  [across(): return lax.ppermute(x, 'comm', [(i, i ^ step) for i in range(peers)])]
  transfers between devices with their start and end apart: 3 -> 12, of which waited for: 0 -> 5; matrix products, arithmetic and copies ran while one was open for 1% -> 1% of each run, Pallas kernels for 0% -> 12%
where the time goes in v1:
time: 159 us; the launch traced here: 158 us
  starting transfers between devices  52.3 us (33%)
  local copies, waits for them, and re-layouts  38.7 us (24%)
  Pallas kernels  30.1 us (19%)
  waiting for transfers between devices  19 us (12%)
  blocking collectives  17.2 us (11%)
    unnamed x47, local copies, waits for them, and re-layouts  37.9 us
    all_to_all x5, starting transfers between devices, exchange(): return lax.all_to_all(x, GROUP, 0, 0)  32.4 us
    pallas_call x16, Pallas kernels, call(): pl.pallas_call(kernel, out_shape=outs, in_specs=[SMEM] * scalars + [VMEM]...  30.1 us
    all_to_all x1, blocking collectives, exchange(): return lax.all_to_all(x, GROUP, 0, 0)  17.2 us
    ppermute x6, starting transfers between devices, across(): return lax.ppermute(x, 'comm', [(i, i ^ step) for i in range(peers)])  16 us
    all_to_all x5, waiting for transfers between devices, exchange(): return lax.all_to_all(x, GROUP, 0, 0)  12.1 us
    ppermute x6, waiting for transfers between devices, across(): return lax.ppermute(x, 'comm', [(i, i ^ step) for i in range(peers)])  3.93 us
    all_to_all x1, starting transfers between devices, body(): notes = lax.all_to_all(notes, 'comm', 0, 0)  3.88 us
  transfers between devices with their start and end apart: 12, of which 5 were waited for; matrix products, arithmetic and copies ran while one was open for 1% of the time, Pallas kernels for 12%

profile of v1, /device:TPU:1, one launch (start us, length us, event | category | flops | bytes accessed | tf_op | source)
XLA Modules:
  0.0 158.2 jit_solution(5779189939217378781)
XLA Ops:
  3.8 8.6 %all-to-all-start = ((f32[32,16,128]{2,1,0:T(8,128)}), f32[32,16,128]{2,1,0:T(8,128)S(1)}, u32[]{:S(2)}, u32[]{:S(2)}) async-start(f32[32,16,128]{2,1,0:T(8,128)} %get-tuple-element.46), calls=%async_computation | async-start | bytes 524288 | tf_op jit(solution)/shard_map/all_to_all | solution.py:344
  14.0 2.8 %copy-done = f32[2,16,3,128,128]{4,3,2,1,0:T(8,128)S(1)} copy-done((f32[2,16,3,128,128]{4,3,2,1,0:T(8,128)S(1)}, f32[2,16,3,128,128]{4,3,2,1,0:T(8,128)}, u32[]{:S(2)}) %copy-start) | copy-done | bytes 6291480
  20.2 1.8 %shard_map.122 = (f32[16,128]{1,0:T(8,128)S(1)}, f32[32,128]{1,0:T(8,128)S(1)}) custom-call(s32[32]{0:T(128)S(1)} %reshape.38.cap_index_ref, f32[16,128]{1,0:T(8,128)S(1)} %copy-done.22, f32[32,128]{1,0:T(8,128)S(1)} %shard_map.121.up_ref, f32[16,128,128]{2,1,0:T(8,128)S(1)} %copy-done.16, f32[32,128,128]{2,1,0:T(8,128)S(1)} %bitcast.14), custom_call_target="tpu_custom_call" | custom-call | flops 1048576 | bytes 4194304 | tf_op jit(solution)/shard_map/pallas_call | solution.py:24
  22.1 4.5 %shard_map.123.turned_ref = f32[32,4,128,128]{3,2,1,0:T(8,128)S(1)} custom-call(f32[32,3,128,128]{3,2,1,0:T(8,128)S(1)} %bitcast.8, f32[32,128,128]{2,1,0:T(8,128)S(1)} %bitcast.15), custom_call_target="tpu_custom_call" | custom-call | flops 5242880 | bytes 4194304 | tf_op jit(solution)/shard_map/pallas_call | solution.py:24
  26.5 3.3 %copy-done.7 = f32[32,4,128,128]{3,2,1,0:T(8,128)} copy-done((f32[32,4,128,128]{3,2,1,0:T(8,128)}, f32[32,4,128,128]{3,2,1,0:T(8,128)S(1)}, u32[]{:S(2)}) %copy-start.7) | copy-done | bytes 8388632
  29.9 2.8 %copy-done.2 = f32[2,16,3,128,128]{4,3,2,1,0:T(8,128)S(1)} copy-done((f32[2,16,3,128,128]{4,3,2,1,0:T(8,128)S(1)}, f32[2,16,3,128,128]{4,3,2,1,0:T(8,128)}, u32[]{:S(2)}) %copy-start.2) | copy-done | bytes 6291480
  32.6 3.4 %copy-done.8 = f32[32,4,128,128]{3,2,1,0:T(8,128)S(1)} copy-done((f32[32,4,128,128]{3,2,1,0:T(8,128)S(1)}, f32[32,4,128,128]{3,2,1,0:T(8,128)}, u32[]{:S(2)}) %copy-start.8) | copy-done | bytes 8388632
  36.0 3.1 %shard_map.124 = (f32[24,128]{1,0:T(8,128)S(1)}, f32[16,128]{1,0:T(8,128)S(1)}, f32[32,4,128]{2,1,0:T(4,128)}) custom-call(s32[96]{0:T(128)S(1)} %reshape.37.index_ref, s32[32]{0:T(128)S(1)} %reshape.38.cap_index_ref, f32[16,128]{1,0:T(8,128)S(1)} %bitcast.22, f32[16,128]{1,0:T(8,128)S(1)} %get-tuple-element.44.v_ref.v0_ref, f32[16,128]{1,0:T(8,128)S(1)} %bitcast.23, ...), custom_call_target="tpu_custom_call" | custom-call | flops 5242880 | bytes 4194304 | tf_op jit(solution)/shard_map/pallas_call | solution.py:24
  39.1 7.4 %all-to-all-start.1 = ((f32[32,4,128]{2,1,0:T(4,128)}), f32[32,4,128]{2,1,0:T(4,128)S(1)}, u32[]{:S(2)}, u32[]{:S(2)}) async-start(f32[32,4,128]{2,1,0:T(4,128)} %get-tuple-element.48), calls=%async_computation.1 | async-start | bytes 131072 | tf_op jit(solution)/shard_map/all_to_all | solution.py:344
  48.2 5.6 %all-to-all-done.1.back_ref = f32[32,4,128]{2,1,0:T(4,128)S(1)} async-done(((f32[32,4,128]{2,1,0:T(4,128)}), f32[32,4,128]{2,1,0:T(4,128)S(1)}, u32[]{:S(2)}, u32[]{:S(2)}) %all-to-all-start.1) | async-done | bytes 65568 | tf_op jit(solution)/shard_map/all_to_all | solution.py:344
  55.4 3.8 %all-to-all-start.2 = ((f32[32,2,128]{2,1,0:T(2,128)}), f32[32,2,128]{2,1,0:T(2,128)S(1)}, u32[]{:S(2)}, u32[]{:S(2)}) async-start(f32[32,2,128]{2,1,0:T(2,128)} %get-tuple-element.55), calls=%async_computation.2 | async-start | bytes 65536 | tf_op jit(solution)/shard_map/all_to_all | solution.py:344
  59.2 3.1 %collective-permute-start.1 = (f32[24,128]{1,0:T(8,128)S(1)}, f32[24,128]{1,0:T(8,128)S(1)}, u32[]{:S(2)}, u32[]{:S(2)}) collective-permute-start(f32[24,128]{1,0:T(8,128)S(1)} %add.12), channel_id=1, source_target_pairs={{0,64},{32,96},{64,0},{96,32},{128,192},{160,224},{192,128},{224,1... | collective-permute-start | bytes 36872 | tf_op jit(solution)/shard_map/ppermute | solution.py:354
  63.7 6.3 %collective-permute-start.2 = (f32[24,128]{1,0:T(8,128)S(1)}, f32[24,128]{1,0:T(8,128)S(1)}, u32[]{:S(2)}, u32[]{:S(2)}) collective-permute-start(f32[24,128]{1,0:T(8,128)S(1)} %add.13.half_ref), channel_id=1, source_target_pairs={{0,128},{32,160},{64,192},{96,224},{128,0},{160,32},{192,64},{224,... | collective-permute-start | bytes 36872 | tf_op jit(solution)/shard_map/ppermute | solution.py:354
  70.0 2.8 %copy-done.3 = f32[2,16,3,128,128]{4,3,2,1,0:T(8,128)S(1)} copy-done((f32[2,16,3,128,128]{4,3,2,1,0:T(8,128)S(1)}, f32[2,16,3,128,128]{4,3,2,1,0:T(8,128)}, u32[]{:S(2)}) %copy-start.3) | copy-done | bytes 6291480
  74.5 1.8 %shard_map.127 = (f32[16,128]{1,0:T(8,128)S(1)}, f32[16,128]{1,0:T(8,128)S(1)}, f32[8,128]{1,0:T(8,128)S(1)}, f32[32,128]{1,0:T(8,128)S(1)}) custom-call(s32[32]{0:T(128)S(1)} %reshape.38.cap_index_ref, f32[16,128]{1,0:T(8,128)S(1)} %copy-done.22, f32[16,128]{1,0:T(8,128)S(1)} %get-tuple-element.51.q0_ref, f32[24,128]{1,0:T(8,128)S(1)} %add.13.half_ref, ...), custom_call_target="tpu_custom_call" | custom-call | flops 1048576 | bytes 4194304 | tf_op jit(solution)/shard_map/pallas_call | solution.py:24
  76.4 2.8 %copy-done.4 = f32[2,16,3,128,128]{4,3,2,1,0:T(8,128)S(1)} copy-done((f32[2,16,3,128,128]{4,3,2,1,0:T(8,128)S(1)}, f32[2,16,3,128,128]{4,3,2,1,0:T(8,128)}, u32[]{:S(2)}) %copy-start.4) | copy-done | bytes 6291480
  79.1 3.4 %copy-done.9 = f32[32,4,128,128]{3,2,1,0:T(8,128)S(1)} copy-done((f32[32,4,128,128]{3,2,1,0:T(8,128)S(1)}, f32[32,4,128,128]{3,2,1,0:T(8,128)}, u32[]{:S(2)}) %copy-start.9) | copy-done | bytes 8388632
  82.5 2.9 %shard_map.128 = (f32[24,128]{1,0:T(8,128)S(1)}, f32[16,128]{1,0:T(8,128)S(1)}, f32[32,4,128]{2,1,0:T(4,128)}) custom-call(s32[96]{0:T(128)S(1)} %reshape.37.index_ref, s32[32]{0:T(128)S(1)} %reshape.38.cap_index_ref, f32[16,128]{1,0:T(8,128)S(1)} %bitcast.24, f32[16,128]{1,0:T(8,128)S(1)} %get-tuple-element.50.v_ref.v1_ref, ...), custom_call_target="tpu_custom_call" | custom-call | flops 5242880 | bytes 4194304 | tf_op jit(solution)/shard_map/pallas_call | solution.py:24
  85.4 8.6 %all-to-all-start.3 = ((f32[32,4,128]{2,1,0:T(4,128)}), f32[32,4,128]{2,1,0:T(4,128)S(1)}, u32[]{:S(2)}, u32[]{:S(2)}) async-start(f32[32,4,128]{2,1,0:T(4,128)} %get-tuple-element.57), calls=%async_computation.3 | async-start | bytes 131072 | tf_op jit(solution)/shard_map/all_to_all | solution.py:344
  94.9 6.5 %all-to-all-done.3.back_ref = f32[32,4,128]{2,1,0:T(4,128)S(1)} async-done(((f32[32,4,128]{2,1,0:T(4,128)}), f32[32,4,128]{2,1,0:T(4,128)S(1)}, u32[]{:S(2)}, u32[]{:S(2)}) %all-to-all-start.3) | async-done | bytes 65568 | tf_op jit(solution)/shard_map/all_to_all | solution.py:344
  102.6 4.0 %all-to-all-start.4 = ((f32[32,2,128]{2,1,0:T(2,128)}), f32[32,2,128]{2,1,0:T(2,128)S(1)}, u32[]{:S(2)}, u32[]{:S(2)}) async-start(f32[32,2,128]{2,1,0:T(2,128)} %get-tuple-element.68), calls=%async_computation.4 | async-start | bytes 65536 | tf_op jit(solution)/shard_map/all_to_all | solution.py:344
  107.9 2.5 %collective-permute-done.4 = f32[24,128]{1,0:T(8,128)S(1)} collective-permute-done((f32[24,128]{1,0:T(8,128)S(1)}, f32[24,128]{1,0:T(8,128)S(1)}, u32[]{:S(2)}, u32[]{:S(2)}) %collective-permute-start.4) | collective-permute-done | bytes 12320 | tf_op jit(solution)/shard_map/ppermute | solution.py:354
  110.5 2.8 %collective-permute-start.5 = (f32[24,128]{1,0:T(8,128)S(1)}, f32[24,128]{1,0:T(8,128)S(1)}, u32[]{:S(2)}, u32[]{:S(2)}) collective-permute-start(f32[24,128]{1,0:T(8,128)S(1)} %add.15.half_ref), channel_id=1, source_target_pairs={{0,128},{32,160},{64,192},{96,224},{128,0},{160,32},{192,64},{224,... | collective-permute-start | bytes 36872 | tf_op jit(solution)/shard_map/ppermute | solution.py:354
  113.3 2.8 %copy-done.5 = f32[2,16,3,128,128]{4,3,2,1,0:T(8,128)S(1)} copy-done((f32[2,16,3,128,128]{4,3,2,1,0:T(8,128)S(1)}, f32[2,16,3,128,128]{4,3,2,1,0:T(8,128)}, u32[]{:S(2)}) %copy-start.5) | copy-done | bytes 6291480
  117.8 1.8 %shard_map.131 = (f32[16,128]{1,0:T(8,128)S(1)}, f32[16,128]{1,0:T(8,128)S(1)}, f32[16,128]{1,0:T(8,128)S(1)}, f32[16,128]{1,0:T(8,128)S(1)}, f32[8,128]{1,0:T(8,128)S(1)}, /*index=5*/f32[32,128]{1,0:T(8,128)S(1)}) custom-call(s32[32]{0:T(128)S(1)} %reshape.38.cap_index_ref, f32[8,128]{1,0:T(8,128)S(1)} %get-tuple-element.59.alpha_ref, ...), custom_call_target="tpu_custom_call" | custom-call | flops 1048576 | bytes 4194304 | tf_op jit(solution)/shard_map/pallas_call | solution.py:24
  119.6 2.8 %copy-done.6 = f32[2,16,3,128,128]{4,3,2,1,0:T(8,128)S(1)} copy-done((f32[2,16,3,128,128]{4,3,2,1,0:T(8,128)S(1)}, f32[2,16,3,128,128]{4,3,2,1,0:T(8,128)}, u32[]{:S(2)}) %copy-start.6) | copy-done | bytes 6291480
  122.4 3.4 %copy-done.10 = f32[32,4,128,128]{3,2,1,0:T(8,128)S(1)} copy-done((f32[32,4,128,128]{3,2,1,0:T(8,128)S(1)}, f32[32,4,128,128]{3,2,1,0:T(8,128)}, u32[]{:S(2)}) %copy-start.10) | copy-done | bytes 8388632
  125.8 2.8 %shard_map.132 = (f32[8,24,128]{2,1,0:T(8,128)}, f32[32,128]{1,0:T(8,128)S(1)}) custom-call(s32[96]{0:T(128)S(1)} %reshape.37.index_ref, s32[32]{0:T(128)S(1)} %reshape.38.cap_index_ref, f32[16,128]{1,0:T(8,128)S(1)} %get-tuple-element.60.z_ref, f32[16,128]{1,0:T(8,128)S(1)} %get-tuple-element.61.yz_ref, f32[16,128]{1,0:T(8,128)S(1)} %get-tuple-element.62.r_ref, ...), custom_call_target="tpu_custom_call" | custom-call | flops 1048576 | bytes 4194304 | tf_op jit(solution)/shard_map/pallas_call | solution.py:24
  128.6 3.9 %all-to-all-start.5 = ((f32[8,24,128]{2,1,0:T(8,128)}), f32[8,24,128]{2,1,0:T(8,128)S(1)}, u32[]{:S(2)}, u32[]{:S(2)}) async-start(f32[8,24,128]{2,1,0:T(8,128)} %get-tuple-element.71), calls=%async_computation.5 | async-start | bytes 196608 | tf_op jit(solution)/shard_map/all_to_all | solution.py:419
  132.5 3.4 %copy-done.11 = f32[32,4,128,128]{3,2,1,0:T(8,128)S(1)} copy-done((f32[32,4,128,128]{3,2,1,0:T(8,128)S(1)}, f32[32,4,128,128]{3,2,1,0:T(8,128)}, u32[]{:S(2)}) %copy-start.11) | copy-done | bytes 8388632
  137.2 2.9 %all-to-all-done.5.notes_ref = f32[8,24,128]{2,1,0:T(8,128)S(1)} async-done(((f32[8,24,128]{2,1,0:T(8,128)}), f32[8,24,128]{2,1,0:T(8,128)S(1)}, u32[]{:S(2)}, u32[]{:S(2)}) %all-to-all-start.5) | async-done | bytes 98336 | tf_op jit(solution)/shard_map/all_to_all | solution.py:419
  140.3 17.2 %all_to_all.35.back_ref = f32[32,4,128]{2,1,0:T(4,128)S(1)} all-to-all(f32[32,4,128]{2,1,0:T(4,128)S(1)} %get-tuple-element.74), channel_id=1, replica_groups=mesh['comm'=8,'stn'=16,'tm'=2] {'stn','tm'}, dimensions={0} | all-to-all | bytes 131072 | tf_op jit(solution)/shard_map/all_to_all | solution.py:344
  (62 shorter events, 21.9 us)
Async XLA Ops:
  2.6 15.9 %copy-start.16 = (f32[16,128,128]{2,1,0:T(8,128)S(1)}, f32[16,128,128]{2,1,0:T(8,128)}, u32[]{:S(2)}) copy-start(f32[16,128,128]{2,1,0:T(8,128)} %cap_precond_ref.5) | copy-start | bytes 3145732
  2.6 15.9 %copy-start.22 = (f32[16,128]{1,0:T(8,128)S(1)}, f32[16,128]{1,0:T(8,128)}, u32[]{:S(2)}) copy-start(f32[16,128]{1,0:T(8,128)} %cap_rhs_ref.5) | copy-start | bytes 24580
  3.8 26.1 %all-to-all-start = ((f32[32,16,128]{2,1,0:T(8,128)}), f32[32,16,128]{2,1,0:T(8,128)S(1)}, u32[]{:S(2)}, u32[]{:S(2)}) async-start(f32[32,16,128]{2,1,0:T(8,128)} %get-tuple-element.46), calls=%async_computation | async-start | bytes 524288 | tf_op jit(solution)/shard_map/all_to_all | solution.py:344
  14.0 2.8 %copy-start = (f32[2,16,3,128,128]{4,3,2,1,0:T(8,128)S(1)}, f32[2,16,3,128,128]{4,3,2,1,0:T(8,128)}, u32[]{:S(2)}) copy-start(f32[2,16,3,128,128]{4,3,2,1,0:T(8,128)} %param.9) | copy-start | bytes 18874372
  16.8 5.2 %copy-start.1 = (f32[2,16,3,128,128]{4,3,2,1,0:T(8,128)S(1)}, f32[2,16,3,128,128]{4,3,2,1,0:T(8,128)}, u32[]{:S(2)}) copy-start(f32[2,16,3,128,128]{4,3,2,1,0:T(8,128)} %param.9) | copy-start | bytes 18874372
  22.0 7.8 %copy-start.20 = (f32[2,8,128]{2,1,0:T(8,128)S(1)}, f32[2,8,128]{2,1,0:T(8,128)}, u32[]{:S(2)}) copy-start(f32[2,8,128]{2,1,0:T(8,128)} %param.14) | copy-start | bytes 24580
  22.1 7.8 %copy-start.21 = (f32[2,16,128]{2,1,0:T(8,128)S(1)}, f32[2,16,128]{2,1,0:T(8,128)}, u32[]{:S(2)}) copy-start(f32[2,16,128]{2,1,0:T(8,128)} %param.13) | copy-start | bytes 49156
  26.5 3.3 %copy-start.7 = (f32[32,4,128,128]{3,2,1,0:T(8,128)}, f32[32,4,128,128]{3,2,1,0:T(8,128)S(1)}, u32[]{:S(2)}) copy-start(f32[32,4,128,128]{3,2,1,0:T(8,128)S(1)} %shard_map.123.turned_ref) | copy-start | bytes 25165828
  29.8 2.8 %copy-start.2 = (f32[2,16,3,128,128]{4,3,2,1,0:T(8,128)S(1)}, f32[2,16,3,128,128]{4,3,2,1,0:T(8,128)}, u32[]{:S(2)}) copy-start(f32[2,16,3,128,128]{4,3,2,1,0:T(8,128)} %param.9) | copy-start | bytes 18874372
  32.6 3.4 %copy-start.8 = (f32[32,4,128,128]{3,2,1,0:T(8,128)S(1)}, f32[32,4,128,128]{3,2,1,0:T(8,128)}, u32[]{:S(2)}) copy-start(f32[32,4,128,128]{3,2,1,0:T(8,128)} %copy-done.7) | copy-start | bytes 25165828
  36.0 17.8 %copy-start.15 = (f32[2,8,128,128]{3,2,1,0:T(8,128)S(1)}, f32[2,8,128,128]{3,2,1,0:T(8,128)}, u32[]{:S(2)}) copy-start(f32[2,8,128,128]{3,2,1,0:T(8,128)} %param.16) | copy-start | bytes 3145732
  36.0 38.5 %copy-start.13 = (f32[2,16,128,128]{3,2,1,0:T(8,128)S(1)}, f32[2,16,128,128]{3,2,1,0:T(8,128)}, u32[]{:S(2)}) copy-start(f32[2,16,128,128]{3,2,1,0:T(8,128)} %param.10) | copy-start | bytes 6291460
  39.1 14.7 %all-to-all-start.1 = ((f32[32,4,128]{2,1,0:T(4,128)}), f32[32,4,128]{2,1,0:T(4,128)S(1)}, u32[]{:S(2)}, u32[]{:S(2)}) async-start(f32[32,4,128]{2,1,0:T(4,128)} %get-tuple-element.48), calls=%async_computation.1 | async-start | bytes 131072 | tf_op jit(solution)/shard_map/all_to_all | solution.py:344
  46.5 12.8 %collective-permute-start = (f32[24,128]{1,0:T(8,128)S(1)}, f32[24,128]{1,0:T(8,128)S(1)}, u32[]{:S(2)}, u32[]{:S(2)}) collective-permute-start(f32[24,128]{1,0:T(8,128)S(1)} %get-tuple-element.52), channel_id=1, source_target_pairs={{0,32},{32,0},{64,96},{96,64},{128,160},{160,128},{192,224},{224,1... | collective-permute-start | bytes 36872 | tf_op jit(solution)/shard_map/ppermute | solution.py:354
  55.4 21.0 %all-to-all-start.2 = ((f32[32,2,128]{2,1,0:T(2,128)}), f32[32,2,128]{2,1,0:T(2,128)S(1)}, u32[]{:S(2)}, u32[]{:S(2)}) async-start(f32[32,2,128]{2,1,0:T(2,128)} %get-tuple-element.55), calls=%async_computation.2 | async-start | bytes 65536 | tf_op jit(solution)/shard_map/all_to_all | solution.py:344
  59.2 4.5 %collective-permute-start.1 = (f32[24,128]{1,0:T(8,128)S(1)}, f32[24,128]{1,0:T(8,128)S(1)}, u32[]{:S(2)}, u32[]{:S(2)}) collective-permute-start(f32[24,128]{1,0:T(8,128)S(1)} %add.12), channel_id=1, source_target_pairs={{0,64},{32,96},{64,0},{96,32},{128,192},{160,224},{192,128},{224,1... | collective-permute-start | bytes 36872 | tf_op jit(solution)/shard_map/ppermute | solution.py:354
  63.7 10.8 %collective-permute-start.2 = (f32[24,128]{1,0:T(8,128)S(1)}, f32[24,128]{1,0:T(8,128)S(1)}, u32[]{:S(2)}, u32[]{:S(2)}) collective-permute-start(f32[24,128]{1,0:T(8,128)S(1)} %add.13.half_ref), channel_id=1, source_target_pairs={{0,128},{32,160},{64,192},{96,224},{128,0},{160,32},{192,64},{224,... | collective-permute-start | bytes 36872 | tf_op jit(solution)/shard_map/ppermute | solution.py:354
  70.0 2.8 %copy-start.3 = (f32[2,16,3,128,128]{4,3,2,1,0:T(8,128)S(1)}, f32[2,16,3,128,128]{4,3,2,1,0:T(8,128)}, u32[]{:S(2)}) copy-start(f32[2,16,3,128,128]{4,3,2,1,0:T(8,128)} %param.9) | copy-start | bytes 18874372
  72.8 1.8 %copy-start.17 = (f32[16,128,128]{2,1,0:T(8,128)S(1)}, f32[16,128,128]{2,1,0:T(8,128)}, u32[]{:S(2)}) copy-start(f32[16,128,128]{2,1,0:T(8,128)} %cap_precond_ref.5) | copy-start | bytes 3145732
  76.4 2.8 %copy-start.4 = (f32[2,16,3,128,128]{4,3,2,1,0:T(8,128)S(1)}, f32[2,16,3,128,128]{4,3,2,1,0:T(8,128)}, u32[]{:S(2)}) copy-start(f32[2,16,3,128,128]{4,3,2,1,0:T(8,128)} %param.9) | copy-start | bytes 18874372
  79.1 3.4 %copy-start.9 = (f32[32,4,128,128]{3,2,1,0:T(8,128)S(1)}, f32[32,4,128,128]{3,2,1,0:T(8,128)}, u32[]{:S(2)}) copy-start(f32[32,4,128,128]{3,2,1,0:T(8,128)} %copy-done.7) | copy-start | bytes 25165828
  85.4 16.0 %all-to-all-start.3 = ((f32[32,4,128]{2,1,0:T(4,128)}), f32[32,4,128]{2,1,0:T(4,128)S(1)}, u32[]{:S(2)}, u32[]{:S(2)}) async-start(f32[32,4,128]{2,1,0:T(4,128)} %get-tuple-element.57), calls=%async_computation.3 | async-start | bytes 131072 | tf_op jit(solution)/shard_map/all_to_all | solution.py:344
  94.1 12.6 %collective-permute-start.3 = (f32[24,128]{1,0:T(8,128)S(1)}, f32[24,128]{1,0:T(8,128)S(1)}, u32[]{:S(2)}, u32[]{:S(2)}) collective-permute-start(f32[24,128]{1,0:T(8,128)S(1)} %get-tuple-element.66), channel_id=1, source_target_pairs={{0,32},{32,0},{64,96},{96,64},{128,160},{160,128},{192,224},{224,1... | collective-permute-start | bytes 36872 | tf_op jit(solution)/shard_map/ppermute | solution.py:354
  102.6 17.0 %all-to-all-start.4 = ((f32[32,2,128]{2,1,0:T(2,128)}), f32[32,2,128]{2,1,0:T(2,128)S(1)}, u32[]{:S(2)}, u32[]{:S(2)}) async-start(f32[32,2,128]{2,1,0:T(2,128)} %get-tuple-element.68), calls=%async_computation.4 | async-start | bytes 65536 | tf_op jit(solution)/shard_map/all_to_all | solution.py:344
  106.7 3.8 %collective-permute-start.4 = (f32[24,128]{1,0:T(8,128)S(1)}, f32[24,128]{1,0:T(8,128)S(1)}, u32[]{:S(2)}, u32[]{:S(2)}) collective-permute-start(f32[24,128]{1,0:T(8,128)S(1)} %add.14), channel_id=1, source_target_pairs={{0,64},{32,96},{64,0},{96,32},{128,192},{160,224},{192,128},{224,1... | collective-permute-start | bytes 36872 | tf_op jit(solution)/shard_map/ppermute | solution.py:354
  110.5 7.3 %collective-permute-start.5 = (f32[24,128]{1,0:T(8,128)S(1)}, f32[24,128]{1,0:T(8,128)S(1)}, u32[]{:S(2)}, u32[]{:S(2)}) collective-permute-start(f32[24,128]{1,0:T(8,128)S(1)} %add.15.half_ref), channel_id=1, source_target_pairs={{0,128},{32,160},{64,192},{96,224},{128,0},{160,32},{192,64},{224,... | collective-permute-start | bytes 36872 | tf_op jit(solution)/shard_map/ppermute | solution.py:354
  113.2 2.8 %copy-start.5 = (f32[2,16,3,128,128]{4,3,2,1,0:T(8,128)S(1)}, f32[2,16,3,128,128]{4,3,2,1,0:T(8,128)}, u32[]{:S(2)}) copy-start(f32[2,16,3,128,128]{4,3,2,1,0:T(8,128)} %param.9) | copy-start | bytes 18874372
  116.0 1.8 %copy-start.18 = (f32[16,128,128]{2,1,0:T(8,128)S(1)}, f32[16,128,128]{2,1,0:T(8,128)}, u32[]{:S(2)}) copy-start(f32[16,128,128]{2,1,0:T(8,128)} %cap_precond_ref.5) | copy-start | bytes 3145732
  119.6 2.8 %copy-start.6 = (f32[2,16,3,128,128]{4,3,2,1,0:T(8,128)S(1)}, f32[2,16,3,128,128]{4,3,2,1,0:T(8,128)}, u32[]{:S(2)}) copy-start(f32[2,16,3,128,128]{4,3,2,1,0:T(8,128)} %param.9) | copy-start | bytes 18874372
  122.4 3.4 %copy-start.10 = (f32[32,4,128,128]{3,2,1,0:T(8,128)S(1)}, f32[32,4,128,128]{3,2,1,0:T(8,128)}, u32[]{:S(2)}) copy-start(f32[32,4,128,128]{3,2,1,0:T(8,128)} %copy-done.7) | copy-start | bytes 25165828
  128.6 11.6 %all-to-all-start.5 = ((f32[8,24,128]{2,1,0:T(8,128)}), f32[8,24,128]{2,1,0:T(8,128)S(1)}, u32[]{:S(2)}, u32[]{:S(2)}) async-start(f32[8,24,128]{2,1,0:T(8,128)} %get-tuple-element.71), calls=%async_computation.5 | async-start | bytes 196608 | tf_op jit(solution)/shard_map/all_to_all | solution.py:419
  132.5 3.4 %copy-start.11 = (f32[32,4,128,128]{3,2,1,0:T(8,128)S(1)}, f32[32,4,128,128]{3,2,1,0:T(8,128)}, u32[]{:S(2)}) copy-start(f32[32,4,128,128]{3,2,1,0:T(8,128)} %copy-done.7) | copy-start | bytes 25165828
  (3 other events, 3.6 us)

commit v2 on v1

v2 whole, which is shorter than its diff:
```python
import functools

import jax
import jax.numpy as jnp
from jax import lax
from jax.experimental import pallas as pl
from jax.experimental.pallas import tpu as pltpu
from jax.sharding import PartitionSpec as P

GROUP = ("stn", "tm")
F32 = jnp.float32
SLOT = 4
NOTE = 8
VMEM = pl.BlockSpec(memory_space=pltpu.VMEM)
SMEM = pl.BlockSpec(memory_space=pltpu.SMEM)
HBM = pl.BlockSpec(memory_space=pltpu.HBM)
PARTS = 4


def call(kernel, outs, args, scalars=0, scratch=(), aliases=None, flops=0, hbm=(), hbm_outs=()):
    outs = [
        pltpu.HBM(o, F32) if n in hbm_outs else jax.ShapeDtypeStruct(o, F32) for n, o in enumerate(outs)
    ]
    args = [
        pltpu.with_memory_space_constraint(x, pltpu.HBM) if n in hbm else x for n, x in enumerate(args)
    ]
    specs = [SMEM] * scalars + [VMEM] * (len(args) - scalars)
    return pl.pallas_call(
        kernel,
        out_shape=outs,
        in_specs=[HBM if n in hbm else spec for n, spec in enumerate(specs)],
        out_specs=[HBM if n in hbm_outs else VMEM for n in range(len(outs))],
        scratch_shapes=list(scratch),
        input_output_aliases=aliases or {},
        compiler_params=pltpu.CompilerParams(vmem_limit_bytes=32 * 1024 * 1024),
        cost_estimate=pl.CostEstimate(flops=flops, bytes_accessed=4 * 1024 * 1024, transcendentals=0),
    )(*args)


def fetch(source, target, sems, first, parts):
    step = target.shape[0] // parts
    copies = []
    for n in range(parts):
        part = pl.ds(n * step, step)
        copies.append(pltpu.make_async_copy(source.at[part], target.at[part], sems.at[first + n]))
        copies[-1].start()
    return copies


def down(block, column):
    return jnp.sum(block * jnp.broadcast_to(column, block.shape), axis=0, keepdims=True)


def fold(x):
    return jnp.sum(x, axis=0, keepdims=True)


def precondition(blocks_ref, x, out_ref, copies=()):
    xt = x.T
    for i in range(x.shape[0]):
        if copies and i % (x.shape[0] // len(copies)) == 0:
            copies[i // (x.shape[0] // len(copies))].wait()
        out_ref[i : i + 1] = down(blocks_ref[i], xt[:, i : i + 1])


def first_kernel(rhs_hbm, precond_hbm, v_ref, send_ref, rhs_ref, precond_ref, sems):
    (small,) = fetch(rhs_hbm, rhs_ref, sems, PARTS, 1)
    copies = fetch(precond_hbm, precond_ref, sems, 0, PARTS)
    small.wait()
    precondition(precond_ref, rhs_ref[...], v_ref, copies)
    send_ref[...] = jnp.broadcast_to(v_ref[...][None], send_ref.shape)


def widen(x, wide_ref):
    xt = x.T
    for i in range(x.shape[0]):
        wide_ref[i] = jnp.broadcast_to(xt[:, i : i + 1], wide_ref.shape[1:])


def own_rows(i, blocks, arcs, index_ref, tiles_ref, wide_ref):
    c, j = lax.div(i, arcs), lax.rem(i, arcs)
    total = tiles_ref[i, 0] * wide_ref[c * blocks + lax.rem(index_ref[0, c, j], blocks)]
    return total + tiles_ref[i, 1] * wide_ref[c * blocks + lax.rem(index_ref[1, c, j], blocks)]


def start_kernel(comms, index_ref, cap_index_ref, v_ref, cap_rhs_ref, tiles_hbm, cap_tiles_hbm, cap_precond_hbm,
                 up_ref, q_ref, turned_hbm, cap_turned_hbm, tiles_ref, third_ref, turned_ref, cap_turned_ref,
                 cap_tiles_ref, cap_precond_ref, wide_ref, cap_wide_ref, sems):
    count = up_ref.shape[0]
    arcs = count // comms
    blocks = v_ref.shape[0] // comms
    (pre,) = fetch(cap_precond_hbm, cap_precond_ref, sems, 5 * PARTS, 1)
    own = fetch(tiles_hbm.at[:, pl.ds(0, 2)], tiles_ref, sems, 0, PARTS)
    caps = fetch(cap_tiles_hbm, cap_tiles_ref, sems, PARTS, PARTS)
    thirds = fetch(tiles_hbm.at[:, 2], third_ref, sems, 2 * PARTS, PARTS)
    widen(v_ref[...], wide_ref)
    pre.wait()
    precondition(cap_precond_ref, cap_rhs_ref[...], q_ref)
    widen(q_ref[...], cap_wide_ref)
    step = count // PARTS
    out = []
    for n in range(PARTS):
        own[n].wait()
        caps[n].wait()
        thirds[n].wait()

        def one(i, _):
            total = own_rows(i, blocks, arcs, index_ref, tiles_ref, wide_ref)
            cap = cap_index_ref[lax.div(i, arcs), lax.rem(i, arcs)]
            up_ref[pl.ds(i, 1)] = fold(total + cap_tiles_ref[i] * cap_wide_ref[cap])
            for k in range(2):
                turned_ref[i, k] = tiles_ref[i, k].T
            turned_ref[i, 2] = third_ref[i].T
            cap_turned_ref[i] = cap_tiles_ref[i].T
            return 0

        lax.fori_loop(n * step, (n + 1) * step, one, 0)
        part = pl.ds(n * step, step)
        out.append(
            pltpu.make_async_copy(turned_ref.at[part], turned_hbm.at[part], sems.at[3 * PARTS + n])
        )
        out[-1].start()
        out.append(
            pltpu.make_async_copy(
                cap_turned_ref.at[part], cap_turned_hbm.at[part], sems.at[4 * PARTS + n]
            )
        )
        out[-1].start()
    for copy in out:
        copy.wait()


def near_kernel(comms, index_ref, v_ref, tiles_hbm, up_ref, tiles_ref, wide_ref, sems):
    count = up_ref.shape[0]
    arcs = count // comms
    blocks = v_ref.shape[0] // comms
    own = fetch(tiles_hbm.at[:, pl.ds(0, 2)], tiles_ref, sems, 0, PARTS)
    widen(v_ref[...], wide_ref)
    step = count // PARTS
    for n in range(PARTS):
        own[n].wait()

        def one(i, _):
            up_ref[pl.ds(i, 1)] = fold(own_rows(i, blocks, arcs, index_ref, tiles_ref, wide_ref))
            return 0

        lax.fori_loop(n * step, (n + 1) * step, one, 0, unroll=4)


def cap_up(comms, cap_index_ref, q_ref, cap_tiles_ref, up_ref, out_ref, wide_ref, copy):
    copy.wait()
    arcs = out_ref.shape[0] // comms
    widen(q_ref[...], wide_ref)

    def one(i, _):
        cap = cap_index_ref[lax.div(i, arcs), lax.rem(i, arcs)]
        out_ref[pl.ds(i, 1)] = up_ref[pl.ds(i, 1)] + fold(cap_tiles_ref[i] * wide_ref[cap])
        return 0

    lax.fori_loop(0, cap_tiles_ref.shape[0], one, 0, unroll=4)


def cap_second_kernel(
    comms, cap_index_ref, cap_rhs_ref, q0_ref, half_ref, other_ref, up_ref, cap_precond_hbm, cap_tiles_hbm,
    yq_ref, q_ref, sums_ref, out_ref, wide_ref, cap_precond_ref, cap_tiles_ref, sems,
):
    (pre,) = fetch(cap_precond_hbm, cap_precond_ref, sems, 0, 1)
    (caps_in,) = fetch(cap_tiles_hbm, cap_tiles_ref, sems, 1, 1)
    caps = q0_ref.shape[0]
    note = half_ref[...] + other_ref[...]
    q0 = q0_ref[...]
    yq_ref[...] = q0 + note[:caps]
    sums_ref[...] = note[caps:]
    sums_ref[0:1] += fold(cap_rhs_ref[...] * q0)
    sums_ref[1:2] += fold(q0 * q0)
    precondition(cap_precond_ref, yq_ref[...], q_ref, [pre])
    cap_up(comms, cap_index_ref, q_ref, cap_tiles_ref, up_ref, out_ref, wide_ref, caps_in)


def cap_third_kernel(
    comms, cap_index_ref, alpha_ref, cap_rhs_ref, q0_ref, yq0_ref, q1_ref, half_ref, other_ref, up_ref,
    cap_precond_hbm, cap_tiles_hbm, zq_ref, yzq_ref, rq_ref, q_ref, sums_ref, out_ref, wide_ref,
    cap_precond_ref, cap_tiles_ref, sems,
):
    (pre,) = fetch(cap_precond_hbm, cap_precond_ref, sems, 0, 1)
    (caps_in,) = fetch(cap_tiles_hbm, cap_tiles_ref, sems, 1, 1)
    caps = q0_ref.shape[0]
    alpha = alpha_ref[0:1]
    yq0, q1 = yq0_ref[...], q1_ref[...]
    yq1 = q1 + half_ref[:caps] + other_ref[:caps]
    zq = q0_ref[...] - alpha * q1
    yzq = yq0 - alpha * yq1
    rq = cap_rhs_ref[...] - alpha * yq0
    zq_ref[...] = zq
    yzq_ref[...] = yzq
    rq_ref[...] = rq
    precondition(cap_precond_ref, alpha * yzq, q_ref, [pre])
    q = q_ref[...]
    pairs = ((zq, yq0), (zq, yzq), (q, yq0), (q, yzq), (q, q), (zq, rq), (q, rq))
    for n, (one, other) in enumerate(pairs):
        sums_ref[n : n + 1] = fold(one * other)
    sums_ref[7:8] = jnp.zeros_like(sums_ref[7:8])
    cap_up(comms, cap_index_ref, q_ref, cap_tiles_ref, up_ref, out_ref, wide_ref, caps_in)


def arcs_up(comms, index_ref, blocks, up_ref, got_ref, scale_ref, third_ref, far_ref, scaled_ref, copies):
    count = up_ref.shape[0]
    arcs = count // comms
    for i in range(count):
        c = i // arcs
        far = index_ref[2, c, i % arcs]
        row = c if got_ref.shape[1] == comms else c * blocks + lax.rem(far, blocks)
        far_ref[i : i + 1] = got_ref[lax.div(far, blocks), pl.ds(row, 1)]
    ft = far_ref[...].T
    for i in range(count):
        if i % (count // len(copies)) == 0:
            copies[i // (count // len(copies))].wait()
        far_ref[i : i + 1] = up_ref[i : i + 1] + down(third_ref[i], ft[:, i : i + 1])
    upward = far_ref[...]
    scaled = scale_ref[...] * upward
    scaled_ref[...] = scaled
    return fold(upward * scaled)


def arcs_cap(comms, cap_index_ref, scaled_ref, cap_turned_ref, note_ref, copies):
    count = scaled_ref.shape[0]
    arcs = count // comms
    st = scaled_ref[...].T
    for i in range(count):
        if i % (count // len(copies)) == 0:
            copies[i // (count // len(copies))].wait()
        cap = cap_index_ref[i // arcs, i % arcs]
        note_ref[pl.ds(cap, 1)] += down(cap_turned_ref[i], st[:, i : i + 1])


def arcs_rows(comms, index_ref, blocks, scaled_ref, turned_ref, local_ref, back_ref, first, copies):
    count = scaled_ref.shape[0]
    arcs = count // comms
    st = scaled_ref[...].T
    local_ref[...] = jnp.zeros_like(local_ref)
    if first:
        back_ref[...] = jnp.full(back_ref.shape, -1.0, F32)
    for i in range(count):
        if i % (count // len(copies)) == 0:
            copies[i // (count // len(copies))].wait()
        c, j = i // arcs, i % arcs
        wide = jnp.broadcast_to(st[:, i : i + 1], turned_ref.shape[2:])
        for k in range(2):
            b = c * blocks + lax.rem(index_ref[k, c, j], blocks)
            local_ref[pl.ds(b, 1)] += fold(turned_ref[i, k] * wide)
        far = index_ref[2, c, j]
        to = lax.div(far, blocks)
        back_ref[to, c : c + 1] = fold(turned_ref[i, 2] * wide)
        if first:
            local = lax.rem(far, blocks).astype(F32)
            back_ref[to, comms + c : comms + c + 1] = jnp.full((1, back_ref.shape[2]), local, F32)


def both_kernel(comms, blocks, caps, first, index_ref, cap_index_ref, rhs_ref, v_ref, sums_ref, up_ref, got_ref,
                scale_ref, tiles_hbm, turned_hbm, cap_turned_hbm, note_ref, local_ref, back_ref, far_ref,
                scaled_ref, third_ref, turned_ref, cap_turned_ref, sems):
    thirds = fetch(tiles_hbm.at[:, 2], third_ref, sems, 0, PARTS)
    caps_in = fetch(cap_turned_hbm, cap_turned_ref, sems, PARTS, PARTS)
    rows_in = fetch(turned_hbm, turned_ref, sems, 2 * PARTS, PARTS)
    energy = arcs_up(comms, index_ref, blocks, up_ref, got_ref, scale_ref, third_ref, far_ref, scaled_ref, thirds)
    note_ref[...] = jnp.zeros_like(note_ref)
    arcs_cap(comms, cap_index_ref, scaled_ref, cap_turned_ref, note_ref, caps_in)
    arcs_rows(comms, index_ref, blocks, scaled_ref, turned_ref, local_ref, back_ref, first, rows_in)
    if first:
        v = v_ref[...]
        note_ref[caps : caps + 1] = fold(rhs_ref[...] * v)
        note_ref[caps + 1 : caps + 2] = fold(v * v) + energy
    else:
        shape = (back_ref.shape[0], 2, back_ref.shape[2])
        back_ref[:, comms : comms + 2] = jnp.broadcast_to(sums_ref[0:2][None], shape)


def last_up_kernel(comms, blocks, caps, index_ref, cap_index_ref, z_ref, yz_ref, r_ref, y0_ref, v_ref,
                   up_ref, got_ref, scale_ref, tiles_hbm, cap_turned_hbm, notes_ref, scaled_ref, far_ref,
                   note_ref, third_ref, cap_turned_ref, sems):
    thirds = fetch(tiles_hbm.at[:, 2], third_ref, sems, 0, PARTS)
    caps_in = fetch(cap_turned_hbm, cap_turned_ref, sems, PARTS, PARTS)
    energy = arcs_up(comms, index_ref, blocks, up_ref, got_ref, scale_ref, third_ref, far_ref, scaled_ref, thirds)
    note_ref[...] = jnp.zeros_like(note_ref)
    arcs_cap(comms, cap_index_ref, scaled_ref, cap_turned_ref, note_ref, caps_in)
    z, yz, r, y0, v = z_ref[...], yz_ref[...], r_ref[...], y0_ref[...], v_ref[...]
    pairs = ((z, y0), (z, yz), (v, y0), (v, yz), (v, v), (z, r), (v, r))
    for n, (one, other) in enumerate(pairs):
        note_ref[caps + n : caps + n + 1] = fold(one * other)
    note_ref[caps + 4 : caps + 5] += energy
    notes_ref[...] = jnp.broadcast_to(note_ref[...][None], notes_ref.shape)


def last_down_kernel(comms, blocks, index_ref, scaled_ref, turned_hbm, local_ref, back_ref, turned_ref, sems):
    rows_in = fetch(turned_hbm, turned_ref, sems, 0, PARTS)
    arcs_rows(comms, index_ref, blocks, scaled_ref, turned_ref, local_ref, back_ref, False, rows_in)


def insert_kernel(comms, caps, notes_ref, sums_ref, back_ref, cap_ref, out_ref):
    del back_ref
    total = jnp.sum(notes_ref[...], axis=0)
    cap_ref[...] = total[:caps]
    sums = jnp.sum(total[caps:] + sums_ref[...], axis=1, keepdims=True)
    width = out_ref.shape[2]
    pick = lax.broadcasted_iota(jnp.int32, (NOTE, width), 0) == lax.broadcasted_iota(
        jnp.int32, (NOTE, width), 1
    )
    row = fold(jnp.where(pick, jnp.broadcast_to(sums, (NOTE, width)), 0.0))
    out_ref[:, comms : comms + 1] = jnp.broadcast_to(row[None], (out_ref.shape[0], 1, width))


def collect(comms, v_ref, local_ref, back_ref, asked, y_ref):
    blocks = v_ref.shape[0] // comms
    for c in range(comms):
        part = back_ref[:, c]
        for b in range(blocks):
            n = c * blocks + b
            came = fold(jnp.where(asked[c] == b, part, 0.0))
            y_ref[n : n + 1] = v_ref[n : n + 1] + local_ref[n : n + 1] + came


def pack(comms, v_ref, asked, send_ref):
    blocks = v_ref.shape[0] // comms
    for c in range(comms):
        row = jnp.zeros_like(asked[c])
        for b in range(blocks):
            n = c * blocks + b
            row = jnp.where(asked[c] == b, v_ref[n : n + 1], row)
        send_ref[:, c] = row


def rows_second_kernel(comms, v0_ref, local_ref, back_ref, note_ref, came_ref, precond_hbm, half_ref, y_ref,
                       v_ref, send_ref, asked_ref, precond_ref, sems):
    (pre,) = fetch(precond_hbm, precond_ref, sems, 0, 1)
    half_ref[...] = note_ref[...] + came_ref[...]
    asked = [back_ref[:, comms + c] for c in range(comms)]
    for c in range(comms):
        asked_ref[c] = asked[c]
    collect(comms, v0_ref, local_ref, back_ref, asked, y_ref)
    precondition(precond_ref, y_ref[...], v_ref, [pre])
    pack(comms, v_ref, asked, send_ref)


def rows_third_kernel(comms, rhs_ref, v0_ref, y0_ref, v1_ref, local_ref, back_ref, note_ref, came_ref, asked_ref,
                      precond_hbm, half_ref, alpha_ref, z_ref, yz_ref, r_ref, v_ref, send_ref, precond_ref,
                      sems):
    (pre,) = fetch(precond_hbm, precond_ref, sems, 0, 1)
    half_ref[...] = note_ref[...] + came_ref[...]
    asked = [asked_ref[c] for c in range(comms)]
    collect(comms, v1_ref, local_ref, back_ref, asked, yz_ref)
    first = jnp.sum(fold(back_ref[:, comms]), axis=1, keepdims=True)
    second = jnp.sum(fold(back_ref[:, comms + 1]), axis=1, keepdims=True)
    alpha = jnp.broadcast_to(first / second, (1, alpha_ref.shape[1]))
    alpha_ref[...] = jnp.broadcast_to(alpha, alpha_ref.shape)
    alpha_ref[1:2] = jnp.broadcast_to(second, (1, alpha_ref.shape[1]))
    y0 = y0_ref[...]
    z_ref[...] = v0_ref[...] - alpha * v1_ref[...]
    yz = y0 - alpha * yz_ref[...]
    yz_ref[...] = yz
    r_ref[...] = rhs_ref[...] - alpha * y0
    precondition(precond_ref, alpha * yz, v_ref, [pre])
    pack(comms, v_ref, asked, send_ref)


def last_kernel(comms, alpha_ref, v0_ref, y0_ref, z_ref, yz_ref, r_ref, v2_ref, local_ref, back_ref,
                asked_ref, q0_ref, yq0_ref, zq_ref, yzq_ref, rq_ref, q2_ref, cap_ref,
                sol_ref, cap_sol_ref, res_ref, cap_res_ref, y_ref):
    asked = [asked_ref[c] for c in range(comms)]
    collect(comms, v2_ref, local_ref, back_ref, asked, y_ref)
    row = fold(back_ref[:, comms])
    width = row.shape[1]
    lane = lax.broadcasted_iota(jnp.int32, row.shape, 1)
    s = [
        jnp.broadcast_to(
            jnp.sum(jnp.where(lane == n, row, 0.0), axis=1, keepdims=True), (1, width)
        )
        for n in range(7)
    ]
    alpha, h00 = alpha_ref[0:1], alpha_ref[1:2]
    h1, h2 = s[0] / h00, s[2] / h00
    a11 = s[1] - h1 * s[0]
    a12 = s[3] - h1 * s[2]
    a22 = s[4] - h2 * s[2]
    lower = a12 / a11
    c2 = (s[6] - lower * s[5]) / (a22 - lower * a12)
    c1 = s[5] / a11 - lower * c2
    c0 = c1 * h1 + c2 * h2
    sol_ref[...] = (alpha - c0) * v0_ref[...] + c1 * z_ref[...] + c2 * v2_ref[...]
    cap_sol_ref[...] = (alpha - c0) * q0_ref[...] + c1 * zq_ref[...] + c2 * q2_ref[...]
    res_ref[...] = r_ref[...] + c0 * y0_ref[...] - c1 * yz_ref[...] - c2 * y_ref[...]
    yq2 = q2_ref[...] + cap_ref[...]
    cap_res_ref[...] = rq_ref[...] + c0 * yq0_ref[...] - c1 * yzq_ref[...] - c2 * yq2


def body(
    tiles, cap_tiles, row_index, cap_index, arc_scale, rows_rhs, cap_rhs, precond, cap_precond
):
    comms, arcs, touched = row_index.shape
    blocks, width = rows_rhs.shape[1:]
    caps = cap_rhs.shape[0]
    groups = lax.axis_size("stn") * lax.axis_size("tm")
    peers = lax.axis_size("comm")
    rows, count = comms * blocks, comms * arcs
    flat = (width, width)
    tiles = tiles.reshape(count, touched, *flat)
    cap_tiles = cap_tiles.reshape(count, *flat)
    precond = precond.reshape(rows, *flat)
    index = jnp.transpose(row_index, (2, 0, 1))
    scale = arc_scale.reshape(count, width)
    rhs = rows_rhs.reshape(rows, width)
    row_shape, cap_shape, arc_shape = (rows, width), (caps, width), (count, width)
    tall, cap_tall = (count, touched, *flat), (count, *flat)
    wide_rows = pltpu.VMEM((rows, *flat), F32)
    wide_caps = pltpu.VMEM((caps, *flat), F32)
    own_tiles = pltpu.VMEM((count, 2, *flat), F32)
    cap_blocks = pltpu.VMEM((caps, *flat), F32)
    row_blocks = pltpu.VMEM((rows, *flat), F32)
    cap_scratch = pltpu.VMEM(cap_tall, F32)
    arc_scratch = pltpu.VMEM(arc_shape, F32)
    small = (NOTE, width)
    note_shape = (caps + NOTE, width)
    send_shape = (groups, comms, width)
    back_shape = (groups, SLOT, width)
    unit = 2 * count * width * width

    def exchange(x):
        return lax.all_to_all(x, GROUP, 0, 0)

    def across(x, step):
        return lax.ppermute(x, "comm", [(i, i ^ step) for i in range(peers)])

    def sems(n):
        return pltpu.SemaphoreType.DMA((n,))

    v0, send = call(
        first_kernel, [row_shape, (groups, rows, width)], (rhs, precond), 0,
        [pltpu.VMEM(row_shape, F32), pltpu.VMEM((rows, *flat), F32), sems(PARTS + 1)], hbm=(0, 1),
    )
    got = exchange(send)
    up, q0, turned, cap_turned = call(
        functools.partial(start_kernel, comms),
        [arc_shape, cap_shape, tall, cap_tall],
        (index, cap_index, v0, cap_rhs, tiles, cap_tiles, cap_precond),
        2,
        [own_tiles, cap_scratch, pltpu.VMEM(tall, F32), cap_scratch, cap_scratch, cap_blocks, wide_rows, wide_caps,
         sems(5 * PARTS + 1)],
        flops=8 * unit,
        hbm=(4, 5, 6),
        hbm_outs=(2, 3),
    )

    def both(first, v, sums, up, got):
        return call(
            functools.partial(both_kernel, comms, blocks, caps, first),
            [note_shape, row_shape, back_shape],
            (index, cap_index, rhs, v, sums, up, got, scale, tiles, turned, cap_turned),
            2,
            [arc_scratch, arc_scratch, cap_scratch, pltpu.VMEM(tall, F32), cap_scratch, sems(3 * PARTS)],
            flops=5 * unit,
            hbm=(8, 9, 10),
        )

    def near(v):
        (up,) = call(
            functools.partial(near_kernel, comms),
            [arc_shape],
            (index, v, tiles),
            1,
            [own_tiles, wide_rows, sems(PARTS)],
            flops=2 * unit,
            hbm=(2,),
        )
        return up

    note, local, back = both(True, v0, rhs, up, got)
    back = exchange(back)
    note = note + across(note, 1)
    half, y0, v1, send, asked = call(
        functools.partial(rows_second_kernel, comms),
        [note_shape, row_shape, row_shape, send_shape, (comms, groups, width)],
        (v0, local, back, note, across(note, 2), precond), 0, [row_blocks, sems(1)], hbm=(5,),
    )
    got = exchange(send)
    other = across(half, 4)
    cap_room = [wide_caps, cap_blocks, cap_scratch, sems(2)]
    up = near(v1)
    yq0, q1, sums, up = call(
        functools.partial(cap_second_kernel, comms), [cap_shape, cap_shape, small, arc_shape],
        (cap_index, cap_rhs, q0, half, other, up, cap_precond, cap_tiles), 1, cap_room, flops=2 * unit,
        hbm=(6, 7),
    )
    note, local, back = both(False, v1, sums, up, got)
    back = exchange(back)
    note = note + across(note, 1)
    half, alpha, z1, yz, r1, v2, send = call(
        functools.partial(rows_third_kernel, comms),
        [note_shape, small, row_shape, row_shape, row_shape, row_shape, send_shape],
        (rhs, v0, y0, v1, local, back, note, across(note, 2), asked, precond), 0, [row_blocks, sems(1)],
        hbm=(9,),
    )
    got = exchange(send)
    other = across(half, 4)
    up = near(v2)
    zq1, yzq, rq1, q2, sums, up = call(
        functools.partial(cap_third_kernel, comms), [cap_shape] * 4 + [small, arc_shape],
        (cap_index, alpha, cap_rhs, q0, yq0, q1, half, other, up, cap_precond, cap_tiles), 1, cap_room,
        flops=2 * unit, hbm=(9, 10),
    )
    notes, scaled = call(
        functools.partial(last_up_kernel, comms, blocks, caps),
        [(peers, *note_shape), arc_shape],
        (index, cap_index, z1, yz, r1, y0, v2, up, got, scale, tiles, cap_turned), 2,
        [arc_scratch, pltpu.VMEM(note_shape, F32), cap_scratch, cap_scratch, sems(2 * PARTS)],
        flops=2 * unit,
        hbm=(10, 11),
    )
    notes = lax.all_to_all(notes, "comm", 0, 0)
    local, back = call(
        functools.partial(last_down_kernel, comms, blocks), [row_shape, back_shape],
        (index, scaled, turned), 1, [pltpu.VMEM(tall, F32), sems(PARTS)], flops=3 * unit, hbm=(2,),
    )
    cap_sum, back = call(
        functools.partial(insert_kernel, comms, caps), [cap_shape, back_shape], (notes, sums, back),
        aliases={2: 1},
    )
    back = exchange(back)
    sol, cap_sol, res, cap_res = call(
        functools.partial(last_kernel, comms), [row_shape, cap_shape, row_shape, cap_shape],
        (alpha, v0, y0, z1, yz, r1, v2, local, back, asked, q0, yq0, zq1, yzq, rq1, q2, cap_sum), 0,
        [pltpu.VMEM(row_shape, F32)],
    )
    return sol.reshape(rows_rhs.shape), cap_sol, res.reshape(rows_rhs.shape), cap_res


def solution(mesh):
    placed = (
        P("comm", GROUP, None, None, None),
        P("comm", GROUP, None, None),
        P("comm", GROUP, None),
        P("comm", GROUP),
        P("comm", GROUP, None),
        P("comm", GROUP, None),
        P(GROUP, None),
        P("comm", GROUP, None, None),
        P(GROUP, None, None),
    )
    return jax.shard_map(
        body,
        mesh=mesh,
        in_specs=placed,
        out_specs=(
            P("comm", GROUP, None),
            P(GROUP, None),
            P("comm", GROUP, None),
            P(GROUP, None),
        ),
        check_vma=False,
    )
```

time: 159 us -> 146 us (0.918)
  local copies, waits for them, and re-layouts: 38.7 us -> 2.08 us
  Pallas kernels: 30.1 us -> 49.8 us
  starting transfers between devices: 52.3 us -> 64.1 us
  waiting for transfers between devices: 19 us -> 11.8 us
    unnamed x47 -> x16, local copies, waits for them, and re-layouts: 37.9 us -> 2.08 us
    pallas_call x16 -> x14, Pallas kernels: 30.1 us -> 49.8 us  [call(): pl.pallas_call(kernel, out_shape=outs, in_specs=[HBM if n in hbm else spe...]
    all_to_all x5, waiting for transfers between devices: 12.1 us -> 0.93 us  [exchange(): return lax.all_to_all(x, GROUP, 0, 0)]
    all_to_all x5, starting transfers between devices: 32.4 us -> 41 us  [exchange(): return lax.all_to_all(x, GROUP, 0, 0)]
    ppermute x6, waiting for transfers between devices: 3.93 us -> 6.98 us  [across(): return lax.ppermute(x, 'comm', [(i, i ^ step) for i in range(peers)])]
    ppermute x6, starting transfers between devices: 16 us -> 17.9 us  [across(): return lax.ppermute(x, 'comm', [(i, i ^ step) for i in range(peers)])]
  transfers between devices with their start and end apart: 12 -> 12, of which waited for: 5 -> 7; matrix products, arithmetic and copies ran while one was open for 1% -> 0% of each run, Pallas kernels for 12% -> 18%
where the time goes in v2:
time: 146 us; the launch traced here: 145 us
  starting transfers between devices  64.1 us (44%)
  Pallas kernels  49.8 us (34%)
  blocking collectives  16.8 us (12%)
  waiting for transfers between devices  11.8 us (8%)
  local copies, waits for them, and re-layouts  2.08 us (1%)
    pallas_call x14, Pallas kernels, call(): pl.pallas_call(kernel, out_shape=outs, in_specs=[HBM if n in hbm else spe...  49.8 us
    all_to_all x5, starting transfers between devices, exchange(): return lax.all_to_all(x, GROUP, 0, 0)  41 us
    ppermute x6, starting transfers between devices, across(): return lax.ppermute(x, 'comm', [(i, i ^ step) for i in range(peers)])  17.9 us
    all_to_all x1, blocking collectives, exchange(): return lax.all_to_all(x, GROUP, 0, 0)  16.8 us
    ppermute x6, waiting for transfers between devices, across(): return lax.ppermute(x, 'comm', [(i, i ^ step) for i in range(peers)])  6.98 us
    all_to_all x1, starting transfers between devices, body(): notes = lax.all_to_all(notes, 'comm', 0, 0)  5.09 us
    all_to_all x1, waiting for transfers between devices, body(): notes = lax.all_to_all(notes, 'comm', 0, 0)  3.9 us
  transfers between devices with their start and end apart: 12, of which 7 were waited for; matrix products, arithmetic and copies ran while one was open for 0% of the time, Pallas kernels for 18%

profile of v2, /device:TPU:1, one launch (start us, length us, event | category | flops | bytes accessed | tf_op | source)
XLA Modules:
  0.0 145.4 jit_solution(16266920872916378272)
XLA Ops:
  0.7 2.4 %shard_map.120 = (f32[16,128]{1,0:T(8,128)S(1)}, f32[32,16,128]{2,1,0:T(8,128)}) custom-call(f32[16,128]{1,0:T(8,128)} %bitcast.8, f32[16,128,128]{2,1,0:T(8,128)} %bitcast.32), custom_call_target="tpu_custom_call" | custom-call | bytes 4194304 | tf_op jit(solution)/shard_map/pallas_call | solution.py:28
  3.0 8.6 %all-to-all-start = ((f32[32,16,128]{2,1,0:T(8,128)}), f32[32,16,128]{2,1,0:T(8,128)S(1)}, u32[]{:S(2)}, u32[]{:S(2)}) async-start(f32[32,16,128]{2,1,0:T(8,128)} %get-tuple-element.50), calls=%async_computation | async-start | bytes 524288 | tf_op jit(solution)/shard_map/all_to_all | solution.py:427
  13.7 9.7 %shard_map.121 = (f32[32,128]{1,0:T(8,128)S(1)}, f32[16,128]{1,0:T(8,128)S(1)}, f32[32,3,128,128]{3,2,1,0:T(8,128)}, f32[32,128,128]{2,1,0:T(8,128)}) custom-call(s32[3,2,16]{2,1,0:T(2,128)S(1)} %bitcast.13, s32[2,16]{1,0:T(2,128)S(1)} %copy-done.6, f32[16,128]{1,0:T(8,128)S(1)} %get-tuple-element.48.v_ref.v0_ref, f32[16,128]{1,0:T(8,128)S(1)} %copy-done.4, ...), custom_call_target="tpu_custom_call" | custom-call | flops 8388608 | bytes 4194304 | tf_op jit(solution)/shard_map/pallas_call | solution.py:28
  23.4 5.7 %shard_map.122 = (f32[24,128]{1,0:T(8,128)S(1)}, f32[16,128]{1,0:T(8,128)S(1)}, f32[32,4,128]{2,1,0:T(4,128)}) custom-call(s32[3,2,16]{2,1,0:T(2,128)S(1)} %bitcast.14, s32[2,16]{1,0:T(2,128)S(1)} %copy-done.7, f32[16,128]{1,0:T(8,128)S(1)} %bitcast.9, f32[16,128]{1,0:T(8,128)S(1)} %get-tuple-element.48.v_ref.v0_ref, f32[16,128]{1,0:T(8,128)S(1)} %bitcast.10, ...), custom_call_target="tpu_custom_call" | custom-call | flops 5242880 | bytes 4194304 | tf_op jit(solution)/shard_map/pallas_call | solution.py:28
  29.2 7.4 %all-to-all-start.1 = ((f32[32,4,128]{2,1,0:T(4,128)}), f32[32,4,128]{2,1,0:T(4,128)S(1)}, u32[]{:S(2)}, u32[]{:S(2)}) async-start(f32[32,4,128]{2,1,0:T(4,128)} %get-tuple-element.54), calls=%async_computation.1 | async-start | bytes 131072 | tf_op jit(solution)/shard_map/all_to_all | solution.py:427
  36.6 1.7 %collective-permute-start = (f32[24,128]{1,0:T(8,128)S(1)}, f32[24,128]{1,0:T(8,128)S(1)}, u32[]{:S(2)}, u32[]{:S(2)}) collective-permute-start(f32[24,128]{1,0:T(8,128)S(1)} %get-tuple-element.55), channel_id=1, source_target_pairs={{0,32},{32,0},{64,96},{96,64},{128,160},{160,128},{192,224},{224,1... | collective-permute-start | bytes 36872 | tf_op jit(solution)/shard_map/ppermute | solution.py:430
  38.3 1.1 collective-permute-done
  39.4 3.0 %collective-permute-start.1 = (f32[24,128]{1,0:T(8,128)S(1)}, f32[24,128]{1,0:T(8,128)S(1)}, u32[]{:S(2)}, u32[]{:S(2)}) collective-permute-start(f32[24,128]{1,0:T(8,128)S(1)} %add.6.note_ref), channel_id=1, source_target_pairs={{0,64},{32,96},{64,0},{96,32},{128,192},{160,224},{192,128},{224,1... | collective-permute-start | bytes 36872 | tf_op jit(solution)/shard_map/ppermute | solution.py:430
  42.4 1.4 collective-permute-done.1.came_ref
  43.9 2.7 %shard_map.123 = (f32[24,128]{1,0:T(8,128)S(1)}, f32[16,128]{1,0:T(8,128)S(1)}, f32[16,128]{1,0:T(8,128)S(1)}, f32[32,2,128]{2,1,0:T(2,128)}, f32[2,32,128]{2,1,0:T(8,128)S(1)}) custom-call(f32[16,128]{1,0:T(8,128)S(1)} %get-tuple-element.48.v_ref.v0_ref, f32[16,128]{1,0:T(8,128)S(1)} %get-tuple-element.53.local_ref, ...), custom_call_target="tpu_custom_call" | custom-call | bytes 4194304 | tf_op jit(solution)/shard_map/pallas_call | solution.py:28
  46.6 8.9 %all-to-all-start.2 = ((f32[32,2,128]{2,1,0:T(2,128)}), f32[32,2,128]{2,1,0:T(2,128)S(1)}, u32[]{:S(2)}, u32[]{:S(2)}) async-start(f32[32,2,128]{2,1,0:T(2,128)} %get-tuple-element.62), calls=%async_computation.2 | async-start | bytes 65536 | tf_op jit(solution)/shard_map/all_to_all | solution.py:427
  55.5 6.7 %collective-permute-start.2 = (f32[24,128]{1,0:T(8,128)S(1)}, f32[24,128]{1,0:T(8,128)S(1)}, u32[]{:S(2)}, u32[]{:S(2)}) collective-permute-start(f32[24,128]{1,0:T(8,128)S(1)} %get-tuple-element.59.half_ref), channel_id=1, source_target_pairs={{0,128},{32,160},{64,192},{96,224},{128,0},{160,32},{192,64},{224,... | collective-permute-start | bytes 36872 | tf_op jit(solution)/shard_map/ppermute | solution.py:430
  62.2 2.9 %shard_map.124.up_ref = f32[32,128]{1,0:T(8,128)S(1)} custom-call(s32[3,2,16]{2,1,0:T(2,128)S(1)} %bitcast.15, f32[16,128]{1,0:T(8,128)S(1)} %get-tuple-element.57.v_ref.v1_ref, f32[32,3,128,128]{3,2,1,0:T(8,128)} %bitcast.25), custom_call_target="tpu_custom_call" | custom-call | flops 2097152 | bytes 4194304 | tf_op jit(solution)/shard_map/pallas_call | solution.py:28
  65.2 3.3 %shard_map.125 = (f32[16,128]{1,0:T(8,128)S(1)}, f32[16,128]{1,0:T(8,128)S(1)}, f32[8,128]{1,0:T(8,128)S(1)}, f32[32,128]{1,0:T(8,128)S(1)}) custom-call(s32[2,16]{1,0:T(2,128)S(1)} %copy-done.7, f32[16,128]{1,0:T(8,128)S(1)} %copy-done.5, f32[16,128]{1,0:T(8,128)S(1)} %get-tuple-element.58.q0_ref, f32[24,128]{1,0:T(8,128)S(1)} %get-tuple-element.59.half_ref, ...), custom_call_target="tpu_custom_call" | custom-call | flops 2097152 | bytes 4194304 | tf_op jit(solution)/shard_map/pallas_call | solution.py:28
  68.5 5.7 %shard_map.126 = (f32[24,128]{1,0:T(8,128)S(1)}, f32[16,128]{1,0:T(8,128)S(1)}, f32[32,4,128]{2,1,0:T(4,128)}) custom-call(s32[3,2,16]{2,1,0:T(2,128)S(1)} %bitcast.16, s32[2,16]{1,0:T(2,128)S(1)} %copy-done.7, f32[16,128]{1,0:T(8,128)S(1)} %bitcast.11, f32[16,128]{1,0:T(8,128)S(1)} %get-tuple-element.57.v_ref.v1_ref, ...), custom_call_target="tpu_custom_call" | custom-call | flops 5242880 | bytes 4194304 | tf_op jit(solution)/shard_map/pallas_call | solution.py:28
  74.2 7.7 %all-to-all-start.3 = ((f32[32,4,128]{2,1,0:T(4,128)}), f32[32,4,128]{2,1,0:T(4,128)S(1)}, u32[]{:S(2)}, u32[]{:S(2)}) async-start(f32[32,4,128]{2,1,0:T(4,128)} %get-tuple-element.64), calls=%async_computation.3 | async-start | bytes 131072 | tf_op jit(solution)/shard_map/all_to_all | solution.py:427
  81.9 0.8 collective-permute-start.3
  82.7 2.0 %collective-permute-done.3 = f32[24,128]{1,0:T(8,128)S(1)} collective-permute-done((f32[24,128]{1,0:T(8,128)S(1)}, f32[24,128]{1,0:T(8,128)S(1)}, u32[]{:S(2)}, u32[]{:S(2)}) %collective-permute-start.3) | collective-permute-done | bytes 12320 | tf_op jit(solution)/shard_map/ppermute | solution.py:430
  84.7 1.2 collective-permute-start.4
  85.8 2.5 %collective-permute-done.4.came_ref = f32[24,128]{1,0:T(8,128)S(1)} collective-permute-done((f32[24,128]{1,0:T(8,128)S(1)}, f32[24,128]{1,0:T(8,128)S(1)}, u32[]{:S(2)}, u32[]{:S(2)}) %collective-permute-start.4) | collective-permute-done | bytes 12320 | tf_op jit(solution)/shard_map/ppermute | solution.py:430
  88.4 0.8 all-to-all-done.3.back_ref
  89.2 2.3 %shard_map.127 = (f32[24,128]{1,0:T(8,128)S(1)}, f32[8,128]{1,0:T(8,128)S(1)}, f32[16,128]{1,0:T(8,128)S(1)}, f32[16,128]{1,0:T(8,128)S(1)}, f32[16,128]{1,0:T(8...) custom-call(f32[16,128]{1,0:T(8,128)S(1)} %bitcast.12, f32[16,128]{1,0:T(8,128)S(1)} %get-tuple-element.48.v_ref.v0_ref, ...), custom_call_target="tpu_custom_call" | custom-call | bytes 4194304 | tf_op jit(solution)/shard_map/pallas_call | solution.py:28
  91.5 8.5 %all-to-all-start.4 = ((f32[32,2,128]{2,1,0:T(2,128)}), f32[32,2,128]{2,1,0:T(2,128)S(1)}, u32[]{:S(2)}, u32[]{:S(2)}) async-start(f32[32,2,128]{2,1,0:T(2,128)} %get-tuple-element.76), calls=%async_computation.4 | async-start | bytes 65536 | tf_op jit(solution)/shard_map/all_to_all | solution.py:427
  100.0 4.5 %collective-permute-start.5 = (f32[24,128]{1,0:T(8,128)S(1)}, f32[24,128]{1,0:T(8,128)S(1)}, u32[]{:S(2)}, u32[]{:S(2)}) collective-permute-start(f32[24,128]{1,0:T(8,128)S(1)} %get-tuple-element.74.half_ref), channel_id=1, source_target_pairs={{0,128},{32,160},{64,192},{96,224},{128,0},{160,32},{192,64},{224,... | collective-permute-start | bytes 36872 | tf_op jit(solution)/shard_map/ppermute | solution.py:430
  104.5 2.9 %shard_map.128.up_ref = f32[32,128]{1,0:T(8,128)S(1)} custom-call(s32[3,2,16]{2,1,0:T(2,128)S(1)} %bitcast.17, f32[16,128]{1,0:T(8,128)S(1)} %get-tuple-element.71.v_ref.v2_ref, f32[32,3,128,128]{3,2,1,0:T(8,128)} %bitcast.27), custom_call_target="tpu_custom_call" | custom-call | flops 2097152 | bytes 4194304 | tf_op jit(solution)/shard_map/pallas_call | solution.py:28
  107.4 3.3 %shard_map.129 = (f32[16,128]{1,0:T(8,128)S(1)}, f32[16,128]{1,0:T(8,128)S(1)}, f32[16,128]{1,0:T(8,128)S(1)}, f32[16,128]{1,0:T(8,128)S(1)}, f32[8,128]{1,0:T(8,128)S(1)}, /*index=5*/f32[32,128]{1,0:T(8,128)S(1)}) custom-call(s32[2,16]{1,0:T(2,128)S(1)} %copy-done.7, f32[8,128]{1,0:T(8,128)S(1)} %get-tuple-element.67.alpha_ref, f32[16,128]{1,0:T(8,128)S(1)} %copy-done.5, ...), custom_call_target="tpu_custom_call" | custom-call | flops 2097152 | bytes 4194304 | tf_op jit(solution)/shard_map/pallas_call | solution.py:28
  110.7 4.4 %shard_map.130 = (f32[8,24,128]{2,1,0:T(8,128)}, f32[32,128]{1,0:T(8,128)S(1)}) custom-call(s32[3,2,16]{2,1,0:T(2,128)S(1)} %bitcast.18, s32[2,16]{1,0:T(2,128)S(1)} %copy-done.7, f32[16,128]{1,0:T(8,128)S(1)} %get-tuple-element.68.z_ref, f32[16,128]{1,0:T(8,128)S(1)} %get-tuple-element.69.yz_ref, f32[16,128]{1,0:T(8,128)S(1)} %get-tuple-element.70.r_ref, ...), custom_call_target="tpu_custom_call" | custom-call | flops 2097152 | bytes 4194304 | tf_op jit(solution)/shard_map/pallas_call | solution.py:28
  115.1 5.1 %all-to-all-start.5 = ((f32[8,24,128]{2,1,0:T(8,128)}), f32[8,24,128]{2,1,0:T(8,128)S(1)}, u32[]{:S(2)}, u32[]{:S(2)}) async-start(f32[8,24,128]{2,1,0:T(8,128)} %get-tuple-element.79), calls=%async_computation.5 | async-start | bytes 196608 | tf_op jit(solution)/shard_map/all_to_all | solution.py:517
  120.2 3.7 %shard_map.131 = (f32[16,128]{1,0:T(8,128)S(1)}, f32[32,4,128]{2,1,0:T(4,128)S(1)}) custom-call(s32[3,2,16]{2,1,0:T(2,128)S(1)} %bitcast.19, f32[32,128]{1,0:T(8,128)S(1)} %get-tuple-element.77.scaled_ref, f32[32,3,128,128]{3,2,1,0:T(8,128)} %get-tuple-element.51.turned_hbm), custom_call_target="tpu_custom_call" | custom-call | flops 3145728 | bytes 4194304 | tf_op jit(solution)/shard_map/pallas_call | solution.py:28
  123.9 3.9 %all-to-all-done.5.notes_ref = f32[8,24,128]{2,1,0:T(8,128)S(1)} async-done(((f32[8,24,128]{2,1,0:T(8,128)}), f32[8,24,128]{2,1,0:T(8,128)S(1)}, u32[]{:S(2)}, u32[]{:S(2)}) %all-to-all-start.5) | async-done | bytes 98336 | tf_op jit(solution)/shard_map/all_to_all | solution.py:517
  127.9 16.8 %all_to_all.35.back_ref = f32[32,4,128]{2,1,0:T(4,128)S(1)} all-to-all(f32[32,4,128]{2,1,0:T(4,128)S(1)} %get-tuple-element.82), channel_id=1, replica_groups=mesh['comm'=8,'stn'=16,'tm'=2] {'stn','tm'}, dimensions={0} | all-to-all | bytes 131072 | tf_op jit(solution)/shard_map/all_to_all | solution.py:427
  144.7 0.7 shard_map.133
  (25 shorter events, 2.3 us)
Async XLA Ops:
  0.6 22.8 %copy-start = (f32[2,8,128]{2,1,0:T(8,128)S(1)}, f32[2,8,128]{2,1,0:T(8,128)}, u32[]{:S(2)}) copy-start(f32[2,8,128]{2,1,0:T(8,128)} %param.14) | copy-start | bytes 24580
  0.6 22.8 %copy-start.7 = (s32[2,16]{1,0:T(2,128)S(1)}, s32[2,16]{1,0:T(2,128)}, u32[]{:S(2)}) copy-start(s32[2,16]{1,0:T(2,128)} %cap_index_ref.11) | copy-start | bytes 388
  0.7 22.8 %copy-start.2 = (s32[2,16,3]{1,0,2:T(2,128)S(1)}, s32[2,16,3]{1,0,2:T(2,128)}, u32[]{:S(2)}) copy-start(s32[2,16,3]{1,0,2:T(2,128)} %param.11) | copy-start | bytes 1156
  0.7 22.8 %copy-start.3 = (f32[2,16,128]{2,1,0:T(8,128)S(1)}, f32[2,16,128]{2,1,0:T(8,128)}, u32[]{:S(2)}) copy-start(f32[2,16,128]{2,1,0:T(8,128)} %param.13) | copy-start | bytes 49156
  3.0 20.4 %all-to-all-start = ((f32[32,16,128]{2,1,0:T(8,128)}), f32[32,16,128]{2,1,0:T(8,128)S(1)}, u32[]{:S(2)}, u32[]{:S(2)}) async-start(f32[32,16,128]{2,1,0:T(8,128)} %get-tuple-element.50), calls=%async_computation | async-start | bytes 524288 | tf_op jit(solution)/shard_map/all_to_all | solution.py:427
  11.6 0.7 copy-start.1
  12.3 0.7 copy-start.4
  13.0 0.7 copy-start.6
  29.2 36.0 %copy-start.5 = (f32[16,128]{1,0:T(8,128)S(1)}, f32[16,128]{1,0:T(8,128)}, u32[]{:S(2)}) copy-start(f32[16,128]{1,0:T(8,128)} %cap_rhs_ref.5) | copy-start | bytes 24580
  29.2 14.7 %all-to-all-start.1 = ((f32[32,4,128]{2,1,0:T(4,128)}), f32[32,4,128]{2,1,0:T(4,128)S(1)}, u32[]{:S(2)}, u32[]{:S(2)}) async-start(f32[32,4,128]{2,1,0:T(4,128)} %get-tuple-element.54), calls=%async_computation.1 | async-start | bytes 131072 | tf_op jit(solution)/shard_map/all_to_all | solution.py:427
  36.6 2.8 %collective-permute-start = (f32[24,128]{1,0:T(8,128)S(1)}, f32[24,128]{1,0:T(8,128)S(1)}, u32[]{:S(2)}, u32[]{:S(2)}) collective-permute-start(f32[24,128]{1,0:T(8,128)S(1)} %get-tuple-element.55), channel_id=1, source_target_pairs={{0,32},{32,0},{64,96},{96,64},{128,160},{160,128},{192,224},{224,1... | collective-permute-start | bytes 36872 | tf_op jit(solution)/shard_map/ppermute | solution.py:430
  39.4 4.4 %collective-permute-start.1 = (f32[24,128]{1,0:T(8,128)S(1)}, f32[24,128]{1,0:T(8,128)S(1)}, u32[]{:S(2)}, u32[]{:S(2)}) collective-permute-start(f32[24,128]{1,0:T(8,128)S(1)} %add.6.note_ref), channel_id=1, source_target_pairs={{0,64},{32,96},{64,0},{96,32},{128,192},{160,224},{192,128},{224,1... | collective-permute-start | bytes 36872 | tf_op jit(solution)/shard_map/ppermute | solution.py:430
  46.6 21.9 %all-to-all-start.2 = ((f32[32,2,128]{2,1,0:T(2,128)}), f32[32,2,128]{2,1,0:T(2,128)S(1)}, u32[]{:S(2)}, u32[]{:S(2)}) async-start(f32[32,2,128]{2,1,0:T(2,128)} %get-tuple-element.62), calls=%async_computation.2 | async-start | bytes 65536 | tf_op jit(solution)/shard_map/all_to_all | solution.py:427
  55.5 9.7 %collective-permute-start.2 = (f32[24,128]{1,0:T(8,128)S(1)}, f32[24,128]{1,0:T(8,128)S(1)}, u32[]{:S(2)}, u32[]{:S(2)}) collective-permute-start(f32[24,128]{1,0:T(8,128)S(1)} %get-tuple-element.59.half_ref), channel_id=1, source_target_pairs={{0,128},{32,160},{64,192},{96,224},{128,0},{160,32},{192,64},{224,... | collective-permute-start | bytes 36872 | tf_op jit(solution)/shard_map/ppermute | solution.py:430
  74.2 15.0 %all-to-all-start.3 = ((f32[32,4,128]{2,1,0:T(4,128)}), f32[32,4,128]{2,1,0:T(4,128)S(1)}, u32[]{:S(2)}, u32[]{:S(2)}) async-start(f32[32,4,128]{2,1,0:T(4,128)} %get-tuple-element.64), calls=%async_computation.3 | async-start | bytes 131072 | tf_op jit(solution)/shard_map/all_to_all | solution.py:427
  81.9 2.8 %collective-permute-start.3 = (f32[24,128]{1,0:T(8,128)S(1)}, f32[24,128]{1,0:T(8,128)S(1)}, u32[]{:S(2)}, u32[]{:S(2)}) collective-permute-start(f32[24,128]{1,0:T(8,128)S(1)} %get-tuple-element.65), channel_id=1, source_target_pairs={{0,32},{32,0},{64,96},{96,64},{128,160},{160,128},{192,224},{224,1... | collective-permute-start | bytes 36872 | tf_op jit(solution)/shard_map/ppermute | solution.py:430
  84.7 3.7 %collective-permute-start.4 = (f32[24,128]{1,0:T(8,128)S(1)}, f32[24,128]{1,0:T(8,128)S(1)}, u32[]{:S(2)}, u32[]{:S(2)}) collective-permute-start(f32[24,128]{1,0:T(8,128)S(1)} %add.7.note_ref), channel_id=1, source_target_pairs={{0,64},{32,96},{64,0},{96,32},{128,192},{160,224},{192,128},{224,1... | collective-permute-start | bytes 36872 | tf_op jit(solution)/shard_map/ppermute | solution.py:430
  91.5 19.2 %all-to-all-start.4 = ((f32[32,2,128]{2,1,0:T(2,128)}), f32[32,2,128]{2,1,0:T(2,128)S(1)}, u32[]{:S(2)}, u32[]{:S(2)}) async-start(f32[32,2,128]{2,1,0:T(2,128)} %get-tuple-element.76), calls=%async_computation.4 | async-start | bytes 65536 | tf_op jit(solution)/shard_map/all_to_all | solution.py:427
  100.0 7.4 %collective-permute-start.5 = (f32[24,128]{1,0:T(8,128)S(1)}, f32[24,128]{1,0:T(8,128)S(1)}, u32[]{:S(2)}, u32[]{:S(2)}) collective-permute-start(f32[24,128]{1,0:T(8,128)S(1)} %get-tuple-element.74.half_ref), channel_id=1, source_target_pairs={{0,128},{32,160},{64,192},{96,224},{128,0},{160,32},{192,64},{224,... | collective-permute-start | bytes 36872 | tf_op jit(solution)/shard_map/ppermute | solution.py:430
  115.1 12.7 %all-to-all-start.5 = ((f32[8,24,128]{2,1,0:T(8,128)}), f32[8,24,128]{2,1,0:T(8,128)S(1)}, u32[]{:S(2)}, u32[]{:S(2)}) async-start(f32[8,24,128]{2,1,0:T(8,128)} %get-tuple-element.79), calls=%async_computation.5 | async-start | bytes 196608 | tf_op jit(solution)/shard_map/all_to_all | solution.py:517

commit v3 on v2

v3 whole, which is shorter than its diff:
```python
import functools

import jax
import jax.numpy as jnp
from jax import lax
from jax.experimental import pallas as pl
from jax.experimental.pallas import tpu as pltpu
from jax.sharding import PartitionSpec as P

GROUP = ("stn", "tm")
F32 = jnp.float32
SLOT = 4
NOTE = 8
VMEM = pl.BlockSpec(memory_space=pltpu.VMEM)
SMEM = pl.BlockSpec(memory_space=pltpu.SMEM)
HBM = pl.BlockSpec(memory_space=pltpu.HBM)
ANY = pl.BlockSpec(memory_space=pl.ANY)
PARTS = 4


def call(kernel, outs, args, scalars=0, scratch=(), aliases=None, flops=0, hbm=(), still=()):
    outs = [jax.ShapeDtypeStruct(o, F32) for o in outs]
    args = [
        pltpu.with_memory_space_constraint(x, pltpu.HBM) if n in hbm else x for n, x in enumerate(args)
    ]
    specs = [SMEM] * scalars + [VMEM] * (len(args) - scalars)
    return pl.pallas_call(
        kernel,
        out_shape=outs,
        in_specs=[
            HBM if n in hbm else ANY if (aliases or {}).get(n) in still else spec for n, spec in enumerate(specs)
        ],
        out_specs=[ANY if n in still else VMEM for n in range(len(outs))],
        scratch_shapes=list(scratch),
        input_output_aliases=aliases or {},
        compiler_params=pltpu.CompilerParams(vmem_limit_bytes=32 * 1024 * 1024),
        cost_estimate=pl.CostEstimate(flops=flops, bytes_accessed=4 * 1024 * 1024, transcendentals=0),
    )(*args)


def fetch(source, target, sems, first, parts):
    step = target.shape[0] // parts
    copies = []
    for n in range(parts):
        part = pl.ds(n * step, step)
        copies.append(pltpu.make_async_copy(source.at[part], target.at[part], sems.at[first + n]))
        copies[-1].start()
    return copies


def kept(x):
    return pltpu.with_memory_space_constraint(x, pltpu.VMEM)


def down(block, column):
    return jnp.sum(block * jnp.broadcast_to(column, block.shape), axis=0, keepdims=True)


def fold(x):
    return jnp.sum(x, axis=0, keepdims=True)


def precondition(blocks_ref, x, out_ref, copies=()):
    xt = x.T
    for i in range(x.shape[0]):
        if copies and i % (x.shape[0] // len(copies)) == 0:
            copies[i // (x.shape[0] // len(copies))].wait()
        out_ref[i : i + 1] = down(blocks_ref[i], xt[:, i : i + 1])


def first_kernel(rhs_hbm, precond_hbm, v_ref, send_ref, rhs_ref, precond_ref, sems):
    (small,) = fetch(rhs_hbm, rhs_ref, sems, PARTS, 1)
    copies = fetch(precond_hbm, precond_ref, sems, 0, PARTS)
    small.wait()
    precondition(precond_ref, rhs_ref[...], v_ref, copies)
    send_ref[...] = jnp.broadcast_to(v_ref[...][None], send_ref.shape)


def widen(x, wide_ref):
    xt = x.T
    for i in range(x.shape[0]):
        wide_ref[i] = jnp.broadcast_to(xt[:, i : i + 1], wide_ref.shape[1:])


def own_rows(i, blocks, arcs, index_ref, tiles_ref, wide_ref):
    c, j = lax.div(i, arcs), lax.rem(i, arcs)
    total = tiles_ref[i, 0] * wide_ref[c * blocks + lax.rem(index_ref[0, c, j], blocks)]
    return total + tiles_ref[i, 1] * wide_ref[c * blocks + lax.rem(index_ref[1, c, j], blocks)]


def near_kernel(comms, index_ref, v_ref, tiles_hbm, up_ref, tiles_ref, wide_ref, sems):
    count = up_ref.shape[0]
    arcs = count // comms
    blocks = v_ref.shape[0] // comms
    own = fetch(tiles_hbm.at[:, pl.ds(0, 2)], tiles_ref, sems, 0, PARTS)
    widen(v_ref[...], wide_ref)
    step = count // PARTS
    for n in range(PARTS):
        own[n].wait()

        def one(i, _):
            up_ref[pl.ds(i, 1)] = fold(own_rows(i, blocks, arcs, index_ref, tiles_ref, wide_ref))
            return 0

        lax.fori_loop(n * step, (n + 1) * step, one, 0, unroll=4)


def cap_first_kernel(cap_rhs_ref, cap_precond_ref, q_ref):
    precondition(cap_precond_ref, cap_rhs_ref[...], q_ref)


def cap_second_kernel(
    cap_rhs_ref, q0_ref, half_ref, other_ref, cap_precond_ref, yq_ref, q_ref, sums_ref
):
    caps = q0_ref.shape[0]
    note = half_ref[...] + other_ref[...]
    q0 = q0_ref[...]
    yq_ref[...] = q0 + note[:caps]
    sums_ref[...] = note[caps:]
    sums_ref[0:1] += fold(cap_rhs_ref[...] * q0)
    sums_ref[1:2] += fold(q0 * q0)
    precondition(cap_precond_ref, yq_ref[...], q_ref)


def cap_third_kernel(
    alpha_ref, cap_rhs_ref, q0_ref, yq0_ref, q1_ref, half_ref, other_ref, cap_precond_ref,
    zq_ref, yzq_ref, rq_ref, q_ref, sums_ref,
):
    caps = q0_ref.shape[0]
    alpha = alpha_ref[0:1]
    yq0, q1 = yq0_ref[...], q1_ref[...]
    yq1 = q1 + half_ref[:caps] + other_ref[:caps]
    zq = q0_ref[...] - alpha * q1
    yzq = yq0 - alpha * yq1
    rq = cap_rhs_ref[...] - alpha * yq0
    zq_ref[...] = zq
    yzq_ref[...] = yzq
    rq_ref[...] = rq
    precondition(cap_precond_ref, alpha * yzq, q_ref)
    q = q_ref[...]
    pairs = ((zq, yq0), (zq, yzq), (q, yq0), (q, yzq), (q, q), (zq, rq), (q, rq))
    for n, (one, other) in enumerate(pairs):
        sums_ref[n : n + 1] = fold(one * other)
    sums_ref[7:8] = jnp.zeros_like(sums_ref[7:8])


def beside(block, row, lane, n, total):
    return jnp.where(lane == n, jnp.sum(block * row, axis=1, keepdims=True), total)


def arcs_up(comms, blocks, index_ref, cap_index_ref, up_ref, got_ref, q_ref, scale_ref, tiles_hbm, cap_tiles_hbm,
            scaled_ref, note_ref, far_ref, third_ref, cap_tiles_ref, wide_ref, turn_ref, sems):
    count = up_ref.shape[0]
    arcs = count // comms
    width = scale_ref.shape[1]
    thirds = fetch(tiles_hbm.at[:, 2], third_ref, sems, 0, PARTS)
    caps_in = fetch(cap_tiles_hbm, cap_tiles_ref, sems, PARTS, PARTS)

    def place(i, _):
        c, j = lax.div(i, arcs), lax.rem(i, arcs)
        far = index_ref[2, c, j]
        row = c if got_ref.shape[1] == comms else c * blocks + lax.rem(far, blocks)
        far_ref[pl.ds(i, 1)] = got_ref[lax.div(far, blocks), pl.ds(row, 1)]
        return 0

    lax.fori_loop(0, count, place, 0, unroll=4)
    widen(q_ref[...], wide_ref)
    ft = far_ref[...].T
    step = count // PARTS
    for i in range(count):
        if i % step == 0:
            thirds[i // step].wait()
            caps_in[i // step].wait()
        column = jnp.broadcast_to(ft[:, i : i + 1], third_ref.shape[1:])
        total = third_ref[i] * column + cap_tiles_ref[i] * wide_ref[cap_index_ref[i // arcs, i % arcs]]
        far_ref[i : i + 1] = up_ref[i : i + 1] + fold(total)
    upward = far_ref[...]
    scaled = scale_ref[...] * upward
    scaled_ref[...] = scaled
    lane = lax.broadcasted_iota(jnp.int32, (width, width), 1)

    def one(i, total):
        return beside(cap_tiles_ref[i], scaled_ref[pl.ds(i, 1)], lane, i, total)

    turn_ref[...] = lax.fori_loop(0, count, one, jnp.zeros((width, width), F32), unroll=2).T
    note_ref[...] = jnp.zeros_like(note_ref)

    def put(i, _):
        cap = cap_index_ref[lax.div(i, arcs), lax.rem(i, arcs)]
        note_ref[pl.ds(cap, 1)] += turn_ref[pl.ds(i, 1)]
        return 0

    lax.fori_loop(0, count, put, 0, unroll=4)
    return fold(upward * scaled)


def up_first_kernel(comms, blocks, caps, index_ref, cap_index_ref, up_ref, got_ref, q_ref, scale_ref, rhs_ref, v_ref,
                    tiles_hbm, cap_tiles_hbm, scaled_ref, note_ref, *room):
    energy = arcs_up(comms, blocks, index_ref, cap_index_ref, up_ref, got_ref, q_ref, scale_ref, tiles_hbm,
                     cap_tiles_hbm, scaled_ref, note_ref, *room)
    v = v_ref[...]
    note_ref[caps : caps + 1] = fold(rhs_ref[...] * v)
    note_ref[caps + 1 : caps + 2] = fold(v * v) + energy


def up_second_kernel(comms, blocks, index_ref, cap_index_ref, up_ref, got_ref, q_ref, scale_ref, tiles_hbm,
                     cap_tiles_hbm, scaled_ref, note_ref, *room):
    arcs_up(comms, blocks, index_ref, cap_index_ref, up_ref, got_ref, q_ref, scale_ref, tiles_hbm,
            cap_tiles_hbm, scaled_ref, note_ref, *room)


def up_third_kernel(comms, blocks, caps, index_ref, cap_index_ref, up_ref, got_ref, q_ref, scale_ref, z_ref, yz_ref,
                    r_ref, y0_ref, v_ref, tiles_hbm, cap_tiles_hbm, scaled_ref, notes_ref, note_ref, *room):
    energy = arcs_up(comms, blocks, index_ref, cap_index_ref, up_ref, got_ref, q_ref, scale_ref, tiles_hbm,
                     cap_tiles_hbm, scaled_ref, note_ref, *room)
    z, yz, r, y0, v = z_ref[...], yz_ref[...], r_ref[...], y0_ref[...], v_ref[...]
    pairs = ((z, y0), (z, yz), (v, y0), (v, yz), (v, v), (z, r), (v, r))
    for n, (one, other) in enumerate(pairs):
        note_ref[caps + n : caps + n + 1] = fold(one * other)
    note_ref[caps + 4 : caps + 5] += energy
    notes_ref[...] = jnp.broadcast_to(note_ref[...][None], notes_ref.shape)


def down_kernel(comms, blocks, step_number, index_ref, scaled_ref, sums_ref, tiles_hbm, local_ref, back_ref,
                tiles_ref, turn_ref, sems):
    count, touched = tiles_ref.shape[:2]
    width = tiles_ref.shape[3]
    arcs = count // comms
    parts = 2 * PARTS
    step = count // parts
    copies = fetch(tiles_hbm, tiles_ref, sems, 0, parts)
    local_ref[...] = jnp.zeros_like(local_ref)
    if step_number == 0:
        back_ref[...] = jnp.full(back_ref.shape, -1.0, F32)
    lane = lax.broadcasted_iota(jnp.int32, (width, width), 1)
    total = jnp.zeros((width, width), F32)
    for n in range(parts):
        copies[n].wait()

        def one(i, total):
            row = scaled_ref[pl.ds(i, 1)]
            for k in range(touched):
                total = beside(tiles_ref[i, k], row, lane, k * count + i, total)
            return total

        total = lax.fori_loop(n * step, (n + 1) * step, one, total)
    turn_ref[...] = total.T

    def put(i, _):
        c, j = lax.div(i, arcs), lax.rem(i, arcs)
        for k in range(2):
            b = c * blocks + lax.rem(index_ref[k, c, j], blocks)
            local_ref[pl.ds(b, 1)] += turn_ref[pl.ds(k * count + i, 1)]
        far = index_ref[2, c, j]
        to = lax.div(far, blocks)
        back_ref[to, pl.ds(c, 1)] = turn_ref[pl.ds(2 * count + i, 1)]
        if step_number == 0:
            local = lax.rem(far, blocks).astype(F32)
            back_ref[to, pl.ds(comms + c, 1)] = jnp.full((1, width), local, F32)
        return 0

    lax.fori_loop(0, count, put, 0, unroll=4)
    if step_number == 1:
        shape = (back_ref.shape[0], 2, width)
        back_ref[:, comms : comms + 2] = jnp.broadcast_to(sums_ref[0:2][None], shape)


def add_kernel(note_ref, other_ref, back_ref, out_ref, same_ref):
    del back_ref, same_ref
    out_ref[...] = note_ref[...] + other_ref[...]


def insert_kernel(comms, caps, notes_ref, sums_ref, back_ref, cap_ref, out_ref):
    del back_ref
    total = jnp.sum(notes_ref[...], axis=0)
    cap_ref[...] = total[:caps]
    sums = jnp.sum(total[caps:] + sums_ref[...], axis=1, keepdims=True)
    width = out_ref.shape[2]
    pick = lax.broadcasted_iota(jnp.int32, (NOTE, width), 0) == lax.broadcasted_iota(
        jnp.int32, (NOTE, width), 1
    )
    row = fold(jnp.where(pick, jnp.broadcast_to(sums, (NOTE, width)), 0.0))
    out_ref[:, comms : comms + 1] = jnp.broadcast_to(row[None], (out_ref.shape[0], 1, width))


def collect(comms, v_ref, local_ref, back_ref, asked, y_ref):
    blocks = v_ref.shape[0] // comms
    for c in range(comms):
        part = back_ref[:, c]
        for b in range(blocks):
            n = c * blocks + b
            came = fold(jnp.where(asked[c] == b, part, 0.0))
            y_ref[n : n + 1] = v_ref[n : n + 1] + local_ref[n : n + 1] + came


def pack(comms, v_ref, asked, send_ref):
    blocks = v_ref.shape[0] // comms
    for c in range(comms):
        row = jnp.zeros_like(asked[c])
        for b in range(blocks):
            n = c * blocks + b
            row = jnp.where(asked[c] == b, v_ref[n : n + 1], row)
        send_ref[:, c] = row


def rows_second_kernel(comms, v0_ref, local_ref, back_ref, note_ref, came_ref, precond_ref, half_ref, y_ref,
                       v_ref, send_ref, asked_ref):
    half_ref[...] = note_ref[...] + came_ref[...]
    asked = [back_ref[:, comms + c] for c in range(comms)]
    for c in range(comms):
        asked_ref[c] = asked[c]
    collect(comms, v0_ref, local_ref, back_ref, asked, y_ref)
    precondition(precond_ref, y_ref[...], v_ref)
    pack(comms, v_ref, asked, send_ref)


def rows_third_kernel(comms, rhs_ref, v0_ref, y0_ref, v1_ref, local_ref, back_ref, note_ref, came_ref, asked_ref,
                      precond_ref, half_ref, alpha_ref, z_ref, yz_ref, r_ref, v_ref, send_ref):
    half_ref[...] = note_ref[...] + came_ref[...]
    asked = [asked_ref[c] for c in range(comms)]
    collect(comms, v1_ref, local_ref, back_ref, asked, yz_ref)
    first = jnp.sum(fold(back_ref[:, comms]), axis=1, keepdims=True)
    second = jnp.sum(fold(back_ref[:, comms + 1]), axis=1, keepdims=True)
    alpha = jnp.broadcast_to(first / second, (1, alpha_ref.shape[1]))
    alpha_ref[...] = jnp.broadcast_to(alpha, alpha_ref.shape)
    alpha_ref[1:2] = jnp.broadcast_to(second, (1, alpha_ref.shape[1]))
    y0 = y0_ref[...]
    z_ref[...] = v0_ref[...] - alpha * v1_ref[...]
    yz = y0 - alpha * yz_ref[...]
    yz_ref[...] = yz
    r_ref[...] = rhs_ref[...] - alpha * y0
    precondition(precond_ref, alpha * yz, v_ref)
    pack(comms, v_ref, asked, send_ref)


def last_kernel(comms, alpha_ref, v0_ref, y0_ref, z_ref, yz_ref, r_ref, v2_ref, local_ref, back_ref,
                asked_ref, q0_ref, yq0_ref, zq_ref, yzq_ref, rq_ref, q2_ref, cap_ref,
                sol_ref, cap_sol_ref, res_ref, cap_res_ref, y_ref):
    asked = [asked_ref[c] for c in range(comms)]
    collect(comms, v2_ref, local_ref, back_ref, asked, y_ref)
    row = fold(back_ref[:, comms])
    width = row.shape[1]
    lane = lax.broadcasted_iota(jnp.int32, row.shape, 1)
    s = [
        jnp.broadcast_to(
            jnp.sum(jnp.where(lane == n, row, 0.0), axis=1, keepdims=True), (1, width)
        )
        for n in range(7)
    ]
    alpha, h00 = alpha_ref[0:1], alpha_ref[1:2]
    h1, h2 = s[0] / h00, s[2] / h00
    a11 = s[1] - h1 * s[0]
    a12 = s[3] - h1 * s[2]
    a22 = s[4] - h2 * s[2]
    lower = a12 / a11
    c2 = (s[6] - lower * s[5]) / (a22 - lower * a12)
    c1 = s[5] / a11 - lower * c2
    c0 = c1 * h1 + c2 * h2
    sol_ref[...] = (alpha - c0) * v0_ref[...] + c1 * z_ref[...] + c2 * v2_ref[...]
    cap_sol_ref[...] = (alpha - c0) * q0_ref[...] + c1 * zq_ref[...] + c2 * q2_ref[...]
    res_ref[...] = r_ref[...] + c0 * y0_ref[...] - c1 * yz_ref[...] - c2 * y_ref[...]
    yq2 = q2_ref[...] + cap_ref[...]
    cap_res_ref[...] = rq_ref[...] + c0 * yq0_ref[...] - c1 * yzq_ref[...] - c2 * yq2


def body(
    tiles, cap_tiles, row_index, cap_index, arc_scale, rows_rhs, cap_rhs, precond, cap_precond
):
    comms, arcs, touched = row_index.shape
    blocks, width = rows_rhs.shape[1:]
    caps = cap_rhs.shape[0]
    groups = lax.axis_size("stn") * lax.axis_size("tm")
    peers = lax.axis_size("comm")
    rows, count = comms * blocks, comms * arcs
    flat = (width, width)
    tiles = tiles.reshape(count, touched, *flat)
    cap_tiles = cap_tiles.reshape(count, *flat)
    precond = precond.reshape(rows, *flat)
    index = jnp.transpose(row_index, (2, 0, 1))
    scale = arc_scale.reshape(count, width)
    rhs = rows_rhs.reshape(rows, width)
    row_shape, cap_shape, arc_shape = (rows, width), (caps, width), (count, width)
    small = (NOTE, width)
    note_shape = (caps + NOTE, width)
    send_shape = (groups, comms, width)
    back_shape = (groups, SLOT, width)
    unit = 2 * count * width * width

    def room(*shape):
        return pltpu.VMEM(shape, F32)

    def sems(n):
        return pltpu.SemaphoreType.DMA((n,))

    def exchange(x):
        return lax.all_to_all(x, GROUP, 0, 0)

    def across(x, step):
        return lax.ppermute(x, "comm", [(i, i ^ step) for i in range(peers)])

    def near(v):
        (up,) = call(
            functools.partial(near_kernel, comms), [arc_shape], (index, v, tiles), 1,
            [room(count, 2, *flat), room(rows, *flat), sems(PARTS)], flops=2 * unit, hbm=(2,),
        )
        return up

    up_room = [
        room(*arc_shape), room(count, *flat), room(count, *flat), room(caps, *flat), room(*flat), sems(2 * PARTS),
    ]

    def spread(step_number, scaled, sums):
        return call(
            functools.partial(down_kernel, comms, blocks, step_number), [row_shape, back_shape],
            (index, scaled, sums, tiles), 1,
            [room(count, touched, *flat), room(*flat), sems(2 * PARTS)], flops=3 * unit, hbm=(3,),
        )

    def add(note, other, back):
        return call(add_kernel, [note_shape, back_shape], (note, other, back), aliases={2: 1}, still=(1,))

    v0, send = call(
        first_kernel, [row_shape, (groups, rows, width)], (rhs, precond), 0,
        [room(*row_shape), room(rows, *flat), sems(PARTS + 1)], hbm=(0, 1),
    )
    got = exchange(send)
    up = near(v0)
    (q0,) = call(cap_first_kernel, [cap_shape], (cap_rhs, kept(cap_precond)), flops=unit)
    scaled, note = call(
        functools.partial(up_first_kernel, comms, blocks, caps), [arc_shape, note_shape],
        (index, cap_index, up, got, q0, scale, rhs, v0, tiles, cap_tiles), 2, up_room, flops=3 * unit, hbm=(8, 9),
    )
    other = across(note, 4)
    local, back = spread(0, scaled, rhs)
    note, back = add(note, other, back)
    back = exchange(back)
    half, y0, v1, send, asked = call(
        functools.partial(rows_second_kernel, comms),
        [note_shape, row_shape, row_shape, send_shape, (comms, groups, width)],
        (v0, local, back, note, across(note, 1), kept(precond)),
    )
    got = exchange(send)
    other = across(half, 2)
    up = near(v1)
    yq0, q1, sums = call(
        cap_second_kernel, [cap_shape, cap_shape, small], (cap_rhs, q0, half, other, kept(cap_precond)), flops=unit,
    )
    scaled, note = call(
        functools.partial(up_second_kernel, comms, blocks), [arc_shape, note_shape],
        (index, cap_index, up, got, q1, scale, tiles, cap_tiles), 2, up_room, flops=3 * unit, hbm=(6, 7),
    )
    other = across(note, 4)
    local, back = spread(1, scaled, sums)
    note, back = add(note, other, back)
    back = exchange(back)
    half, alpha, z1, yz, r1, v2, send = call(
        functools.partial(rows_third_kernel, comms),
        [note_shape, small, row_shape, row_shape, row_shape, row_shape, send_shape],
        (rhs, v0, y0, v1, local, back, note, across(note, 1), asked, kept(precond)),
    )
    got = exchange(send)
    other = across(half, 2)
    up = near(v2)
    zq1, yzq, rq1, q2, sums = call(
        cap_third_kernel, [cap_shape] * 4 + [small],
        (alpha, cap_rhs, q0, yq0, q1, half, other, kept(cap_precond)), flops=unit,
    )
    scaled, notes = call(
        functools.partial(up_third_kernel, comms, blocks, caps), [arc_shape, (peers, *note_shape)],
        (index, cap_index, up, got, q2, scale, z1, yz, r1, y0, v2, tiles, cap_tiles), 2,
        [room(*note_shape), *up_room], flops=3 * unit, hbm=(11, 12),
    )
    notes = lax.all_to_all(notes, "comm", 0, 0)
    local, back = spread(2, scaled, sums)
    cap_sum, back = call(
        functools.partial(insert_kernel, comms, caps), [cap_shape, back_shape], (notes, sums, back),
        aliases={2: 1},
    )
    back = exchange(back)
    sol, cap_sol, res, cap_res = call(
        functools.partial(last_kernel, comms), [row_shape, cap_shape, row_shape, cap_shape],
        (alpha, v0, y0, z1, yz, r1, v2, local, back, asked, q0, yq0, zq1, yzq, rq1, q2, cap_sum), 0,
        [pltpu.VMEM(row_shape, F32)],
    )
    return sol.reshape(rows_rhs.shape), cap_sol, res.reshape(rows_rhs.shape), cap_res


def solution(mesh):
    placed = (
        P("comm", GROUP, None, None, None),
        P("comm", GROUP, None, None),
        P("comm", GROUP, None),
        P("comm", GROUP),
        P("comm", GROUP, None),
        P("comm", GROUP, None),
        P(GROUP, None),
        P("comm", GROUP, None, None),
        P(GROUP, None, None),
    )
    return jax.shard_map(
        body,
        mesh=mesh,
        in_specs=placed,
        out_specs=(
            P("comm", GROUP, None),
            P(GROUP, None),
            P("comm", GROUP, None),
            P(GROUP, None),
        ),
        check_vma=False,
    )
```

time: 146 us -> 138 us (0.945)
  starting transfers between devices: 64.1 us -> 45.7 us
  waiting for transfers between devices: 11.8 us -> 21.3 us
  Pallas kernels: 49.8 us -> 53.2 us
  blocking collectives: 16.8 us -> 14 us
    all_to_all x5, waiting for transfers between devices: 0.93 us -> 17.1 us  [exchange(): return lax.all_to_all(x, GROUP, 0, 0)]
    all_to_all x5, starting transfers between devices: 41 us -> 26.9 us  [exchange(): return lax.all_to_all(x, GROUP, 0, 0)]
    ppermute x6, starting transfers between devices: 17.9 us -> 12.4 us  [across(): return lax.ppermute(x, 'comm', [(i, i ^ step) for i in range(peers)])]
    ppermute x6, waiting for transfers between devices: 6.98 us -> 3.08 us  [across(): return lax.ppermute(x, 'comm', [(i, i ^ step) for i in range(peers)])]
    pallas_call x14 -> x19, Pallas kernels: 49.8 us -> 53.2 us  [call(): pl.pallas_call(kernel, out_shape=outs, in_specs=[HBM if n in hbm else ANY...]
    all_to_all x1, waiting for transfers between devices: 3.9 us -> 1.09 us  [body(): notes = lax.all_to_all(notes, 'comm', 0, 0)]
    all_to_all x1, blocking collectives: 16.8 us -> 14 us  [exchange(): return lax.all_to_all(x, GROUP, 0, 0)]
  transfers between devices with their start and end apart: 12 -> 12, of which waited for: 7 -> 8; matrix products, arithmetic and copies ran while one was open for 0% -> 0% of each run, Pallas kernels for 18% -> 22%
where the time goes in v3:
time: 138 us
  Pallas kernels  53.2 us (39%)
  starting transfers between devices  45.7 us (33%)
  waiting for transfers between devices  21.3 us (15%)
  blocking collectives  14 us (10%)
  local copies, waits for them, and re-layouts  2.63 us (2%)
    pallas_call x19, Pallas kernels, call(): pl.pallas_call(kernel, out_shape=outs, in_specs=[HBM if n in hbm else ANY...  53.2 us
    all_to_all x5, starting transfers between devices, exchange(): return lax.all_to_all(x, GROUP, 0, 0)  26.9 us
    all_to_all x5, waiting for transfers between devices, exchange(): return lax.all_to_all(x, GROUP, 0, 0)  17.1 us
    all_to_all x1, blocking collectives, exchange(): return lax.all_to_all(x, GROUP, 0, 0)  14 us
    ppermute x6, starting transfers between devices, across(): return lax.ppermute(x, 'comm', [(i, i ^ step) for i in range(peers)])  12.4 us
    all_to_all x1, starting transfers between devices, body(): notes = lax.all_to_all(notes, 'comm', 0, 0)  6.37 us
    ppermute x6, waiting for transfers between devices, across(): return lax.ppermute(x, 'comm', [(i, i ^ step) for i in range(peers)])  3.08 us
  transfers between devices with their start and end apart: 12, of which 8 were waited for; matrix products, arithmetic and copies ran while one was open for 0% of the time, Pallas kernels for 22%

profile of v3, /device:TPU:1, one launch (start us, length us, event | category | flops | bytes accessed | tf_op | source)
XLA Modules:
  0.0 137.8 jit_solution(2844640750177511890)
XLA Ops:
  0.7 2.3 %shard_map.120 = (f32[16,128]{1,0:T(8,128)S(1)}, f32[32,16,128]{2,1,0:T(8,128)}) custom-call(f32[16,128]{1,0:T(8,128)} %bitcast.23, f32[16,128,128]{2,1,0:T(8,128)} %bitcast.8), custom_call_target="tpu_custom_call" | custom-call | bytes 4194304 | tf_op jit(solution)/shard_map/pallas_call | solution.py:27
  3.0 8.6 %all-to-all-start = ((f32[32,16,128]{2,1,0:T(8,128)}), f32[32,16,128]{2,1,0:T(8,128)S(1)}, u32[]{:S(2)}, u32[]{:S(2)}) async-start(f32[32,16,128]{2,1,0:T(8,128)} %get-tuple-element.49), calls=%async_computation | async-start | bytes 524288 | tf_op jit(solution)/shard_map/all_to_all | solution.py:396
  11.6 1.2 copy-done.1
  14.7 2.9 %shard_map.121.up_ref = f32[32,128]{1,0:T(8,128)S(1)} custom-call(s32[3,2,16]{2,1,0:T(2,128)S(1)} %bitcast.11, f32[16,128]{1,0:T(8,128)S(1)} %get-tuple-element.48.v_ref.v0_ref, f32[32,3,128,128]{3,2,1,0:T(8,128)} %bitcast.27), custom_call_target="tpu_custom_call" | custom-call | flops 2097152 | bytes 4194304 | tf_op jit(solution)/shard_map/pallas_call | solution.py:27
  17.6 2.9 %all-to-all-done.got_ref = f32[32,16,128]{2,1,0:T(8,128)S(1)} async-done(((f32[32,16,128]{2,1,0:T(8,128)}), f32[32,16,128]{2,1,0:T(8,128)S(1)}, u32[]{:S(2)}, u32[]{:S(2)}) %all-to-all-start) | async-done | bytes 262176 | tf_op jit(solution)/shard_map/all_to_all | solution.py:396
  20.5 5.3 %shard_map.123 = (f32[32,128]{1,0:T(8,128)S(1)}, f32[24,128]{1,0:T(8,128)S(1)}) custom-call(s32[3,2,16]{2,1,0:T(2,128)S(1)} %bitcast.12, s32[2,16]{1,0:T(2,128)S(1)} %copy-done.9, f32[32,128]{1,0:T(8,128)S(1)} %shard_map.121.up_ref, f32[32,16,128]{2,1,0:T(8,128)S(1)} %all-to-all-done.got_ref, f32[16,128]{1,0:T(8,128)S(1)} %shard_map.122.q_ref.q0_ref, ...), custom_call_target="tpu_custom_call" | custom-call | flops 3145728 | bytes 4194304 | tf_op jit(solution)/shard_map/pallas_call | solution.py:27
  25.9 7.0 %collective-permute-start = (f32[24,128]{1,0:T(8,128)S(1)}, f32[24,128]{1,0:T(8,128)S(1)}, u32[]{:S(2)}, u32[]{:S(2)}) collective-permute-start(f32[24,128]{1,0:T(8,128)S(1)} %get-tuple-element.52.note_ref), channel_id=1, source_target_pairs={{0,128},{32,160},{64,192},{96,224},{128,0},{160,32},{192,64},{224,... | collective-permute-start | bytes 36872 | tf_op jit(solution)/shard_map/ppermute | solution.py:399
  32.9 7.0 %shard_map.124 = (f32[16,128]{1,0:T(8,128)S(1)}, f32[32,4,128]{2,1,0:T(4,128)}) custom-call(s32[3,2,16]{2,1,0:T(2,128)S(1)} %bitcast.13, f32[32,128]{1,0:T(8,128)S(1)} %get-tuple-element.50.scaled_ref, f32[16,128]{1,0:T(8,128)S(1)} %bitcast.25, f32[32,3,128,128]{3,2,1,0:T(8,128)} %bitcast.29), custom_call_target="tpu_custom_call" | custom-call | flops 3145728 | bytes 4194304 | tf_op jit(solution)/shard_map/pallas_call | solution.py:27
  39.9 4.8 %all-to-all-start.1 = ((f32[32,4,128]{2,1,0:T(4,128)}), f32[32,4,128]{2,1,0:T(4,128)S(1)}, u32[]{:S(2)}, u32[]{:S(2)}) async-start(f32[32,4,128]{2,1,0:T(4,128)} %get-tuple-element.54), calls=%async_computation.1 | async-start | bytes 131072 | tf_op jit(solution)/shard_map/all_to_all | solution.py:396
  45.6 2.0 %collective-permute-done.1.came_ref = f32[24,128]{1,0:T(8,128)S(1)} collective-permute-done((f32[24,128]{1,0:T(8,128)S(1)}, f32[24,128]{1,0:T(8,128)S(1)}, u32[]{:S(2)}, u32[]{:S(2)}) %collective-permute-start.1) | collective-permute-done | bytes 12320 | tf_op jit(solution)/shard_map/ppermute | solution.py:399
  47.5 4.5 %all-to-all-done.1.back_ref = f32[32,4,128]{2,1,0:T(4,128)S(1)} async-done(((f32[32,4,128]{2,1,0:T(4,128)}), f32[32,4,128]{2,1,0:T(4,128)S(1)}, u32[]{:S(2)}, u32[]{:S(2)}) %all-to-all-start.1) | async-done | bytes 65568 | tf_op jit(solution)/shard_map/all_to_all | solution.py:396
  52.1 1.6 %shard_map.126 = (f32[24,128]{1,0:T(8,128)S(1)}, f32[16,128]{1,0:T(8,128)S(1)}, f32[16,128]{1,0:T(8,128)S(1)}, f32[32,2,128]{2,1,0:T(2,128)}, f32[2,32,128]{2,1,0:T(8,128)S(1)}) custom-call(f32[16,128]{1,0:T(8,128)S(1)} %get-tuple-element.48.v_ref.v0_ref, f32[16,128]{1,0:T(8,128)S(1)} %get-tuple-element.51.local_ref, ...), custom_call_target="tpu_custom_call" | custom-call | bytes 4194304 | tf_op jit(solution)/shard_map/pallas_call | solution.py:27
  53.7 3.9 %all-to-all-start.2 = ((f32[32,2,128]{2,1,0:T(2,128)}), f32[32,2,128]{2,1,0:T(2,128)S(1)}, u32[]{:S(2)}, u32[]{:S(2)}) async-start(f32[32,2,128]{2,1,0:T(2,128)} %get-tuple-element.58), calls=%async_computation.2 | async-start | bytes 65536 | tf_op jit(solution)/shard_map/all_to_all | solution.py:396
  57.5 1.3 collective-permute-start.2
  58.8 2.9 %shard_map.127.up_ref = f32[32,128]{1,0:T(8,128)S(1)} custom-call(s32[3,2,16]{2,1,0:T(2,128)S(1)} %bitcast.14, f32[16,128]{1,0:T(8,128)S(1)} %get-tuple-element.57.v_ref.v1_ref, f32[32,3,128,128]{3,2,1,0:T(8,128)} %bitcast.30), custom_call_target="tpu_custom_call" | custom-call | flops 2097152 | bytes 4194304 | tf_op jit(solution)/shard_map/pallas_call | solution.py:27
  62.2 2.6 %all-to-all-done.2.got_ref = f32[32,2,128]{2,1,0:T(2,128)S(1)} async-done(((f32[32,2,128]{2,1,0:T(2,128)}), f32[32,2,128]{2,1,0:T(2,128)S(1)}, u32[]{:S(2)}, u32[]{:S(2)}) %all-to-all-start.2) | async-done | bytes 32800 | tf_op jit(solution)/shard_map/all_to_all | solution.py:396
  64.9 5.3 %shard_map.129 = (f32[32,128]{1,0:T(8,128)S(1)}, f32[24,128]{1,0:T(8,128)S(1)}) custom-call(s32[3,2,16]{2,1,0:T(2,128)S(1)} %bitcast.15, s32[2,16]{1,0:T(2,128)S(1)} %copy-done.9, f32[32,128]{1,0:T(8,128)S(1)} %shard_map.127.up_ref, f32[32,2,128]{2,1,0:T(2,128)S(1)} %all-to-all-done.2.got_ref, f32[16,128]{1,0:T(8,128)S(1)} %get-tuple-element.60.q_ref.q1_ref, ...), custom_call_target="tpu_custom_call" | custom-call | flops 3145728 | bytes 4194304 | tf_op jit(solution)/shard_map/pallas_call | solution.py:27
  70.5 7.0 %shard_map.130 = (f32[16,128]{1,0:T(8,128)S(1)}, f32[32,4,128]{2,1,0:T(4,128)}) custom-call(s32[3,2,16]{2,1,0:T(2,128)S(1)} %bitcast.16, f32[32,128]{1,0:T(8,128)S(1)} %get-tuple-element.61.scaled_ref, f32[8,128]{1,0:T(8,128)S(1)} %get-tuple-element.62.sums_ref, f32[32,3,128,128]{3,2,1,0:T(8,128)} %bitcast.32), custom_call_target="tpu_custom_call" | custom-call | flops 3145728 | bytes 4194304 | tf_op jit(solution)/shard_map/pallas_call | solution.py:27
  77.6 5.6 %all-to-all-start.3 = ((f32[32,4,128]{2,1,0:T(4,128)}), f32[32,4,128]{2,1,0:T(4,128)S(1)}, u32[]{:S(2)}, u32[]{:S(2)}) async-start(f32[32,4,128]{2,1,0:T(4,128)} %get-tuple-element.66), calls=%async_computation.3 | async-start | bytes 131072 | tf_op jit(solution)/shard_map/all_to_all | solution.py:396
  83.2 1.7 %collective-permute-start.4 = (f32[24,128]{1,0:T(8,128)S(1)}, f32[24,128]{1,0:T(8,128)S(1)}, u32[]{:S(2)}, u32[]{:S(2)}) collective-permute-start(f32[24,128]{1,0:T(8,128)S(1)} %get-tuple-element.67.note_ref), channel_id=1, source_target_pairs={{0,32},{32,0},{64,96},{96,64},{128,160},{160,128},{192,224},{224,1... | collective-permute-start | bytes 36872 | tf_op jit(solution)/shard_map/ppermute | solution.py:399
  84.9 1.1 collective-permute-done.4.came_ref
  86.0 4.5 %all-to-all-done.3.back_ref = f32[32,4,128]{2,1,0:T(4,128)S(1)} async-done(((f32[32,4,128]{2,1,0:T(4,128)}), f32[32,4,128]{2,1,0:T(4,128)S(1)}, u32[]{:S(2)}, u32[]{:S(2)}) %all-to-all-start.3) | async-done | bytes 65568 | tf_op jit(solution)/shard_map/all_to_all | solution.py:396
  90.5 1.2 shard_map.132
  91.7 4.0 %all-to-all-start.4 = ((f32[32,2,128]{2,1,0:T(2,128)}), f32[32,2,128]{2,1,0:T(2,128)S(1)}, u32[]{:S(2)}, u32[]{:S(2)}) async-start(f32[32,2,128]{2,1,0:T(2,128)} %get-tuple-element.74), calls=%async_computation.4 | async-start | bytes 65536 | tf_op jit(solution)/shard_map/all_to_all | solution.py:396
  95.8 1.3 collective-permute-start.5
  97.1 2.9 %shard_map.133.up_ref = f32[32,128]{1,0:T(8,128)S(1)} custom-call(s32[3,2,16]{2,1,0:T(2,128)S(1)} %bitcast.17, f32[16,128]{1,0:T(8,128)S(1)} %get-tuple-element.73.v_ref.v2_ref, f32[32,3,128,128]{3,2,1,0:T(8,128)} %bitcast.33), custom_call_target="tpu_custom_call" | custom-call | flops 2097152 | bytes 4194304 | tf_op jit(solution)/shard_map/pallas_call | solution.py:27
  100.5 2.5 %all-to-all-done.4.got_ref = f32[32,2,128]{2,1,0:T(2,128)S(1)} async-done(((f32[32,2,128]{2,1,0:T(2,128)}), f32[32,2,128]{2,1,0:T(2,128)S(1)}, u32[]{:S(2)}, u32[]{:S(2)}) %all-to-all-start.4) | async-done | bytes 32800 | tf_op jit(solution)/shard_map/all_to_all | solution.py:396
  103.0 6.1 %shard_map.135 = (f32[32,128]{1,0:T(8,128)S(1)}, f32[8,24,128]{2,1,0:T(8,128)}) custom-call(s32[3,2,16]{2,1,0:T(2,128)S(1)} %bitcast.18, s32[2,16]{1,0:T(2,128)S(1)} %copy-done.9, f32[32,128]{1,0:T(8,128)S(1)} %shard_map.133.up_ref, f32[32,2,128]{2,1,0:T(2,128)S(1)} %all-to-all-done.4.got_ref, f32[16,128]{1,0:T(8,128)S(1)} %get-tuple-element.77.q_ref.q2_ref, ...), custom_call_target="tpu_custom_call" | custom-call | flops 3145728 | bytes 4194304 | tf_op jit(solution)/shard_map/pallas_call | solution.py:27
  109.1 6.4 %all-to-all-start.5 = ((f32[8,24,128]{2,1,0:T(8,128)}), f32[8,24,128]{2,1,0:T(8,128)S(1)}, u32[]{:S(2)}, u32[]{:S(2)}) async-start(f32[8,24,128]{2,1,0:T(8,128)} %get-tuple-element.81), calls=%async_computation.5 | async-start | bytes 196608 | tf_op jit(solution)/shard_map/all_to_all | solution.py:473
  115.5 6.4 %shard_map.136 = (f32[16,128]{1,0:T(8,128)S(1)}, f32[32,4,128]{2,1,0:T(4,128)S(1)}) custom-call(s32[3,2,16]{2,1,0:T(2,128)S(1)} %bitcast.19, f32[32,128]{1,0:T(8,128)S(1)} %get-tuple-element.78.scaled_ref, f32[8,128]{1,0:T(8,128)S(1)} %get-tuple-element.79.sums_ref, f32[32,3,128,128]{3,2,1,0:T(8,128)} %bitcast.35), custom_call_target="tpu_custom_call" | custom-call | flops 3145728 | bytes 4194304 | tf_op jit(solution)/shard_map/pallas_call | solution.py:27
  121.8 1.1 all-to-all-done.5.notes_ref
  123.0 14.0 %all_to_all.35.back_ref = f32[32,4,128]{2,1,0:T(4,128)S(1)} all-to-all(f32[32,4,128]{2,1,0:T(4,128)S(1)} %get-tuple-element.83), channel_id=1, replica_groups=mesh['comm'=8,'stn'=16,'tm'=2] {'stn','tm'}, dimensions={0} | all-to-all | bytes 131072 | tf_op jit(solution)/shard_map/all_to_all | solution.py:396
  (32 shorter events, 4.9 us)
Async XLA Ops:
  0.6 19.9 %copy-start.6 = (f32[2,8,128]{2,1,0:T(8,128)S(1)}, f32[2,8,128]{2,1,0:T(8,128)}, u32[]{:S(2)}) copy-start(f32[2,8,128]{2,1,0:T(8,128)} %param.14) | copy-start | bytes 24580
  0.6 19.9 %copy-start.4 = (s32[2,16,3]{1,0,2:T(2,128)S(1)}, s32[2,16,3]{1,0,2:T(2,128)}, u32[]{:S(2)}) copy-start(s32[2,16,3]{1,0,2:T(2,128)} %param.11) | copy-start | bytes 1156
  0.7 19.9 %copy-start.9 = (s32[2,16]{1,0:T(2,128)S(1)}, s32[2,16]{1,0:T(2,128)}, u32[]{:S(2)}) copy-start(s32[2,16]{1,0:T(2,128)} %cap_index_ref.5) | copy-start | bytes 388
  0.7 19.9 %copy-start.5 = (f32[2,16,128]{2,1,0:T(8,128)S(1)}, f32[2,16,128]{2,1,0:T(8,128)}, u32[]{:S(2)}) copy-start(f32[2,16,128]{2,1,0:T(8,128)} %param.13) | copy-start | bytes 49156
  3.0 17.5 %all-to-all-start = ((f32[32,16,128]{2,1,0:T(8,128)}), f32[32,16,128]{2,1,0:T(8,128)S(1)}, u32[]{:S(2)}, u32[]{:S(2)}) async-start(f32[32,16,128]{2,1,0:T(8,128)} %get-tuple-element.49), calls=%async_computation | async-start | bytes 524288 | tf_op jit(solution)/shard_map/all_to_all | solution.py:396
  11.6 1.2 copy-start.1
  12.8 0.7 copy-start.7
  14.0 0.7 copy-start.3
  20.5 31.5 %copy-start = (f32[2,8,128,128]{3,2,1,0:T(8,128)S(1)}, f32[2,8,128,128]{3,2,1,0:T(8,128)}, u32[]{:S(2)}) copy-start(f32[2,8,128,128]{3,2,1,0:T(8,128)} %param.16) | copy-start | bytes 3145732
  25.9 14.0 %collective-permute-start = (f32[24,128]{1,0:T(8,128)S(1)}, f32[24,128]{1,0:T(8,128)S(1)}, u32[]{:S(2)}, u32[]{:S(2)}) collective-permute-start(f32[24,128]{1,0:T(8,128)S(1)} %get-tuple-element.52.note_ref), channel_id=1, source_target_pairs={{0,128},{32,160},{64,192},{96,224},{128,0},{160,32},{192,64},{224,... | collective-permute-start | bytes 36872 | tf_op jit(solution)/shard_map/ppermute | solution.py:399
  32.9 28.9 %copy-start.2 = (f32[16,128,128]{2,1,0:T(8,128)S(1)}, f32[16,128,128]{2,1,0:T(8,128)}, u32[]{:S(2)}) copy-start(f32[16,128,128]{2,1,0:T(8,128)} %cap_precond_ref.5) | copy-start | bytes 3145732
  32.9 28.9 %copy-start.8 = (f32[16,128]{1,0:T(8,128)S(1)}, f32[16,128]{1,0:T(8,128)}, u32[]{:S(2)}) copy-start(f32[16,128]{1,0:T(8,128)} %cap_rhs_ref.5) | copy-start | bytes 24580
  39.9 12.1 %all-to-all-start.1 = ((f32[32,4,128]{2,1,0:T(4,128)}), f32[32,4,128]{2,1,0:T(4,128)S(1)}, u32[]{:S(2)}, u32[]{:S(2)}) async-start(f32[32,4,128]{2,1,0:T(4,128)} %get-tuple-element.54), calls=%async_computation.1 | async-start | bytes 131072 | tf_op jit(solution)/shard_map/all_to_all | solution.py:396
  44.7 2.8 %collective-permute-start.1 = (f32[24,128]{1,0:T(8,128)S(1)}, f32[24,128]{1,0:T(8,128)S(1)}, u32[]{:S(2)}, u32[]{:S(2)}) collective-permute-start(f32[24,128]{1,0:T(8,128)S(1)} %get-tuple-element.55.note_ref), channel_id=1, source_target_pairs={{0,32},{32,0},{64,96},{96,64},{128,160},{160,128},{192,224},{224,1... | collective-permute-start | bytes 36872 | tf_op jit(solution)/shard_map/ppermute | solution.py:399
  53.7 11.2 %all-to-all-start.2 = ((f32[32,2,128]{2,1,0:T(2,128)}), f32[32,2,128]{2,1,0:T(2,128)S(1)}, u32[]{:S(2)}, u32[]{:S(2)}) async-start(f32[32,2,128]{2,1,0:T(2,128)} %get-tuple-element.58), calls=%async_computation.2 | async-start | bytes 65536 | tf_op jit(solution)/shard_map/all_to_all | solution.py:396
  57.5 4.2 %collective-permute-start.2 = (f32[24,128]{1,0:T(8,128)S(1)}, f32[24,128]{1,0:T(8,128)S(1)}, u32[]{:S(2)}, u32[]{:S(2)}) collective-permute-start(f32[24,128]{1,0:T(8,128)S(1)} %get-tuple-element.59.half_ref), channel_id=1, source_target_pairs={{0,64},{32,96},{64,0},{96,32},{128,192},{160,224},{192,128},{224,1... | collective-permute-start | bytes 36872 | tf_op jit(solution)/shard_map/ppermute | solution.py:399
  70.2 7.4 %collective-permute-start.3 = (f32[24,128]{1,0:T(8,128)S(1)}, f32[24,128]{1,0:T(8,128)S(1)}, u32[]{:S(2)}, u32[]{:S(2)}) collective-permute-start(f32[24,128]{1,0:T(8,128)S(1)} %get-tuple-element.64.note_ref), channel_id=1, source_target_pairs={{0,128},{32,160},{64,192},{96,224},{128,0},{160,32},{192,64},{224,... | collective-permute-start | bytes 36872 | tf_op jit(solution)/shard_map/ppermute | solution.py:399
  77.6 13.0 %all-to-all-start.3 = ((f32[32,4,128]{2,1,0:T(4,128)}), f32[32,4,128]{2,1,0:T(4,128)S(1)}, u32[]{:S(2)}, u32[]{:S(2)}) async-start(f32[32,4,128]{2,1,0:T(4,128)} %get-tuple-element.66), calls=%async_computation.3 | async-start | bytes 131072 | tf_op jit(solution)/shard_map/all_to_all | solution.py:396
  83.2 2.8 %collective-permute-start.4 = (f32[24,128]{1,0:T(8,128)S(1)}, f32[24,128]{1,0:T(8,128)S(1)}, u32[]{:S(2)}, u32[]{:S(2)}) collective-permute-start(f32[24,128]{1,0:T(8,128)S(1)} %get-tuple-element.67.note_ref), channel_id=1, source_target_pairs={{0,32},{32,0},{64,96},{96,64},{128,160},{160,128},{192,224},{224,1... | collective-permute-start | bytes 36872 | tf_op jit(solution)/shard_map/ppermute | solution.py:399
  91.7 11.3 %all-to-all-start.4 = ((f32[32,2,128]{2,1,0:T(2,128)}), f32[32,2,128]{2,1,0:T(2,128)S(1)}, u32[]{:S(2)}, u32[]{:S(2)}) async-start(f32[32,2,128]{2,1,0:T(2,128)} %get-tuple-element.74), calls=%async_computation.4 | async-start | bytes 65536 | tf_op jit(solution)/shard_map/all_to_all | solution.py:396
  95.8 4.2 %collective-permute-start.5 = (f32[24,128]{1,0:T(8,128)S(1)}, f32[24,128]{1,0:T(8,128)S(1)}, u32[]{:S(2)}, u32[]{:S(2)}) collective-permute-start(f32[24,128]{1,0:T(8,128)S(1)} %get-tuple-element.76.half_ref), channel_id=1, source_target_pairs={{0,64},{32,96},{64,0},{96,32},{128,192},{160,224},{192,128},{224,1... | collective-permute-start | bytes 36872 | tf_op jit(solution)/shard_map/ppermute | solution.py:399
  109.1 13.8 %all-to-all-start.5 = ((f32[8,24,128]{2,1,0:T(8,128)}), f32[8,24,128]{2,1,0:T(8,128)S(1)}, u32[]{:S(2)}, u32[]{:S(2)}) async-start(f32[8,24,128]{2,1,0:T(8,128)} %get-tuple-element.81), calls=%async_computation.5 | async-start | bytes 196608 | tf_op jit(solution)/shard_map/all_to_all | solution.py:473

commit v4 on v3

--- a/solution.py
+++ b/solution.py
@@ -33,7 +33,7 @@
         out_specs=[ANY if n in still else VMEM for n in range(len(outs))],
         scratch_shapes=list(scratch),
         input_output_aliases=aliases or {},
-        compiler_params=pltpu.CompilerParams(vmem_limit_bytes=32 * 1024 * 1024),
+        compiler_params=pltpu.CompilerParams(vmem_limit_bytes=12 * 1024 * 1024),
         cost_estimate=pl.CostEstimate(flops=flops, bytes_accessed=4 * 1024 * 1024, transcendentals=0),
     )(*args)
 
@@ -148,13 +148,12 @@
     return jnp.where(lane == n, jnp.sum(block * row, axis=1, keepdims=True), total)
 
 
-def arcs_up(comms, blocks, index_ref, cap_index_ref, up_ref, got_ref, q_ref, scale_ref, tiles_hbm, cap_tiles_hbm,
-            scaled_ref, note_ref, far_ref, third_ref, cap_tiles_ref, wide_ref, turn_ref, sems):
+def arcs_up(comms, blocks, index_ref, cap_index_ref, up_ref, got_ref, q_ref, scale_ref, tiles_hbm, cap_tiles_ref,
+            scaled_ref, note_ref, far_ref, third_ref, wide_ref, turn_ref, sems, caps_in=None):
     count = up_ref.shape[0]
     arcs = count // comms
     width = scale_ref.shape[1]
     thirds = fetch(tiles_hbm.at[:, 2], third_ref, sems, 0, PARTS)
-    caps_in = fetch(cap_tiles_hbm, cap_tiles_ref, sems, PARTS, PARTS)
 
     def place(i, _):
         c, j = lax.div(i, arcs), lax.rem(i, arcs)
@@ -170,7 +169,8 @@
     for i in range(count):
         if i % step == 0:
             thirds[i // step].wait()
-            caps_in[i // step].wait()
+            if caps_in:
+                caps_in[i // step].wait()
         column = jnp.broadcast_to(ft[:, i : i + 1], third_ref.shape[1:])
         total = third_ref[i] * column + cap_tiles_ref[i] * wide_ref[cap_index_ref[i // arcs, i % arcs]]
         far_ref[i : i + 1] = up_ref[i : i + 1] + fold(total)
@@ -179,10 +179,10 @@
     scaled_ref[...] = scaled
     lane = lax.broadcasted_iota(jnp.int32, (width, width), 1)
 
-    def one(i, total):
-        return beside(cap_tiles_ref[i], scaled_ref[pl.ds(i, 1)], lane, i, total)
-
-    turn_ref[...] = lax.fori_loop(0, count, one, jnp.zeros((width, width), F32), unroll=2).T
+    total = jnp.zeros((width, width), F32)
+    for i in range(count):
+        total = beside(cap_tiles_ref[i], scaled[i : i + 1], lane, i, total)
+    turn_ref[...] = total.T
     note_ref[...] = jnp.zeros_like(note_ref)
 
     def put(i, _):
@@ -195,24 +195,26 @@
 
 
 def up_first_kernel(comms, blocks, caps, index_ref, cap_index_ref, up_ref, got_ref, q_ref, scale_ref, rhs_ref, v_ref,
-                    tiles_hbm, cap_tiles_hbm, scaled_ref, note_ref, *room):
+                    tiles_hbm, cap_tiles_hbm, scaled_ref, note_ref, cap_tiles_ref, *room):
+    caps_in = fetch(cap_tiles_hbm, cap_tiles_ref, room[-1], PARTS, PARTS)
     energy = arcs_up(comms, blocks, index_ref, cap_index_ref, up_ref, got_ref, q_ref, scale_ref, tiles_hbm,
-                     cap_tiles_hbm, scaled_ref, note_ref, *room)
+                     cap_tiles_ref, scaled_ref, note_ref, *room, caps_in)
     v = v_ref[...]
     note_ref[caps : caps + 1] = fold(rhs_ref[...] * v)
     note_ref[caps + 1 : caps + 2] = fold(v * v) + energy
 
 
 def up_second_kernel(comms, blocks, index_ref, cap_index_ref, up_ref, got_ref, q_ref, scale_ref, tiles_hbm,
-                     cap_tiles_hbm, scaled_ref, note_ref, *room):
+                     cap_tiles_hbm, scaled_ref, note_ref, cap_tiles_ref, *room):
+    caps_in = fetch(cap_tiles_hbm, cap_tiles_ref, room[-1], PARTS, PARTS)
     arcs_up(comms, blocks, index_ref, cap_index_ref, up_ref, got_ref, q_ref, scale_ref, tiles_hbm,
-            cap_tiles_hbm, scaled_ref, note_ref, *room)
+            cap_tiles_ref, scaled_ref, note_ref, *room, caps_in)
 
 
 def up_third_kernel(comms, blocks, caps, index_ref, cap_index_ref, up_ref, got_ref, q_ref, scale_ref, z_ref, yz_ref,
-                    r_ref, y0_ref, v_ref, tiles_hbm, cap_tiles_hbm, scaled_ref, notes_ref, note_ref, *room):
+                    r_ref, y0_ref, v_ref, tiles_hbm, cap_tiles_ref, scaled_ref, notes_ref, note_ref, *room):
     energy = arcs_up(comms, blocks, index_ref, cap_index_ref, up_ref, got_ref, q_ref, scale_ref, tiles_hbm,
-                     cap_tiles_hbm, scaled_ref, note_ref, *room)
+                     cap_tiles_ref, scaled_ref, note_ref, *room)
     z, yz, r, y0, v = z_ref[...], yz_ref[...], r_ref[...], y0_ref[...], v_ref[...]
     pairs = ((z, y0), (z, yz), (v, y0), (v, yz), (v, v), (z, r), (v, r))
     for n, (one, other) in enumerate(pairs):
@@ -221,29 +223,19 @@
     notes_ref[...] = jnp.broadcast_to(note_ref[...][None], notes_ref.shape)
 
 
-def down_kernel(comms, blocks, step_number, index_ref, scaled_ref, sums_ref, tiles_hbm, local_ref, back_ref,
-                tiles_ref, turn_ref, sems):
+def down_kernel(comms, blocks, step_number, index_ref, scaled_ref, sums_ref, tiles_ref, local_ref, back_ref, turn_ref):
     count, touched = tiles_ref.shape[:2]
     width = tiles_ref.shape[3]
     arcs = count // comms
-    parts = 2 * PARTS
-    step = count // parts
-    copies = fetch(tiles_hbm, tiles_ref, sems, 0, parts)
     local_ref[...] = jnp.zeros_like(local_ref)
     if step_number == 0:
         back_ref[...] = jnp.full(back_ref.shape, -1.0, F32)
     lane = lax.broadcasted_iota(jnp.int32, (width, width), 1)
     total = jnp.zeros((width, width), F32)
-    for n in range(parts):
-        copies[n].wait()
-
-        def one(i, total):
-            row = scaled_ref[pl.ds(i, 1)]
-            for k in range(touched):
-                total = beside(tiles_ref[i, k], row, lane, k * count + i, total)
-            return total
-
-        total = lax.fori_loop(n * step, (n + 1) * step, one, total)
+    for i in range(count):
+        row = scaled_ref[i : i + 1]
+        for k in range(touched):
+            total = beside(tiles_ref[i, k], row, lane, k * count + i, total)
     turn_ref[...] = total.T
 
     def put(i, _):
@@ -406,14 +398,14 @@
         return up
 
     up_room = [
-        room(*arc_shape), room(count, *flat), room(count, *flat), room(caps, *flat), room(*flat), sems(2 * PARTS),
+        room(*arc_shape), room(count, *flat), room(caps, *flat), room(*flat), sems(2 * PARTS),
     ]
+    both_room = [room(count, *flat), *up_room]
 
     def spread(step_number, scaled, sums):
         return call(
             functools.partial(down_kernel, comms, blocks, step_number), [row_shape, back_shape],
-            (index, scaled, sums, tiles), 1,
-            [room(count, touched, *flat), room(*flat), sems(2 * PARTS)], flops=3 * unit, hbm=(3,),
+            (index, scaled, sums, kept(tiles)), 1, [room(*flat)], flops=3 * unit,
         )
 
     def add(note, other, back):
@@ -428,7 +420,7 @@
     (q0,) = call(cap_first_kernel, [cap_shape], (cap_rhs, kept(cap_precond)), flops=unit)
     scaled, note = call(
         functools.partial(up_first_kernel, comms, blocks, caps), [arc_shape, note_shape],
-        (index, cap_index, up, got, q0, scale, rhs, v0, tiles, cap_tiles), 2, up_room, flops=3 * unit, hbm=(8, 9),
+        (index, cap_index, up, got, q0, scale, rhs, v0, tiles, cap_tiles), 2, both_room, flops=3 * unit, hbm=(8, 9),
     )
     other = across(note, 4)
     local, back = spread(0, scaled, rhs)
@@ -447,7 +439,7 @@
     )
     scaled, note = call(
         functools.partial(up_second_kernel, comms, blocks), [arc_shape, note_shape],
-        (index, cap_index, up, got, q1, scale, tiles, cap_tiles), 2, up_room, flops=3 * unit, hbm=(6, 7),
+        (index, cap_index, up, got, q1, scale, tiles, cap_tiles), 2, both_room, flops=3 * unit, hbm=(6, 7),
     )
     other = across(note, 4)
     local, back = spread(1, scaled, sums)
@@ -467,8 +459,8 @@
     )
     scaled, notes = call(
         functools.partial(up_third_kernel, comms, blocks, caps), [arc_shape, (peers, *note_shape)],
-        (index, cap_index, up, got, q2, scale, z1, yz, r1, y0, v2, tiles, cap_tiles), 2,
-        [room(*note_shape), *up_room], flops=3 * unit, hbm=(11, 12),
+        (index, cap_index, up, got, q2, scale, z1, yz, r1, y0, v2, tiles, kept(cap_tiles)), 2,
+        [room(*note_shape), *up_room], flops=3 * unit, hbm=(11,),
     )
     notes = lax.all_to_all(notes, "comm", 0, 0)
     local, back = spread(2, scaled, sums)

time: 138 us -> 132 us (0.957)
  Pallas kernels: 53.2 us -> 38.7 us
  local copies, waits for them, and re-layouts: 2.63 us -> 6.65 us
  starting transfers between devices: 45.7 us -> 48.9 us
    pallas_call x19, Pallas kernels: 53.2 us -> 38.7 us  [call(): pl.pallas_call(kernel, out_shape=outs, in_specs=[HBM if n in hbm else ANY...]
    unnamed x20 -> x34, local copies, waits for them, and re-layouts: 2.63 us -> 6.65 us
    ppermute x6, starting transfers between devices: 12.4 us -> 15.4 us  [across(): return lax.ppermute(x, 'comm', [(i, i ^ step) for i in range(peers)])]
    all_to_all x5, starting transfers between devices: 26.9 us -> 28.5 us  [exchange(): return lax.all_to_all(x, GROUP, 0, 0)]
  transfers between devices with their start and end apart: 12 -> 12, of which waited for: 8 -> 8; matrix products, arithmetic and copies ran while one was open for 0% -> 0% of each run, Pallas kernels for 22% -> 15%
where the time goes in v4:
time: 132 us; the launch traced here: 131 us
  starting transfers between devices  48.9 us (37%)
  Pallas kernels  38.7 us (29%)
  waiting for transfers between devices  21.5 us (16%)
  blocking collectives  14 us (11%)
  local copies, waits for them, and re-layouts  6.65 us (5%)
    pallas_call x19, Pallas kernels, call(): pl.pallas_call(kernel, out_shape=outs, in_specs=[HBM if n in hbm else ANY...  38.7 us
    all_to_all x5, starting transfers between devices, exchange(): return lax.all_to_all(x, GROUP, 0, 0)  28.5 us
    all_to_all x5, waiting for transfers between devices, exchange(): return lax.all_to_all(x, GROUP, 0, 0)  15.7 us
    ppermute x6, starting transfers between devices, across(): return lax.ppermute(x, 'comm', [(i, i ^ step) for i in range(peers)])  15.4 us
    all_to_all x1, blocking collectives, exchange(): return lax.all_to_all(x, GROUP, 0, 0)  14 us
    unnamed x34, local copies, waits for them, and re-layouts  6.65 us
    all_to_all x1, starting transfers between devices, body(): notes = lax.all_to_all(notes, 'comm', 0, 0)  5.03 us
    ppermute x6, waiting for transfers between devices, across(): return lax.ppermute(x, 'comm', [(i, i ^ step) for i in range(peers)])  3.94 us
  transfers between devices with their start and end apart: 12, of which 8 were waited for; matrix products, arithmetic and copies ran while one was open for 0% of the time, Pallas kernels for 15%

profile of v4, /device:TPU:1, one launch (start us, length us, event | category | flops | bytes accessed | tf_op | source)
XLA Modules:
  0.0 130.7 jit_solution(15603775716857484718)
XLA Ops:
  0.7 2.3 %shard_map.120 = (f32[16,128]{1,0:T(8,128)S(1)}, f32[32,16,128]{2,1,0:T(8,128)}) custom-call(f32[16,128]{1,0:T(8,128)} %bitcast.39, f32[16,128,128]{2,1,0:T(8,128)} %bitcast.24), custom_call_target="tpu_custom_call" | custom-call | bytes 4194304 | tf_op jit(solution)/shard_map/pallas_call | solution.py:27
  3.0 8.6 %all-to-all-start = ((f32[32,16,128]{2,1,0:T(8,128)}), f32[32,16,128]{2,1,0:T(8,128)S(1)}, u32[]{:S(2)}, u32[]{:S(2)}) async-start(f32[32,16,128]{2,1,0:T(8,128)} %get-tuple-element.49), calls=%async_computation | async-start | bytes 524288 | tf_op jit(solution)/shard_map/all_to_all | solution.py:388
  11.6 1.2 copy-done.3
  14.7 3.0 %shard_map.121.up_ref = f32[32,128]{1,0:T(8,128)S(1)} custom-call(s32[3,2,16]{2,1,0:T(2,128)S(1)} %bitcast.27, f32[16,128]{1,0:T(8,128)S(1)} %get-tuple-element.48.v_ref.v0_ref, f32[32,3,128,128]{3,2,1,0:T(8,128)} %bitcast.8), custom_call_target="tpu_custom_call" | custom-call | flops 2097152 | bytes 4194304 | tf_op jit(solution)/shard_map/pallas_call | solution.py:27
  17.7 2.8 %all-to-all-done.got_ref = f32[32,16,128]{2,1,0:T(8,128)S(1)} async-done(((f32[32,16,128]{2,1,0:T(8,128)}), f32[32,16,128]{2,1,0:T(8,128)S(1)}, u32[]{:S(2)}, u32[]{:S(2)}) %all-to-all-start) | async-done | bytes 262176 | tf_op jit(solution)/shard_map/all_to_all | solution.py:388
  20.6 4.4 %shard_map.123 = (f32[32,128]{1,0:T(8,128)S(1)}, f32[24,128]{1,0:T(8,128)S(1)}) custom-call(s32[3,2,16]{2,1,0:T(2,128)S(1)} %bitcast.28, s32[2,16]{1,0:T(2,128)S(1)} %copy-done.12, f32[32,128]{1,0:T(8,128)S(1)} %shard_map.121.up_ref, f32[32,16,128]{2,1,0:T(8,128)S(1)} %all-to-all-done.got_ref, f32[16,128]{1,0:T(8,128)S(1)} %shard_map.122.q_ref.q0_ref, ...), custom_call_target="tpu_custom_call" | custom-call | flops 3145728 | bytes 4194304 | tf_op jit(solution)/shard_map/pallas_call | solution.py:27
  24.9 7.0 %collective-permute-start = (f32[24,128]{1,0:T(8,128)S(1)}, f32[24,128]{1,0:T(8,128)S(1)}, u32[]{:S(2)}, u32[]{:S(2)}) collective-permute-start(f32[24,128]{1,0:T(8,128)S(1)} %get-tuple-element.52.note_ref), channel_id=1, source_target_pairs={{0,128},{32,160},{64,192},{96,224},{128,0},{160,32},{192,64},{224,... | collective-permute-start | bytes 36872 | tf_op jit(solution)/shard_map/ppermute | solution.py:391
  32.0 3.4 %shard_map.124 = (f32[16,128]{1,0:T(8,128)S(1)}, f32[32,4,128]{2,1,0:T(4,128)}) custom-call(s32[3,2,16]{2,1,0:T(2,128)S(1)} %bitcast.29, f32[32,128]{1,0:T(8,128)S(1)} %get-tuple-element.50.scaled_ref, f32[16,128]{1,0:T(8,128)S(1)} %bitcast.41, f32[32,3,128,128]{3,2,1,0:T(8,128)S(1)} %bitcast.16), custom_call_target="tpu_custom_call" | custom-call | flops 3145728 | bytes 4194304 | tf_op jit(solution)/shard_map/pallas_call | solution.py:27
  35.4 4.9 %all-to-all-start.1 = ((f32[32,4,128]{2,1,0:T(4,128)}), f32[32,4,128]{2,1,0:T(4,128)S(1)}, u32[]{:S(2)}, u32[]{:S(2)}) async-start(f32[32,4,128]{2,1,0:T(4,128)} %get-tuple-element.54), calls=%async_computation.1 | async-start | bytes 131072 | tf_op jit(solution)/shard_map/all_to_all | solution.py:388
  41.1 2.0 %collective-permute-done.1.came_ref = f32[24,128]{1,0:T(8,128)S(1)} collective-permute-done((f32[24,128]{1,0:T(8,128)S(1)}, f32[24,128]{1,0:T(8,128)S(1)}, u32[]{:S(2)}, u32[]{:S(2)}) %collective-permute-start.1) | collective-permute-done | bytes 12320 | tf_op jit(solution)/shard_map/ppermute | solution.py:391
  43.0 4.5 %all-to-all-done.1.back_ref = f32[32,4,128]{2,1,0:T(4,128)S(1)} async-done(((f32[32,4,128]{2,1,0:T(4,128)}), f32[32,4,128]{2,1,0:T(4,128)S(1)}, u32[]{:S(2)}, u32[]{:S(2)}) %all-to-all-start.1) | async-done | bytes 65568 | tf_op jit(solution)/shard_map/all_to_all | solution.py:388
  47.6 1.6 %shard_map.126 = (f32[24,128]{1,0:T(8,128)S(1)}, f32[16,128]{1,0:T(8,128)S(1)}, f32[16,128]{1,0:T(8,128)S(1)}, f32[32,2,128]{2,1,0:T(2,128)}, f32[2,32,128]{2,1,0:T(8,128)S(1)}) custom-call(f32[16,128]{1,0:T(8,128)S(1)} %get-tuple-element.48.v_ref.v0_ref, f32[16,128]{1,0:T(8,128)S(1)} %get-tuple-element.51.local_ref, ...), custom_call_target="tpu_custom_call" | custom-call | bytes 4194304 | tf_op jit(solution)/shard_map/pallas_call | solution.py:27
  49.2 3.9 %all-to-all-start.2 = ((f32[32,2,128]{2,1,0:T(2,128)}), f32[32,2,128]{2,1,0:T(2,128)S(1)}, u32[]{:S(2)}, u32[]{:S(2)}) async-start(f32[32,2,128]{2,1,0:T(2,128)} %get-tuple-element.58), calls=%async_computation.2 | async-start | bytes 65536 | tf_op jit(solution)/shard_map/all_to_all | solution.py:388
  53.1 1.5 %collective-permute-start.2 = (f32[24,128]{1,0:T(8,128)S(1)}, f32[24,128]{1,0:T(8,128)S(1)}, u32[]{:S(2)}, u32[]{:S(2)}) collective-permute-start(f32[24,128]{1,0:T(8,128)S(1)} %get-tuple-element.59.half_ref), channel_id=1, source_target_pairs={{0,64},{32,96},{64,0},{96,32},{128,192},{160,224},{192,128},{224,1... | collective-permute-start | bytes 36872 | tf_op jit(solution)/shard_map/ppermute | solution.py:391
  54.5 3.0 %shard_map.127.up_ref = f32[32,128]{1,0:T(8,128)S(1)} custom-call(s32[3,2,16]{2,1,0:T(2,128)S(1)} %bitcast.30, f32[16,128]{1,0:T(8,128)S(1)} %get-tuple-element.57.v_ref.v1_ref, f32[32,3,128,128]{3,2,1,0:T(8,128)} %bitcast.10), custom_call_target="tpu_custom_call" | custom-call | flops 2097152 | bytes 4194304 | tf_op jit(solution)/shard_map/pallas_call | solution.py:27
  57.5 1.2 copy-done.4
  60.4 4.3 %shard_map.129 = (f32[32,128]{1,0:T(8,128)S(1)}, f32[24,128]{1,0:T(8,128)S(1)}) custom-call(s32[3,2,16]{2,1,0:T(2,128)S(1)} %bitcast.31, s32[2,16]{1,0:T(2,128)S(1)} %copy-done.12, f32[32,128]{1,0:T(8,128)S(1)} %shard_map.127.up_ref, f32[32,2,128]{2,1,0:T(2,128)S(1)} %all-to-all-done.2.got_ref, f32[16,128]{1,0:T(8,128)S(1)} %get-tuple-element.60.q_ref.q1_ref, ...), custom_call_target="tpu_custom_call" | custom-call | flops 3145728 | bytes 4194304 | tf_op jit(solution)/shard_map/pallas_call | solution.py:27
  64.8 4.0 %collective-permute-start.3 = (f32[24,128]{1,0:T(8,128)S(1)}, f32[24,128]{1,0:T(8,128)S(1)}, u32[]{:S(2)}, u32[]{:S(2)}) collective-permute-start(f32[24,128]{1,0:T(8,128)S(1)} %get-tuple-element.64.note_ref), channel_id=1, source_target_pairs={{0,128},{32,160},{64,192},{96,224},{128,0},{160,32},{192,64},{224,... | collective-permute-start | bytes 36872 | tf_op jit(solution)/shard_map/ppermute | solution.py:391
  68.7 3.4 %shard_map.130 = (f32[16,128]{1,0:T(8,128)S(1)}, f32[32,4,128]{2,1,0:T(4,128)}) custom-call(s32[3,2,16]{2,1,0:T(2,128)S(1)} %bitcast.32, f32[32,128]{1,0:T(8,128)S(1)} %get-tuple-element.61.scaled_ref, f32[8,128]{1,0:T(8,128)S(1)} %get-tuple-element.62.sums_ref, f32[32,3,128,128]{3,2,1,0:T(8,128)S(1)} %bitcast.19), custom_call_target="tpu_custom_call" | custom-call | flops 3145728 | bytes 4194304 | tf_op jit(solution)/shard_map/pallas_call | solution.py:27
  72.2 7.2 %all-to-all-start.3 = ((f32[32,4,128]{2,1,0:T(4,128)}), f32[32,4,128]{2,1,0:T(4,128)S(1)}, u32[]{:S(2)}, u32[]{:S(2)}) async-start(f32[32,4,128]{2,1,0:T(4,128)} %get-tuple-element.66), calls=%async_computation.3 | async-start | bytes 131072 | tf_op jit(solution)/shard_map/all_to_all | solution.py:388
  80.2 2.0 %collective-permute-done.4.came_ref = f32[24,128]{1,0:T(8,128)S(1)} collective-permute-done((f32[24,128]{1,0:T(8,128)S(1)}, f32[24,128]{1,0:T(8,128)S(1)}, u32[]{:S(2)}, u32[]{:S(2)}) %collective-permute-start.4) | collective-permute-done | bytes 12320 | tf_op jit(solution)/shard_map/ppermute | solution.py:391
  82.1 4.5 %all-to-all-done.3.back_ref = f32[32,4,128]{2,1,0:T(4,128)S(1)} async-done(((f32[32,4,128]{2,1,0:T(4,128)}), f32[32,4,128]{2,1,0:T(4,128)S(1)}, u32[]{:S(2)}, u32[]{:S(2)}) %all-to-all-start.3) | async-done | bytes 65568 | tf_op jit(solution)/shard_map/all_to_all | solution.py:388
  87.9 4.0 %all-to-all-start.4 = ((f32[32,2,128]{2,1,0:T(2,128)}), f32[32,2,128]{2,1,0:T(2,128)S(1)}, u32[]{:S(2)}, u32[]{:S(2)}) async-start(f32[32,2,128]{2,1,0:T(2,128)} %get-tuple-element.74), calls=%async_computation.4 | async-start | bytes 65536 | tf_op jit(solution)/shard_map/all_to_all | solution.py:388
  91.9 1.3 collective-permute-start.5
  93.2 2.9 %shard_map.133.up_ref = f32[32,128]{1,0:T(8,128)S(1)} custom-call(s32[3,2,16]{2,1,0:T(2,128)S(1)} %bitcast.33, f32[16,128]{1,0:T(8,128)S(1)} %get-tuple-element.73.v_ref.v2_ref, f32[32,3,128,128]{3,2,1,0:T(8,128)} %bitcast.12), custom_call_target="tpu_custom_call" | custom-call | flops 2097152 | bytes 4194304 | tf_op jit(solution)/shard_map/pallas_call | solution.py:27
  96.6 2.6 %all-to-all-done.4.got_ref = f32[32,2,128]{2,1,0:T(2,128)S(1)} async-done(((f32[32,2,128]{2,1,0:T(2,128)}), f32[32,2,128]{2,1,0:T(2,128)S(1)}, u32[]{:S(2)}, u32[]{:S(2)}) %all-to-all-start.4) | async-done | bytes 32800 | tf_op jit(solution)/shard_map/all_to_all | solution.py:388
  99.2 4.1 %shard_map.135 = (f32[32,128]{1,0:T(8,128)S(1)}, f32[8,24,128]{2,1,0:T(8,128)}) custom-call(s32[3,2,16]{2,1,0:T(2,128)S(1)} %bitcast.34, s32[2,16]{1,0:T(2,128)S(1)} %copy-done.12, f32[32,128]{1,0:T(8,128)S(1)} %shard_map.133.up_ref, f32[32,2,128]{2,1,0:T(2,128)S(1)} %all-to-all-done.4.got_ref, f32[16,128]{1,0:T(8,128)S(1)} %get-tuple-element.77.q_ref.q2_ref, ...), custom_call_target="tpu_custom_call" | custom-call | flops 3145728 | bytes 4194304 | tf_op jit(solution)/shard_map/pallas_call | solution.py:27
  103.4 5.0 %all-to-all-start.5 = ((f32[8,24,128]{2,1,0:T(8,128)}), f32[8,24,128]{2,1,0:T(8,128)S(1)}, u32[]{:S(2)}, u32[]{:S(2)}) async-start(f32[8,24,128]{2,1,0:T(8,128)} %get-tuple-element.81), calls=%async_computation.5 | async-start | bytes 196608 | tf_op jit(solution)/shard_map/all_to_all | solution.py:465
  108.4 2.8 %copy-done = f32[2,16,3,128,128]{4,3,2,1,0:T(8,128)S(1)} copy-done((f32[2,16,3,128,128]{4,3,2,1,0:T(8,128)S(1)}, f32[2,16,3,128,128]{4,3,2,1,0:T(8,128)}, u32[]{:S(2)}) %copy-start) | copy-done | bytes 6291480
  111.2 2.8 %shard_map.136 = (f32[16,128]{1,0:T(8,128)S(1)}, f32[32,4,128]{2,1,0:T(4,128)S(1)}) custom-call(s32[3,2,16]{2,1,0:T(2,128)S(1)} %bitcast.35, f32[32,128]{1,0:T(8,128)S(1)} %get-tuple-element.78.scaled_ref, f32[8,128]{1,0:T(8,128)S(1)} %get-tuple-element.79.sums_ref, f32[32,3,128,128]{3,2,1,0:T(8,128)S(1)} %bitcast.20), custom_call_target="tpu_custom_call" | custom-call | flops 3145728 | bytes 4194304 | tf_op jit(solution)/shard_map/pallas_call | solution.py:27
  114.0 1.9 %all-to-all-done.5.notes_ref = f32[8,24,128]{2,1,0:T(8,128)S(1)} async-done(((f32[8,24,128]{2,1,0:T(8,128)}), f32[8,24,128]{2,1,0:T(8,128)S(1)}, u32[]{:S(2)}, u32[]{:S(2)}) %all-to-all-start.5) | async-done | bytes 98336 | tf_op jit(solution)/shard_map/all_to_all | solution.py:465
  116.0 14.0 %all_to_all.35.back_ref = f32[32,4,128]{2,1,0:T(4,128)S(1)} all-to-all(f32[32,4,128]{2,1,0:T(4,128)S(1)} %get-tuple-element.83), channel_id=1, replica_groups=mesh['comm'=8,'stn'=16,'tm'=2] {'stn','tm'}, dimensions={0} | all-to-all | bytes 131072 | tf_op jit(solution)/shard_map/all_to_all | solution.py:388
  (48 shorter events, 7.8 us)
Async XLA Ops:
  0.6 19.9 %copy-start.9 = (f32[2,8,128]{2,1,0:T(8,128)S(1)}, f32[2,8,128]{2,1,0:T(8,128)}, u32[]{:S(2)}) copy-start(f32[2,8,128]{2,1,0:T(8,128)} %param.14) | copy-start | bytes 24580
  0.6 19.9 %copy-start.7 = (s32[2,16,3]{1,0,2:T(2,128)S(1)}, s32[2,16,3]{1,0,2:T(2,128)}, u32[]{:S(2)}) copy-start(s32[2,16,3]{1,0,2:T(2,128)} %param.11) | copy-start | bytes 1156
  0.7 19.9 %copy-start.12 = (s32[2,16]{1,0:T(2,128)S(1)}, s32[2,16]{1,0:T(2,128)}, u32[]{:S(2)}) copy-start(s32[2,16]{1,0:T(2,128)} %cap_index_ref.5) | copy-start | bytes 388
  0.7 19.9 %copy-start.8 = (f32[2,16,128]{2,1,0:T(8,128)S(1)}, f32[2,16,128]{2,1,0:T(8,128)}, u32[]{:S(2)}) copy-start(f32[2,16,128]{2,1,0:T(8,128)} %param.13) | copy-start | bytes 49156
  3.0 17.5 %all-to-all-start = ((f32[32,16,128]{2,1,0:T(8,128)}), f32[32,16,128]{2,1,0:T(8,128)S(1)}, u32[]{:S(2)}, u32[]{:S(2)}) async-start(f32[32,16,128]{2,1,0:T(8,128)} %get-tuple-element.49), calls=%async_computation | async-start | bytes 524288 | tf_op jit(solution)/shard_map/all_to_all | solution.py:388
  11.6 1.2 copy-start.3
  12.9 0.7 copy-start.10
  14.0 0.7 copy-start.6
  14.7 17.2 %slice-start = ((s8[6291456]{0:T(1024)(128)(4,1)}), s8[2097152]{0:T(1024)(128)(4,1)S(1)}, s32[]{:S(2)}) async-start(s8[6291456]{0:T(1024)(128)(4,1)} %bitcast.14), calls=%async_computation.7 | async-start | bytes 4194304
  20.5 11.4 %slice-start.1 = ((s8[6291456]{0:T(1024)(128)(4,1)}), s8[4194304]{0:T(1024)(128)(4,1)S(1)}, s32[]{:S(2)}) async-start(s8[6291456]{0:T(1024)(128)(4,1)} %bitcast.14), calls=%async_computation.8 | async-start | bytes 8388608
  20.6 27.0 %copy-start.2 = (f32[2,8,128,128]{3,2,1,0:T(8,128)S(1)}, f32[2,8,128,128]{3,2,1,0:T(8,128)}, u32[]{:S(2)}) copy-start(f32[2,8,128,128]{3,2,1,0:T(8,128)} %param.16) | copy-start | bytes 3145732
  24.9 10.4 %collective-permute-start = (f32[24,128]{1,0:T(8,128)S(1)}, f32[24,128]{1,0:T(8,128)S(1)}, u32[]{:S(2)}, u32[]{:S(2)}) collective-permute-start(f32[24,128]{1,0:T(8,128)S(1)} %get-tuple-element.52.note_ref), channel_id=1, source_target_pairs={{0,128},{32,160},{64,192},{96,224},{128,0},{160,32},{192,64},{224,... | collective-permute-start | bytes 36872 | tf_op jit(solution)/shard_map/ppermute | solution.py:391
  31.9 25.5 %copy-start.11 = (f32[16,128]{1,0:T(8,128)S(1)}, f32[16,128]{1,0:T(8,128)}, u32[]{:S(2)}) copy-start(f32[16,128]{1,0:T(8,128)} %cap_rhs_ref.5) | copy-start | bytes 24580
  35.4 12.2 %all-to-all-start.1 = ((f32[32,4,128]{2,1,0:T(4,128)}), f32[32,4,128]{2,1,0:T(4,128)S(1)}, u32[]{:S(2)}, u32[]{:S(2)}) async-start(f32[32,4,128]{2,1,0:T(4,128)} %get-tuple-element.54), calls=%async_computation.1 | async-start | bytes 131072 | tf_op jit(solution)/shard_map/all_to_all | solution.py:388
  40.3 2.8 %collective-permute-start.1 = (f32[24,128]{1,0:T(8,128)S(1)}, f32[24,128]{1,0:T(8,128)S(1)}, u32[]{:S(2)}, u32[]{:S(2)}) collective-permute-start(f32[24,128]{1,0:T(8,128)S(1)} %get-tuple-element.55.note_ref), channel_id=1, source_target_pairs={{0,32},{32,0},{64,96},{96,64},{128,160},{160,128},{192,224},{224,1... | collective-permute-start | bytes 36872 | tf_op jit(solution)/shard_map/ppermute | solution.py:391
  49.2 11.3 %all-to-all-start.2 = ((f32[32,2,128]{2,1,0:T(2,128)}), f32[32,2,128]{2,1,0:T(2,128)S(1)}, u32[]{:S(2)}, u32[]{:S(2)}) async-start(f32[32,2,128]{2,1,0:T(2,128)} %get-tuple-element.58), calls=%async_computation.2 | async-start | bytes 65536 | tf_op jit(solution)/shard_map/all_to_all | solution.py:388
  53.1 4.4 %collective-permute-start.2 = (f32[24,128]{1,0:T(8,128)S(1)}, f32[24,128]{1,0:T(8,128)S(1)}, u32[]{:S(2)}, u32[]{:S(2)}) collective-permute-start(f32[24,128]{1,0:T(8,128)S(1)} %get-tuple-element.59.half_ref), channel_id=1, source_target_pairs={{0,64},{32,96},{64,0},{96,32},{128,192},{160,224},{192,128},{224,1... | collective-permute-start | bytes 36872 | tf_op jit(solution)/shard_map/ppermute | solution.py:391
  54.5 14.2 %slice-start.2 = ((s8[6291456]{0:T(1024)(128)(4,1)}), s8[2097152]{0:T(1024)(128)(4,1)S(1)}, s32[]{:S(2)}) async-start(s8[6291456]{0:T(1024)(128)(4,1)} %bitcast.17), calls=%async_computation.9 | async-start | bytes 4194304
  57.5 1.2 copy-start.4
  60.4 8.3 %slice-start.3 = ((s8[6291456]{0:T(1024)(128)(4,1)}), s8[4194304]{0:T(1024)(128)(4,1)S(1)}, s32[]{:S(2)}) async-start(s8[6291456]{0:T(1024)(128)(4,1)} %bitcast.17), calls=%async_computation.10 | async-start | bytes 8388608
  64.8 7.4 %collective-permute-start.3 = (f32[24,128]{1,0:T(8,128)S(1)}, f32[24,128]{1,0:T(8,128)S(1)}, u32[]{:S(2)}, u32[]{:S(2)}) collective-permute-start(f32[24,128]{1,0:T(8,128)S(1)} %get-tuple-element.64.note_ref), channel_id=1, source_target_pairs={{0,128},{32,160},{64,192},{96,224},{128,0},{160,32},{192,64},{224,... | collective-permute-start | bytes 36872 | tf_op jit(solution)/shard_map/ppermute | solution.py:391
  72.2 27.1 %copy-start.1 = (f32[2,16,128,128]{3,2,1,0:T(8,128)S(1)}, f32[2,16,128,128]{3,2,1,0:T(8,128)}, u32[]{:S(2)}) copy-start(f32[2,16,128,128]{3,2,1,0:T(8,128)} %param.10) | copy-start | bytes 6291460
  72.2 14.5 %all-to-all-start.3 = ((f32[32,4,128]{2,1,0:T(4,128)}), f32[32,4,128]{2,1,0:T(4,128)S(1)}, u32[]{:S(2)}, u32[]{:S(2)}) async-start(f32[32,4,128]{2,1,0:T(4,128)} %get-tuple-element.66), calls=%async_computation.3 | async-start | bytes 131072 | tf_op jit(solution)/shard_map/all_to_all | solution.py:388
  79.3 2.8 %collective-permute-start.4 = (f32[24,128]{1,0:T(8,128)S(1)}, f32[24,128]{1,0:T(8,128)S(1)}, u32[]{:S(2)}, u32[]{:S(2)}) collective-permute-start(f32[24,128]{1,0:T(8,128)S(1)} %get-tuple-element.67.note_ref), channel_id=1, source_target_pairs={{0,32},{32,0},{64,96},{96,64},{128,160},{160,128},{192,224},{224,1... | collective-permute-start | bytes 36872 | tf_op jit(solution)/shard_map/ppermute | solution.py:391
  87.9 8.2 %copy-start.5 = (f32[16,128,128]{2,1,0:T(8,128)S(1)}, f32[16,128,128]{2,1,0:T(8,128)}, u32[]{:S(2)}) copy-start(f32[16,128,128]{2,1,0:T(8,128)} %cap_precond_ref.5) | copy-start | bytes 3145732
  87.9 11.4 %all-to-all-start.4 = ((f32[32,2,128]{2,1,0:T(2,128)}), f32[32,2,128]{2,1,0:T(2,128)S(1)}, u32[]{:S(2)}, u32[]{:S(2)}) async-start(f32[32,2,128]{2,1,0:T(2,128)} %get-tuple-element.74), calls=%async_computation.4 | async-start | bytes 65536 | tf_op jit(solution)/shard_map/all_to_all | solution.py:388
  91.9 4.2 %collective-permute-start.5 = (f32[24,128]{1,0:T(8,128)S(1)}, f32[24,128]{1,0:T(8,128)S(1)}, u32[]{:S(2)}, u32[]{:S(2)}) collective-permute-start(f32[24,128]{1,0:T(8,128)S(1)} %get-tuple-element.76.half_ref), channel_id=1, source_target_pairs={{0,64},{32,96},{64,0},{96,32},{128,192},{160,224},{192,128},{224,1... | collective-permute-start | bytes 36872 | tf_op jit(solution)/shard_map/ppermute | solution.py:391
  103.4 12.5 %all-to-all-start.5 = ((f32[8,24,128]{2,1,0:T(8,128)}), f32[8,24,128]{2,1,0:T(8,128)S(1)}, u32[]{:S(2)}, u32[]{:S(2)}) async-start(f32[8,24,128]{2,1,0:T(8,128)} %get-tuple-element.81), calls=%async_computation.5 | async-start | bytes 196608 | tf_op jit(solution)/shard_map/all_to_all | solution.py:465
  108.4 2.8 %copy-start = (f32[2,16,3,128,128]{4,3,2,1,0:T(8,128)S(1)}, f32[2,16,3,128,128]{4,3,2,1,0:T(8,128)}, u32[]{:S(2)}) copy-start(f32[2,16,3,128,128]{4,3,2,1,0:T(8,128)} %param.9) | copy-start | bytes 18874372

commit v5 on v3

--- a/solution.py
+++ b/solution.py
@@ -19,7 +19,7 @@
 
 
 def call(kernel, outs, args, scalars=0, scratch=(), aliases=None, flops=0, hbm=(), still=()):
-    outs = [jax.ShapeDtypeStruct(o, F32) for o in outs]
+    outs = [jax.ShapeDtypeStruct(o, F32) if isinstance(o, tuple) else o for o in outs]
     args = [
         pltpu.with_memory_space_constraint(x, pltpu.HBM) if n in hbm else x for n, x in enumerate(args)
     ]
@@ -33,7 +33,7 @@
         out_specs=[ANY if n in still else VMEM for n in range(len(outs))],
         scratch_shapes=list(scratch),
         input_output_aliases=aliases or {},
-        compiler_params=pltpu.CompilerParams(vmem_limit_bytes=32 * 1024 * 1024),
+        compiler_params=pltpu.CompilerParams(vmem_limit_bytes=12 * 1024 * 1024),
         cost_estimate=pl.CostEstimate(flops=flops, bytes_accessed=4 * 1024 * 1024, transcendentals=0),
     )(*args)
 
@@ -88,11 +88,12 @@
     return total + tiles_ref[i, 1] * wide_ref[c * blocks + lax.rem(index_ref[1, c, j], blocks)]
 
 
-def near_kernel(comms, index_ref, v_ref, tiles_hbm, up_ref, tiles_ref, wide_ref, sems):
+def near_kernel(comms, index_ref, v_ref, tiles_hbm, pre_hbm, up_ref, pre_ref, tiles_ref, wide_ref, sems):
     count = up_ref.shape[0]
     arcs = count // comms
     blocks = v_ref.shape[0] // comms
     own = fetch(tiles_hbm.at[:, pl.ds(0, 2)], tiles_ref, sems, 0, PARTS)
+    (pre,) = fetch(pre_hbm, pre_ref, sems, PARTS, 1)
     widen(v_ref[...], wide_ref)
     step = count // PARTS
     for n in range(PARTS):
@@ -103,6 +104,7 @@
             return 0
 
         lax.fori_loop(n * step, (n + 1) * step, one, 0, unroll=4)
+    pre.wait()
 
 
 def cap_first_kernel(cap_rhs_ref, cap_precond_ref, q_ref):
@@ -167,22 +169,21 @@
     widen(q_ref[...], wide_ref)
     ft = far_ref[...].T
     step = count // PARTS
+    lane = lax.broadcasted_iota(jnp.int32, (width, width), 1)
+    turned = jnp.zeros((width, width), F32)
     for i in range(count):
         if i % step == 0:
             thirds[i // step].wait()
             caps_in[i // step].wait()
         column = jnp.broadcast_to(ft[:, i : i + 1], third_ref.shape[1:])
         total = third_ref[i] * column + cap_tiles_ref[i] * wide_ref[cap_index_ref[i // arcs, i % arcs]]
-        far_ref[i : i + 1] = up_ref[i : i + 1] + fold(total)
+        upward = up_ref[i : i + 1] + fold(total)
+        far_ref[i : i + 1] = upward
+        turned = beside(cap_tiles_ref[i], scale_ref[i : i + 1] * upward, lane, i, turned)
     upward = far_ref[...]
     scaled = scale_ref[...] * upward
     scaled_ref[...] = scaled
-    lane = lax.broadcasted_iota(jnp.int32, (width, width), 1)
-
-    def one(i, total):
-        return beside(cap_tiles_ref[i], scaled_ref[pl.ds(i, 1)], lane, i, total)
-
-    turn_ref[...] = lax.fori_loop(0, count, one, jnp.zeros((width, width), F32), unroll=2).T
+    turn_ref[...] = turned.T
     note_ref[...] = jnp.zeros_like(note_ref)
 
     def put(i, _):
@@ -221,29 +222,19 @@
     notes_ref[...] = jnp.broadcast_to(note_ref[...][None], notes_ref.shape)
 
 
-def down_kernel(comms, blocks, step_number, index_ref, scaled_ref, sums_ref, tiles_hbm, local_ref, back_ref,
-                tiles_ref, turn_ref, sems):
+def down_kernel(comms, blocks, step_number, index_ref, scaled_ref, sums_ref, tiles_ref, local_ref, back_ref, turn_ref):
     count, touched = tiles_ref.shape[:2]
     width = tiles_ref.shape[3]
     arcs = count // comms
-    parts = 2 * PARTS
-    step = count // parts
-    copies = fetch(tiles_hbm, tiles_ref, sems, 0, parts)
     local_ref[...] = jnp.zeros_like(local_ref)
     if step_number == 0:
         back_ref[...] = jnp.full(back_ref.shape, -1.0, F32)
     lane = lax.broadcasted_iota(jnp.int32, (width, width), 1)
     total = jnp.zeros((width, width), F32)
-    for n in range(parts):
-        copies[n].wait()
-
-        def one(i, total):
-            row = scaled_ref[pl.ds(i, 1)]
-            for k in range(touched):
-                total = beside(tiles_ref[i, k], row, lane, k * count + i, total)
-            return total
-
-        total = lax.fori_loop(n * step, (n + 1) * step, one, total)
+    for i in range(count):
+        row = scaled_ref[i : i + 1]
+        for k in range(touched):
+            total = beside(tiles_ref[i, k], row, lane, k * count + i, total)
     turn_ref[...] = total.T
 
     def put(i, _):
@@ -399,11 +390,12 @@
         return lax.ppermute(x, "comm", [(i, i ^ step) for i in range(peers)])
 
     def near(v):
-        (up,) = call(
-            functools.partial(near_kernel, comms), [arc_shape], (index, v, tiles), 1,
-            [room(count, 2, *flat), room(rows, *flat), sems(PARTS)], flops=2 * unit, hbm=(2,),
+        up, pre = call(
+            functools.partial(near_kernel, comms), [arc_shape, pltpu.VMEM((caps, *flat), F32)],
+            (index, v, tiles, cap_precond), 1,
+            [room(count, 2, *flat), room(rows, *flat), sems(PARTS + 1)], flops=2 * unit, hbm=(2, 3),
         )
-        return up
+        return up, kept(pre)
 
     up_room = [
         room(*arc_shape), room(count, *flat), room(count, *flat), room(caps, *flat), room(*flat), sems(2 * PARTS),
@@ -412,8 +404,7 @@
     def spread(step_number, scaled, sums):
         return call(
             functools.partial(down_kernel, comms, blocks, step_number), [row_shape, back_shape],
-            (index, scaled, sums, tiles), 1,
-            [room(count, touched, *flat), room(*flat), sems(2 * PARTS)], flops=3 * unit, hbm=(3,),
+            (index, scaled, sums, kept(tiles)), 1, [room(*flat)], flops=3 * unit,
         )
 
     def add(note, other, back):
@@ -424,46 +415,46 @@
         [room(*row_shape), room(rows, *flat), sems(PARTS + 1)], hbm=(0, 1),
     )
     got = exchange(send)
-    up = near(v0)
-    (q0,) = call(cap_first_kernel, [cap_shape], (cap_rhs, kept(cap_precond)), flops=unit)
+    up, pre = near(v0)
+    (q0,) = call(cap_first_kernel, [cap_shape], (cap_rhs, pre), flops=unit)
     scaled, note = call(
         functools.partial(up_first_kernel, comms, blocks, caps), [arc_shape, note_shape],
         (index, cap_index, up, got, q0, scale, rhs, v0, tiles, cap_tiles), 2, up_room, flops=3 * unit, hbm=(8, 9),
     )
-    other = across(note, 4)
+    other = across(note, 1)
     local, back = spread(0, scaled, rhs)
     note, back = add(note, other, back)
     back = exchange(back)
     half, y0, v1, send, asked = call(
         functools.partial(rows_second_kernel, comms),
         [note_shape, row_shape, row_shape, send_shape, (comms, groups, width)],
-        (v0, local, back, note, across(note, 1), kept(precond)),
+        (v0, local, back, note, across(note, 2), kept(precond)),
     )
     got = exchange(send)
-    other = across(half, 2)
-    up = near(v1)
+    other = across(half, 4)
+    up, pre = near(v1)
     yq0, q1, sums = call(
-        cap_second_kernel, [cap_shape, cap_shape, small], (cap_rhs, q0, half, other, kept(cap_precond)), flops=unit,
+        cap_second_kernel, [cap_shape, cap_shape, small], (cap_rhs, q0, half, other, pre), flops=unit,
     )
     scaled, note = call(
         functools.partial(up_second_kernel, comms, blocks), [arc_shape, note_shape],
         (index, cap_index, up, got, q1, scale, tiles, cap_tiles), 2, up_room, flops=3 * unit, hbm=(6, 7),
     )
-    other = across(note, 4)
+    other = across(note, 1)
     local, back = spread(1, scaled, sums)
     note, back = add(note, other, back)
     back = exchange(back)
     half, alpha, z1, yz, r1, v2, send = call(
         functools.partial(rows_third_kernel, comms),
         [note_shape, small, row_shape, row_shape, row_shape, row_shape, send_shape],
-        (rhs, v0, y0, v1, local, back, note, across(note, 1), asked, kept(precond)),
+        (rhs, v0, y0, v1, local, back, note, across(note, 2), asked, kept(precond)),
     )
     got = exchange(send)
-    other = across(half, 2)
-    up = near(v2)
+    other = across(half, 4)
+    up, pre = near(v2)
     zq1, yzq, rq1, q2, sums = call(
         cap_third_kernel, [cap_shape] * 4 + [small],
-        (alpha, cap_rhs, q0, yq0, q1, half, other, kept(cap_precond)), flops=unit,
+        (alpha, cap_rhs, q0, yq0, q1, half, other, pre), flops=unit,
     )
     scaled, notes = call(
         functools.partial(up_third_kernel, comms, blocks, caps), [arc_shape, (peers, *note_shape)],

time: 138 us -> 137 us (level)
  Pallas kernels: 53.2 us -> 46.3 us
  starting transfers between devices: 45.7 us -> 52.4 us
  waiting for transfers between devices: 21.3 us -> 16.9 us
  blocking collectives: 14 us -> 16.8 us
    pallas_call x19, Pallas kernels: 53.2 us -> 46.3 us  [call(): pl.pallas_call(kernel, out_shape=outs, in_specs=[HBM if n in hbm else ANY...]
    all_to_all x5, waiting for transfers between devices: 17.1 us -> 11 us  [exchange(): return lax.all_to_all(x, GROUP, 0, 0)]
    ppermute x6, starting transfers between devices: 12.4 us -> 17.1 us  [across(): return lax.ppermute(x, 'comm', [(i, i ^ step) for i in range(peers)])]
    all_to_all x5, starting transfers between devices: 26.9 us -> 30.4 us  [exchange(): return lax.all_to_all(x, GROUP, 0, 0)]
    all_to_all x1, blocking collectives: 14 us -> 16.8 us  [exchange(): return lax.all_to_all(x, GROUP, 0, 0)]
    all_to_all x1, starting transfers between devices: 6.37 us -> 4.91 us  [body(): notes = lax.all_to_all(notes, 'comm', 0, 0)]
    unnamed x20 -> x24, local copies, waits for them, and re-layouts: 2.63 us -> 3.51 us
  transfers between devices with their start and end apart: 12 -> 12, of which waited for: 8 -> 6; matrix products, arithmetic and copies ran while one was open for 0% -> 0% of each run, Pallas kernels for 22% -> 15%
where the time goes in v5:
time: 137 us
  starting transfers between devices  52.4 us (38%)
  Pallas kernels  46.3 us (34%)
  waiting for transfers between devices  16.9 us (12%)
  blocking collectives  16.8 us (12%)
  local copies, waits for them, and re-layouts  3.51 us (3%)
    pallas_call x19, Pallas kernels, call(): pl.pallas_call(kernel, out_shape=outs, in_specs=[HBM if n in hbm else ANY...  46.3 us
    all_to_all x5, starting transfers between devices, exchange(): return lax.all_to_all(x, GROUP, 0, 0)  30.4 us
    ppermute x6, starting transfers between devices, across(): return lax.ppermute(x, 'comm', [(i, i ^ step) for i in range(peers)])  17.1 us
    all_to_all x1, blocking collectives, exchange(): return lax.all_to_all(x, GROUP, 0, 0)  16.8 us
    all_to_all x5, waiting for transfers between devices, exchange(): return lax.all_to_all(x, GROUP, 0, 0)  11 us
    all_to_all x1, starting transfers between devices, body(): notes = lax.all_to_all(notes, 'comm', 0, 0)  4.91 us
    ppermute x6, waiting for transfers between devices, across(): return lax.ppermute(x, 'comm', [(i, i ^ step) for i in range(peers)])  3.94 us
    unnamed x24, local copies, waits for them, and re-layouts  3.51 us
  transfers between devices with their start and end apart: 12, of which 6 were waited for; matrix products, arithmetic and copies ran while one was open for 0% of the time, Pallas kernels for 15%

profile of v5, /device:TPU:1, one launch (start us, length us, event | category | flops | bytes accessed | tf_op | source)
XLA Modules:
  0.0 136.8 jit_solution(12459753358433900243)
XLA Ops:
  0.7 2.3 %shard_map.120 = (f32[16,128]{1,0:T(8,128)S(1)}, f32[32,16,128]{2,1,0:T(8,128)}) custom-call(f32[16,128]{1,0:T(8,128)} %bitcast.36, f32[16,128,128]{2,1,0:T(8,128)} %bitcast.21), custom_call_target="tpu_custom_call" | custom-call | bytes 4194304 | tf_op jit(solution)/shard_map/pallas_call | solution.py:27
  3.0 8.6 %all-to-all-start = ((f32[32,16,128]{2,1,0:T(8,128)}), f32[32,16,128]{2,1,0:T(8,128)S(1)}, u32[]{:S(2)}, u32[]{:S(2)}) async-start(f32[32,16,128]{2,1,0:T(8,128)} %get-tuple-element.56), calls=%async_computation | async-start | bytes 524288 | tf_op jit(solution)/shard_map/all_to_all | solution.py:387
  12.3 3.2 %shard_map.121 = (f32[32,128]{1,0:T(8,128)S(1)}, f32[16,128,128]{2,1,0:T(8,128)S(1)}) custom-call(s32[3,2,16]{2,1,0:T(2,128)S(1)} %bitcast.24, f32[16,128]{1,0:T(8,128)S(1)} %get-tuple-element.54.v_ref.v0_ref, f32[32,3,128,128]{3,2,1,0:T(8,128)} %bitcast.8, f32[16,128,128]{2,1,0:T(8,128)} %pre_hbm.5), custom_call_target="tpu_custom_call" | custom-call | flops 2097152 | bytes 4194304 | tf_op jit(solution)/shard_map/pallas_call | solution.py:27
  16.0 4.6 %all-to-all-done.got_ref = f32[32,16,128]{2,1,0:T(8,128)S(1)} async-done(((f32[32,16,128]{2,1,0:T(8,128)}), f32[32,16,128]{2,1,0:T(8,128)S(1)}, u32[]{:S(2)}, u32[]{:S(2)}) %all-to-all-start) | async-done | bytes 262176 | tf_op jit(solution)/shard_map/all_to_all | solution.py:387
  20.6 6.4 %shard_map.123 = (f32[32,128]{1,0:T(8,128)S(1)}, f32[24,128]{1,0:T(8,128)S(1)}) custom-call(s32[3,2,16]{2,1,0:T(2,128)S(1)} %bitcast.25, s32[2,16]{1,0:T(2,128)S(1)} %copy-done.7, f32[32,128]{1,0:T(8,128)S(1)} %get-tuple-element.55.up_ref, f32[32,16,128]{2,1,0:T(8,128)S(1)} %all-to-all-done.got_ref, f32[16,128]{1,0:T(8,128)S(1)} %shard_map.122.q_ref.q0_ref, ...), custom_call_target="tpu_custom_call" | custom-call | flops 3145728 | bytes 4194304 | tf_op jit(solution)/shard_map/pallas_call | solution.py:27
  27.0 1.7 %collective-permute-start = (f32[24,128]{1,0:T(8,128)S(1)}, f32[24,128]{1,0:T(8,128)S(1)}, u32[]{:S(2)}, u32[]{:S(2)}) collective-permute-start(f32[24,128]{1,0:T(8,128)S(1)} %get-tuple-element.60.note_ref), channel_id=1, source_target_pairs={{0,32},{32,0},{64,96},{96,64},{128,160},{160,128},{192,224},{224,1... | collective-permute-start | bytes 36872 | tf_op jit(solution)/shard_map/ppermute | solution.py:390
  28.8 3.4 %shard_map.124 = (f32[16,128]{1,0:T(8,128)S(1)}, f32[32,4,128]{2,1,0:T(4,128)}) custom-call(s32[3,2,16]{2,1,0:T(2,128)S(1)} %bitcast.26, f32[32,128]{1,0:T(8,128)S(1)} %get-tuple-element.58.scaled_ref, f32[16,128]{1,0:T(8,128)S(1)} %bitcast.38, f32[32,3,128,128]{3,2,1,0:T(8,128)S(1)} %bitcast.16), custom_call_target="tpu_custom_call" | custom-call | flops 3145728 | bytes 4194304 | tf_op jit(solution)/shard_map/pallas_call | solution.py:27
  32.2 4.0 %all-to-all-start.1 = ((f32[32,4,128]{2,1,0:T(4,128)}), f32[32,4,128]{2,1,0:T(4,128)S(1)}, u32[]{:S(2)}, u32[]{:S(2)}) async-start(f32[32,4,128]{2,1,0:T(4,128)} %get-tuple-element.62), calls=%async_computation.1 | async-start | bytes 131072 | tf_op jit(solution)/shard_map/all_to_all | solution.py:387
  36.3 3.1 %collective-permute-start.1 = (f32[24,128]{1,0:T(8,128)S(1)}, f32[24,128]{1,0:T(8,128)S(1)}, u32[]{:S(2)}, u32[]{:S(2)}) collective-permute-start(f32[24,128]{1,0:T(8,128)S(1)} %get-tuple-element.63.note_ref), channel_id=1, source_target_pairs={{0,64},{32,96},{64,0},{96,32},{128,192},{160,224},{192,128},{224,1... | collective-permute-start | bytes 36872 | tf_op jit(solution)/shard_map/ppermute | solution.py:390
  39.3 1.4 %collective-permute-done.1.came_ref = f32[24,128]{1,0:T(8,128)S(1)} collective-permute-done((f32[24,128]{1,0:T(8,128)S(1)}, f32[24,128]{1,0:T(8,128)S(1)}, u32[]{:S(2)}, u32[]{:S(2)}) %collective-permute-start.1) | collective-permute-done | bytes 12320 | tf_op jit(solution)/shard_map/ppermute | solution.py:390
  40.7 2.9 %all-to-all-done.1.back_ref = f32[32,4,128]{2,1,0:T(4,128)S(1)} async-done(((f32[32,4,128]{2,1,0:T(4,128)}), f32[32,4,128]{2,1,0:T(4,128)S(1)}, u32[]{:S(2)}, u32[]{:S(2)}) %all-to-all-start.1) | async-done | bytes 65568 | tf_op jit(solution)/shard_map/all_to_all | solution.py:387
  43.7 1.6 %shard_map.126 = (f32[24,128]{1,0:T(8,128)S(1)}, f32[16,128]{1,0:T(8,128)S(1)}, f32[16,128]{1,0:T(8,128)S(1)}, f32[32,2,128]{2,1,0:T(2,128)}, f32[2,32,128]{2,1,0:T(8,128)S(1)}) custom-call(f32[16,128]{1,0:T(8,128)S(1)} %get-tuple-element.54.v_ref.v0_ref, f32[16,128]{1,0:T(8,128)S(1)} %get-tuple-element.59.local_ref, ...), custom_call_target="tpu_custom_call" | custom-call | bytes 4194304 | tf_op jit(solution)/shard_map/pallas_call | solution.py:27
  45.2 5.1 %all-to-all-start.2 = ((f32[32,2,128]{2,1,0:T(2,128)}), f32[32,2,128]{2,1,0:T(2,128)S(1)}, u32[]{:S(2)}, u32[]{:S(2)}) async-start(f32[32,2,128]{2,1,0:T(2,128)} %get-tuple-element.67), calls=%async_computation.2 | async-start | bytes 65536 | tf_op jit(solution)/shard_map/all_to_all | solution.py:387
  50.3 5.9 %collective-permute-start.2 = (f32[24,128]{1,0:T(8,128)S(1)}, f32[24,128]{1,0:T(8,128)S(1)}, u32[]{:S(2)}, u32[]{:S(2)}) collective-permute-start(f32[24,128]{1,0:T(8,128)S(1)} %get-tuple-element.68.half_ref), channel_id=1, source_target_pairs={{0,128},{32,160},{64,192},{96,224},{128,0},{160,32},{192,64},{224,... | collective-permute-start | bytes 36872 | tf_op jit(solution)/shard_map/ppermute | solution.py:390
  56.3 3.2 %shard_map.127 = (f32[32,128]{1,0:T(8,128)S(1)}, f32[16,128,128]{2,1,0:T(8,128)S(1)}) custom-call(s32[3,2,16]{2,1,0:T(2,128)S(1)} %bitcast.27, f32[16,128]{1,0:T(8,128)S(1)} %get-tuple-element.65.v_ref.v1_ref, f32[32,3,128,128]{3,2,1,0:T(8,128)} %bitcast.10, f32[16,128,128]{2,1,0:T(8,128)} %pre_hbm.5), custom_call_target="tpu_custom_call" | custom-call | flops 2097152 | bytes 4194304 | tf_op jit(solution)/shard_map/pallas_call | solution.py:27
  60.0 6.4 %shard_map.129 = (f32[32,128]{1,0:T(8,128)S(1)}, f32[24,128]{1,0:T(8,128)S(1)}) custom-call(s32[3,2,16]{2,1,0:T(2,128)S(1)} %bitcast.28, s32[2,16]{1,0:T(2,128)S(1)} %copy-done.7, f32[32,128]{1,0:T(8,128)S(1)} %get-tuple-element.66.up_ref, f32[32,2,128]{2,1,0:T(2,128)S(1)} %all-to-all-done.2.got_ref, f32[16,128]{1,0:T(8,128)S(1)} %get-tuple-element.70.q_ref.q1_ref, ...), custom_call_target="tpu_custom_call" | custom-call | flops 3145728 | bytes 4194304 | tf_op jit(solution)/shard_map/pallas_call | solution.py:27
  66.4 0.8 collective-permute-start.3
  67.2 3.4 %shard_map.130 = (f32[16,128]{1,0:T(8,128)S(1)}, f32[32,4,128]{2,1,0:T(4,128)}) custom-call(s32[3,2,16]{2,1,0:T(2,128)S(1)} %bitcast.29, f32[32,128]{1,0:T(8,128)S(1)} %get-tuple-element.71.scaled_ref, f32[8,128]{1,0:T(8,128)S(1)} %get-tuple-element.72.sums_ref, f32[32,3,128,128]{3,2,1,0:T(8,128)S(1)} %bitcast.19), custom_call_target="tpu_custom_call" | custom-call | flops 3145728 | bytes 4194304 | tf_op jit(solution)/shard_map/pallas_call | solution.py:27
  70.6 7.9 %all-to-all-start.3 = ((f32[32,4,128]{2,1,0:T(4,128)}), f32[32,4,128]{2,1,0:T(4,128)S(1)}, u32[]{:S(2)}, u32[]{:S(2)}) async-start(f32[32,4,128]{2,1,0:T(4,128)} %get-tuple-element.76), calls=%async_computation.3 | async-start | bytes 131072 | tf_op jit(solution)/shard_map/all_to_all | solution.py:387
  78.6 1.3 collective-permute-start.4
  79.9 2.5 %collective-permute-done.4.came_ref = f32[24,128]{1,0:T(8,128)S(1)} collective-permute-done((f32[24,128]{1,0:T(8,128)S(1)}, f32[24,128]{1,0:T(8,128)S(1)}, u32[]{:S(2)}, u32[]{:S(2)}) %collective-permute-start.4) | collective-permute-done | bytes 12320 | tf_op jit(solution)/shard_map/ppermute | solution.py:390
  82.4 3.5 %all-to-all-done.3.back_ref = f32[32,4,128]{2,1,0:T(4,128)S(1)} async-done(((f32[32,4,128]{2,1,0:T(4,128)}), f32[32,4,128]{2,1,0:T(4,128)S(1)}, u32[]{:S(2)}, u32[]{:S(2)}) %all-to-all-start.3) | async-done | bytes 65568 | tf_op jit(solution)/shard_map/all_to_all | solution.py:387
  85.9 1.2 shard_map.132
  87.1 4.7 %all-to-all-start.4 = ((f32[32,2,128]{2,1,0:T(2,128)}), f32[32,2,128]{2,1,0:T(2,128)S(1)}, u32[]{:S(2)}, u32[]{:S(2)}) async-start(f32[32,2,128]{2,1,0:T(2,128)} %get-tuple-element.85), calls=%async_computation.4 | async-start | bytes 65536 | tf_op jit(solution)/shard_map/all_to_all | solution.py:387
  91.9 4.2 %collective-permute-start.5 = (f32[24,128]{1,0:T(8,128)S(1)}, f32[24,128]{1,0:T(8,128)S(1)}, u32[]{:S(2)}, u32[]{:S(2)}) collective-permute-start(f32[24,128]{1,0:T(8,128)S(1)} %get-tuple-element.87.half_ref), channel_id=1, source_target_pairs={{0,128},{32,160},{64,192},{96,224},{128,0},{160,32},{192,64},{224,... | collective-permute-start | bytes 36872 | tf_op jit(solution)/shard_map/ppermute | solution.py:390
  96.1 3.1 %shard_map.133 = (f32[32,128]{1,0:T(8,128)S(1)}, f32[16,128,128]{2,1,0:T(8,128)S(1)}) custom-call(s32[3,2,16]{2,1,0:T(2,128)S(1)} %bitcast.30, f32[16,128]{1,0:T(8,128)S(1)} %get-tuple-element.83.v_ref.v2_ref, f32[32,3,128,128]{3,2,1,0:T(8,128)} %bitcast.12, f32[16,128,128]{2,1,0:T(8,128)} %pre_hbm.5), custom_call_target="tpu_custom_call" | custom-call | flops 2097152 | bytes 4194304 | tf_op jit(solution)/shard_map/pallas_call | solution.py:27
  99.8 6.9 %shard_map.135 = (f32[32,128]{1,0:T(8,128)S(1)}, f32[8,24,128]{2,1,0:T(8,128)}) custom-call(s32[3,2,16]{2,1,0:T(2,128)S(1)} %bitcast.31, s32[2,16]{1,0:T(2,128)S(1)} %copy-done.7, f32[32,128]{1,0:T(8,128)S(1)} %get-tuple-element.84.up_ref, f32[32,2,128]{2,1,0:T(2,128)S(1)} %all-to-all-done.4.got_ref, f32[16,128]{1,0:T(8,128)S(1)} %get-tuple-element.89.q_ref.q2_ref, ...), custom_call_target="tpu_custom_call" | custom-call | flops 3145728 | bytes 4194304 | tf_op jit(solution)/shard_map/pallas_call | solution.py:27
  106.7 4.9 %all-to-all-start.5 = ((f32[8,24,128]{2,1,0:T(8,128)}), f32[8,24,128]{2,1,0:T(8,128)S(1)}, u32[]{:S(2)}, u32[]{:S(2)}) async-start(f32[8,24,128]{2,1,0:T(8,128)} %get-tuple-element.93), calls=%async_computation.5 | async-start | bytes 196608 | tf_op jit(solution)/shard_map/all_to_all | solution.py:464
  111.6 2.8 %copy-done = f32[2,16,3,128,128]{4,3,2,1,0:T(8,128)S(1)} copy-done((f32[2,16,3,128,128]{4,3,2,1,0:T(8,128)S(1)}, f32[2,16,3,128,128]{4,3,2,1,0:T(8,128)}, u32[]{:S(2)}) %copy-start) | copy-done | bytes 6291480
  114.4 2.8 %shard_map.136 = (f32[16,128]{1,0:T(8,128)S(1)}, f32[32,4,128]{2,1,0:T(4,128)S(1)}) custom-call(s32[3,2,16]{2,1,0:T(2,128)S(1)} %bitcast.32, f32[32,128]{1,0:T(8,128)S(1)} %get-tuple-element.90.scaled_ref, f32[8,128]{1,0:T(8,128)S(1)} %get-tuple-element.91.sums_ref, f32[32,3,128,128]{3,2,1,0:T(8,128)S(1)} %bitcast.20), custom_call_target="tpu_custom_call" | custom-call | flops 3145728 | bytes 4194304 | tf_op jit(solution)/shard_map/pallas_call | solution.py:27
  117.1 2.0 %all-to-all-done.5.notes_ref = f32[8,24,128]{2,1,0:T(8,128)S(1)} async-done(((f32[8,24,128]{2,1,0:T(8,128)}), f32[8,24,128]{2,1,0:T(8,128)S(1)}, u32[]{:S(2)}, u32[]{:S(2)}) %all-to-all-start.5) | async-done | bytes 98336 | tf_op jit(solution)/shard_map/all_to_all | solution.py:464
  119.3 16.8 %all_to_all.35.back_ref = f32[32,4,128]{2,1,0:T(4,128)S(1)} all-to-all(f32[32,4,128]{2,1,0:T(4,128)S(1)} %get-tuple-element.95), channel_id=1, replica_groups=mesh['comm'=8,'stn'=16,'tm'=2] {'stn','tm'}, dimensions={0} | all-to-all | bytes 131072 | tf_op jit(solution)/shard_map/all_to_all | solution.py:387
  (38 shorter events, 3.1 us)
Async XLA Ops:
  0.6 19.9 %copy-start.5 = (f32[2,8,128]{2,1,0:T(8,128)S(1)}, f32[2,8,128]{2,1,0:T(8,128)}, u32[]{:S(2)}) copy-start(f32[2,8,128]{2,1,0:T(8,128)} %param.14) | copy-start | bytes 24580
  0.6 19.9 %copy-start.3 = (s32[2,16,3]{1,0,2:T(2,128)S(1)}, s32[2,16,3]{1,0,2:T(2,128)}, u32[]{:S(2)}) copy-start(s32[2,16,3]{1,0,2:T(2,128)} %param.11) | copy-start | bytes 1156
  0.7 14.8 %copy-start.6 = (f32[16,128]{1,0:T(8,128)S(1)}, f32[16,128]{1,0:T(8,128)}, u32[]{:S(2)}) copy-start(f32[16,128]{1,0:T(8,128)} %cap_rhs_ref.5) | copy-start | bytes 24580
  0.7 19.9 %copy-start.7 = (s32[2,16]{1,0:T(2,128)S(1)}, s32[2,16]{1,0:T(2,128)}, u32[]{:S(2)}) copy-start(s32[2,16]{1,0:T(2,128)} %cap_index_ref.5) | copy-start | bytes 388
  0.7 19.9 %copy-start.4 = (f32[2,16,128]{2,1,0:T(8,128)S(1)}, f32[2,16,128]{2,1,0:T(8,128)}, u32[]{:S(2)}) copy-start(f32[2,16,128]{2,1,0:T(8,128)} %param.13) | copy-start | bytes 49156
  3.0 17.5 %all-to-all-start = ((f32[32,16,128]{2,1,0:T(8,128)}), f32[32,16,128]{2,1,0:T(8,128)S(1)}, u32[]{:S(2)}, u32[]{:S(2)}) async-start(f32[32,16,128]{2,1,0:T(8,128)} %get-tuple-element.56), calls=%async_computation | async-start | bytes 524288 | tf_op jit(solution)/shard_map/all_to_all | solution.py:387
  11.6 0.7 copy-start.2
  12.3 16.4 %slice-start = ((s8[6291456]{0:T(1024)(128)(4,1)}), s8[2097152]{0:T(1024)(128)(4,1)S(1)}, s32[]{:S(2)}) async-start(s8[6291456]{0:T(1024)(128)(4,1)} %bitcast.14), calls=%async_computation.7 | async-start | bytes 4194304
  20.6 8.2 %slice-start.1 = ((s8[6291456]{0:T(1024)(128)(4,1)}), s8[4194304]{0:T(1024)(128)(4,1)S(1)}, s32[]{:S(2)}) async-start(s8[6291456]{0:T(1024)(128)(4,1)} %bitcast.14), calls=%async_computation.8 | async-start | bytes 8388608
  20.6 23.1 %copy-start.1 = (f32[2,8,128,128]{3,2,1,0:T(8,128)S(1)}, f32[2,8,128,128]{3,2,1,0:T(8,128)}, u32[]{:S(2)}) copy-start(f32[2,8,128,128]{3,2,1,0:T(8,128)} %param.16) | copy-start | bytes 3145732
  27.0 5.2 %collective-permute-start = (f32[24,128]{1,0:T(8,128)S(1)}, f32[24,128]{1,0:T(8,128)S(1)}, u32[]{:S(2)}, u32[]{:S(2)}) collective-permute-start(f32[24,128]{1,0:T(8,128)S(1)} %get-tuple-element.60.note_ref), channel_id=1, source_target_pairs={{0,32},{32,0},{64,96},{96,64},{128,160},{160,128},{192,224},{224,1... | collective-permute-start | bytes 36872 | tf_op jit(solution)/shard_map/ppermute | solution.py:390
  32.2 11.4 %all-to-all-start.1 = ((f32[32,4,128]{2,1,0:T(4,128)}), f32[32,4,128]{2,1,0:T(4,128)S(1)}, u32[]{:S(2)}, u32[]{:S(2)}) async-start(f32[32,4,128]{2,1,0:T(4,128)} %get-tuple-element.62), calls=%async_computation.1 | async-start | bytes 131072 | tf_op jit(solution)/shard_map/all_to_all | solution.py:387
  36.3 4.5 %collective-permute-start.1 = (f32[24,128]{1,0:T(8,128)S(1)}, f32[24,128]{1,0:T(8,128)S(1)}, u32[]{:S(2)}, u32[]{:S(2)}) collective-permute-start(f32[24,128]{1,0:T(8,128)S(1)} %get-tuple-element.63.note_ref), channel_id=1, source_target_pairs={{0,64},{32,96},{64,0},{96,32},{128,192},{160,224},{192,128},{224,1... | collective-permute-start | bytes 36872 | tf_op jit(solution)/shard_map/ppermute | solution.py:390
  45.2 14.7 %all-to-all-start.2 = ((f32[32,2,128]{2,1,0:T(2,128)}), f32[32,2,128]{2,1,0:T(2,128)S(1)}, u32[]{:S(2)}, u32[]{:S(2)}) async-start(f32[32,2,128]{2,1,0:T(2,128)} %get-tuple-element.67), calls=%async_computation.2 | async-start | bytes 65536 | tf_op jit(solution)/shard_map/all_to_all | solution.py:387
  50.3 9.1 %collective-permute-start.2 = (f32[24,128]{1,0:T(8,128)S(1)}, f32[24,128]{1,0:T(8,128)S(1)}, u32[]{:S(2)}, u32[]{:S(2)}) collective-permute-start(f32[24,128]{1,0:T(8,128)S(1)} %get-tuple-element.68.half_ref), channel_id=1, source_target_pairs={{0,128},{32,160},{64,192},{96,224},{128,0},{160,32},{192,64},{224,... | collective-permute-start | bytes 36872 | tf_op jit(solution)/shard_map/ppermute | solution.py:390
  56.3 10.9 %slice-start.2 = ((s8[6291456]{0:T(1024)(128)(4,1)}), s8[2097152]{0:T(1024)(128)(4,1)S(1)}, s32[]{:S(2)}) async-start(s8[6291456]{0:T(1024)(128)(4,1)} %bitcast.17), calls=%async_computation.9 | async-start | bytes 4194304
  59.9 7.3 %slice-start.3 = ((s8[6291456]{0:T(1024)(128)(4,1)}), s8[4194304]{0:T(1024)(128)(4,1)S(1)}, s32[]{:S(2)}) async-start(s8[6291456]{0:T(1024)(128)(4,1)} %bitcast.17), calls=%async_computation.10 | async-start | bytes 8388608
  66.4 4.2 %collective-permute-start.3 = (f32[24,128]{1,0:T(8,128)S(1)}, f32[24,128]{1,0:T(8,128)S(1)}, u32[]{:S(2)}, u32[]{:S(2)}) collective-permute-start(f32[24,128]{1,0:T(8,128)S(1)} %get-tuple-element.74.note_ref), channel_id=1, source_target_pairs={{0,32},{32,0},{64,96},{96,64},{128,160},{160,128},{192,224},{224,1... | collective-permute-start | bytes 36872 | tf_op jit(solution)/shard_map/ppermute | solution.py:390
  70.6 15.3 %all-to-all-start.3 = ((f32[32,4,128]{2,1,0:T(4,128)}), f32[32,4,128]{2,1,0:T(4,128)S(1)}, u32[]{:S(2)}, u32[]{:S(2)}) async-start(f32[32,4,128]{2,1,0:T(4,128)} %get-tuple-element.76), calls=%async_computation.3 | async-start | bytes 131072 | tf_op jit(solution)/shard_map/all_to_all | solution.py:387
  78.6 3.8 %collective-permute-start.4 = (f32[24,128]{1,0:T(8,128)S(1)}, f32[24,128]{1,0:T(8,128)S(1)}, u32[]{:S(2)}, u32[]{:S(2)}) collective-permute-start(f32[24,128]{1,0:T(8,128)S(1)} %get-tuple-element.77.note_ref), channel_id=1, source_target_pairs={{0,64},{32,96},{64,0},{96,32},{128,192},{160,224},{192,128},{224,1... | collective-permute-start | bytes 36872 | tf_op jit(solution)/shard_map/ppermute | solution.py:390
  87.1 12.6 %all-to-all-start.4 = ((f32[32,2,128]{2,1,0:T(2,128)}), f32[32,2,128]{2,1,0:T(2,128)S(1)}, u32[]{:S(2)}, u32[]{:S(2)}) async-start(f32[32,2,128]{2,1,0:T(2,128)} %get-tuple-element.85), calls=%async_computation.4 | async-start | bytes 65536 | tf_op jit(solution)/shard_map/all_to_all | solution.py:387
  91.9 7.4 %collective-permute-start.5 = (f32[24,128]{1,0:T(8,128)S(1)}, f32[24,128]{1,0:T(8,128)S(1)}, u32[]{:S(2)}, u32[]{:S(2)}) collective-permute-start(f32[24,128]{1,0:T(8,128)S(1)} %get-tuple-element.87.half_ref), channel_id=1, source_target_pairs={{0,128},{32,160},{64,192},{96,224},{128,0},{160,32},{192,64},{224,... | collective-permute-start | bytes 36872 | tf_op jit(solution)/shard_map/ppermute | solution.py:390
  106.7 12.5 %all-to-all-start.5 = ((f32[8,24,128]{2,1,0:T(8,128)}), f32[8,24,128]{2,1,0:T(8,128)S(1)}, u32[]{:S(2)}, u32[]{:S(2)}) async-start(f32[8,24,128]{2,1,0:T(8,128)} %get-tuple-element.93), calls=%async_computation.5 | async-start | bytes 196608 | tf_op jit(solution)/shard_map/all_to_all | solution.py:464
  111.6 2.8 %copy-start = (f32[2,16,3,128,128]{4,3,2,1,0:T(8,128)S(1)}, f32[2,16,3,128,128]{4,3,2,1,0:T(8,128)}, u32[]{:S(2)}) copy-start(f32[2,16,3,128,128]{4,3,2,1,0:T(8,128)} %param.9) | copy-start | bytes 18874372

commit v6 on v5

--- a/solution.py
+++ b/solution.py
@@ -12,23 +12,40 @@
 SLOT = 4
 NOTE = 8
 VMEM = pl.BlockSpec(memory_space=pltpu.VMEM)
-SMEM = pl.BlockSpec(memory_space=pltpu.SMEM)
 HBM = pl.BlockSpec(memory_space=pltpu.HBM)
 ANY = pl.BlockSpec(memory_space=pl.ANY)
 PARTS = 4
 
 
 def call(kernel, outs, args, scalars=0, scratch=(), aliases=None, flops=0, hbm=(), still=()):
+    if scalars:
+        inner = kernel
+
+        def kernel(*refs):
+            sems, held = refs[-1], refs[-1 - scalars : -1]
+            copies = [pltpu.make_async_copy(refs[n], held[n], sems.at[n]) for n in range(scalars)]
+            for copy in copies:
+                copy.start()
+
+            def ready():
+                for copy in copies:
+                    copy.wait()
+
+            inner(*held, *refs[scalars : -1 - scalars], ready=ready)
+
+        hbm = (*range(scalars), *hbm)
+        scratch = [
+            *scratch, *(pltpu.SMEM(x.shape, x.dtype) for x in args[:scalars]), pltpu.SemaphoreType.DMA((scalars,)),
+        ]
     outs = [jax.ShapeDtypeStruct(o, F32) if isinstance(o, tuple) else o for o in outs]
     args = [
         pltpu.with_memory_space_constraint(x, pltpu.HBM) if n in hbm else x for n, x in enumerate(args)
     ]
-    specs = [SMEM] * scalars + [VMEM] * (len(args) - scalars)
     return pl.pallas_call(
         kernel,
         out_shape=outs,
         in_specs=[
-            HBM if n in hbm else ANY if (aliases or {}).get(n) in still else spec for n, spec in enumerate(specs)
+            HBM if n in hbm else ANY if (aliases or {}).get(n) in still else VMEM for n in range(len(args))
         ],
         out_specs=[ANY if n in still else VMEM for n in range(len(outs))],
         scratch_shapes=list(scratch),
@@ -88,13 +105,14 @@
     return total + tiles_ref[i, 1] * wide_ref[c * blocks + lax.rem(index_ref[1, c, j], blocks)]
 
 
-def near_kernel(comms, index_ref, v_ref, tiles_hbm, pre_hbm, up_ref, pre_ref, tiles_ref, wide_ref, sems):
+def near_kernel(comms, index_ref, v_ref, tiles_hbm, pre_hbm, up_ref, pre_ref, tiles_ref, wide_ref, sems, ready):
     count = up_ref.shape[0]
     arcs = count // comms
     blocks = v_ref.shape[0] // comms
     own = fetch(tiles_hbm.at[:, pl.ds(0, 2)], tiles_ref, sems, 0, PARTS)
     (pre,) = fetch(pre_hbm, pre_ref, sems, PARTS, 1)
     widen(v_ref[...], wide_ref)
+    ready()
     step = count // PARTS
     for n in range(PARTS):
         own[n].wait()
@@ -151,12 +169,14 @@
 
 
 def arcs_up(comms, blocks, index_ref, cap_index_ref, up_ref, got_ref, q_ref, scale_ref, tiles_hbm, cap_tiles_hbm,
-            scaled_ref, note_ref, far_ref, third_ref, cap_tiles_ref, wide_ref, turn_ref, sems):
+            scaled_ref, note_ref, far_ref, third_ref, cap_tiles_ref, wide_ref, turn_ref, sems, ready):
     count = up_ref.shape[0]
     arcs = count // comms
     width = scale_ref.shape[1]
     thirds = fetch(tiles_hbm.at[:, 2], third_ref, sems, 0, PARTS)
     caps_in = fetch(cap_tiles_hbm, cap_tiles_ref, sems, PARTS, PARTS)
+    widen(q_ref[...], wide_ref)
+    ready()
 
     def place(i, _):
         c, j = lax.div(i, arcs), lax.rem(i, arcs)
@@ -166,24 +186,24 @@
         return 0
 
     lax.fori_loop(0, count, place, 0, unroll=4)
-    widen(q_ref[...], wide_ref)
     ft = far_ref[...].T
     step = count // PARTS
-    lane = lax.broadcasted_iota(jnp.int32, (width, width), 1)
-    turned = jnp.zeros((width, width), F32)
     for i in range(count):
         if i % step == 0:
             thirds[i // step].wait()
             caps_in[i // step].wait()
         column = jnp.broadcast_to(ft[:, i : i + 1], third_ref.shape[1:])
         total = third_ref[i] * column + cap_tiles_ref[i] * wide_ref[cap_index_ref[i // arcs, i % arcs]]
-        upward = up_ref[i : i + 1] + fold(total)
-        far_ref[i : i + 1] = upward
-        turned = beside(cap_tiles_ref[i], scale_ref[i : i + 1] * upward, lane, i, turned)
+        far_ref[i : i + 1] = up_ref[i : i + 1] + fold(total)
     upward = far_ref[...]
     scaled = scale_ref[...] * upward
     scaled_ref[...] = scaled
-    turn_ref[...] = turned.T
+    lane = lax.broadcasted_iota(jnp.int32, (width, width), 1)
+
+    total = jnp.zeros((width, width), F32)
+    for i in range(count):
+        total = beside(cap_tiles_ref[i], scaled[i : i + 1], lane, i, total)
+    turn_ref[...] = total.T
     note_ref[...] = jnp.zeros_like(note_ref)
 
     def put(i, _):
@@ -196,24 +216,24 @@
 
 
 def up_first_kernel(comms, blocks, caps, index_ref, cap_index_ref, up_ref, got_ref, q_ref, scale_ref, rhs_ref, v_ref,
-                    tiles_hbm, cap_tiles_hbm, scaled_ref, note_ref, *room):
+                    tiles_hbm, cap_tiles_hbm, scaled_ref, note_ref, *room, ready):
     energy = arcs_up(comms, blocks, index_ref, cap_index_ref, up_ref, got_ref, q_ref, scale_ref, tiles_hbm,
-                     cap_tiles_hbm, scaled_ref, note_ref, *room)
+                     cap_tiles_hbm, scaled_ref, note_ref, *room, ready)
     v = v_ref[...]
     note_ref[caps : caps + 1] = fold(rhs_ref[...] * v)
     note_ref[caps + 1 : caps + 2] = fold(v * v) + energy
 
 
 def up_second_kernel(comms, blocks, index_ref, cap_index_ref, up_ref, got_ref, q_ref, scale_ref, tiles_hbm,
-                     cap_tiles_hbm, scaled_ref, note_ref, *room):
+                     cap_tiles_hbm, scaled_ref, note_ref, *room, ready):
     arcs_up(comms, blocks, index_ref, cap_index_ref, up_ref, got_ref, q_ref, scale_ref, tiles_hbm,
-            cap_tiles_hbm, scaled_ref, note_ref, *room)
+            cap_tiles_hbm, scaled_ref, note_ref, *room, ready)
 
 
 def up_third_kernel(comms, blocks, caps, index_ref, cap_index_ref, up_ref, got_ref, q_ref, scale_ref, z_ref, yz_ref,
-                    r_ref, y0_ref, v_ref, tiles_hbm, cap_tiles_hbm, scaled_ref, notes_ref, note_ref, *room):
+                    r_ref, y0_ref, v_ref, tiles_hbm, cap_tiles_hbm, scaled_ref, notes_ref, note_ref, *room, ready):
     energy = arcs_up(comms, blocks, index_ref, cap_index_ref, up_ref, got_ref, q_ref, scale_ref, tiles_hbm,
-                     cap_tiles_hbm, scaled_ref, note_ref, *room)
+                     cap_tiles_hbm, scaled_ref, note_ref, *room, ready)
     z, yz, r, y0, v = z_ref[...], yz_ref[...], r_ref[...], y0_ref[...], v_ref[...]
     pairs = ((z, y0), (z, yz), (v, y0), (v, yz), (v, v), (z, r), (v, r))
     for n, (one, other) in enumerate(pairs):
@@ -222,7 +242,7 @@
     notes_ref[...] = jnp.broadcast_to(note_ref[...][None], notes_ref.shape)
 
 
-def down_kernel(comms, blocks, step_number, index_ref, scaled_ref, sums_ref, tiles_ref, local_ref, back_ref, turn_ref):
+def down_kernel(comms, blocks, step_number, index_ref, scaled_ref, sums_ref, tiles_ref, local_ref, back_ref, turn_ref, ready):
     count, touched = tiles_ref.shape[:2]
     width = tiles_ref.shape[3]
     arcs = count // comms
@@ -236,6 +256,7 @@
         for k in range(touched):
             total = beside(tiles_ref[i, k], row, lane, k * count + i, total)
     turn_ref[...] = total.T
+    ready()
 
     def put(i, _):
         c, j = lax.div(i, arcs), lax.rem(i, arcs)
@@ -421,17 +442,17 @@
         functools.partial(up_first_kernel, comms, blocks, caps), [arc_shape, note_shape],
         (index, cap_index, up, got, q0, scale, rhs, v0, tiles, cap_tiles), 2, up_room, flops=3 * unit, hbm=(8, 9),
     )
-    other = across(note, 1)
+    other = across(note, 4)
     local, back = spread(0, scaled, rhs)
     note, back = add(note, other, back)
     back = exchange(back)
     half, y0, v1, send, asked = call(
         functools.partial(rows_second_kernel, comms),
         [note_shape, row_shape, row_shape, send_shape, (comms, groups, width)],
-        (v0, local, back, note, across(note, 2), kept(precond)),
+        (v0, local, back, note, across(note, 1), kept(precond)),
     )
     got = exchange(send)
-    other = across(half, 4)
+    other = across(half, 2)
     up, pre = near(v1)
     yq0, q1, sums = call(
         cap_second_kernel, [cap_shape, cap_shape, small], (cap_rhs, q0, half, other, pre), flops=unit,
@@ -440,17 +461,17 @@
         functools.partial(up_second_kernel, comms, blocks), [arc_shape, note_shape],
         (index, cap_index, up, got, q1, scale, tiles, cap_tiles), 2, up_room, flops=3 * unit, hbm=(6, 7),
     )
-    other = across(note, 1)
+    other = across(note, 4)
     local, back = spread(1, scaled, sums)
     note, back = add(note, other, back)
     back = exchange(back)
     half, alpha, z1, yz, r1, v2, send = call(
         functools.partial(rows_third_kernel, comms),
         [note_shape, small, row_shape, row_shape, row_shape, row_shape, send_shape],
-        (rhs, v0, y0, v1, local, back, note, across(note, 2), asked, kept(precond)),
+        (rhs, v0, y0, v1, local, back, note, across(note, 1), asked, kept(precond)),
     )
     got = exchange(send)
-    other = across(half, 4)
+    other = across(half, 2)
     up, pre = near(v2)
     zq1, yzq, rq1, q2, sums = call(
         cap_third_kernel, [cap_shape] * 4 + [small],

time: 137 us -> 128 us (0.934)
  Pallas kernels: 46.3 us -> 36.5 us
  waiting for transfers between devices: 16.9 us -> 26.4 us
  starting transfers between devices: 52.4 us -> 46.7 us
  blocking collectives: 16.8 us -> 14 us
    pallas_call x19, Pallas kernels: 46.3 us -> 36.5 us  [call(): pl.pallas_call(kernel, out_shape=outs, in_specs=[HBM if n in hbm else ANY...]
    all_to_all x5, waiting for transfers between devices: 11 us -> 20.5 us  [exchange(): return lax.all_to_all(x, GROUP, 0, 0)]
    all_to_all x5, starting transfers between devices: 30.4 us -> 26.2 us  [exchange(): return lax.all_to_all(x, GROUP, 0, 0)]
    all_to_all x1, blocking collectives: 16.8 us -> 14 us  [exchange(): return lax.all_to_all(x, GROUP, 0, 0)]
    ppermute x6, starting transfers between devices: 17.1 us -> 15.3 us  [across(): return lax.ppermute(x, 'comm', [(i, i ^ step) for i in range(peers)])]
    unnamed x24 -> x18, local copies, waits for them, and re-layouts: 3.51 us -> 2.81 us
  transfers between devices with their start and end apart: 12 -> 12, of which waited for: 6 -> 8; matrix products, arithmetic and copies ran while one was open for 0% -> 0% of each run, Pallas kernels for 15% -> 15%
where the time goes in v6:
time: 128 us; the launch traced here: 127 us
  starting transfers between devices  46.7 us (36%)
  Pallas kernels  36.5 us (29%)
  waiting for transfers between devices  26.4 us (21%)
  blocking collectives  14 us (11%)
  local copies, waits for them, and re-layouts  2.81 us (2%)
    pallas_call x19, Pallas kernels, call(): pl.pallas_call(kernel, out_shape=outs, in_specs=[HBM if n in hbm else ANY...  36.5 us
    all_to_all x5, starting transfers between devices, exchange(): return lax.all_to_all(x, GROUP, 0, 0)  26.2 us
    all_to_all x5, waiting for transfers between devices, exchange(): return lax.all_to_all(x, GROUP, 0, 0)  20.5 us
    ppermute x6, starting transfers between devices, across(): return lax.ppermute(x, 'comm', [(i, i ^ step) for i in range(peers)])  15.3 us
    all_to_all x1, blocking collectives, exchange(): return lax.all_to_all(x, GROUP, 0, 0)  14 us
    all_to_all x1, starting transfers between devices, body(): notes = lax.all_to_all(notes, 'comm', 0, 0)  5.14 us
    ppermute x6, waiting for transfers between devices, across(): return lax.ppermute(x, 'comm', [(i, i ^ step) for i in range(peers)])  3.97 us
    unnamed x18, local copies, waits for them, and re-layouts  2.81 us
  transfers between devices with their start and end apart: 12, of which 8 were waited for; matrix products, arithmetic and copies ran while one was open for 0% of the time, Pallas kernels for 15%

profile of v6, /device:TPU:1, one launch (start us, length us, event | category | flops | bytes accessed | tf_op | source)
XLA Modules:
  0.0 127.2 jit_solution(800441448945264227)
XLA Ops:
  0.7 2.3 %shard_map.120 = (f32[16,128]{1,0:T(8,128)S(1)}, f32[32,16,128]{2,1,0:T(8,128)}) custom-call(f32[16,128]{1,0:T(8,128)} %bitcast.27, f32[16,128,128]{2,1,0:T(8,128)} %bitcast.21), custom_call_target="tpu_custom_call" | custom-call | bytes 4194304 | tf_op jit(solution)/shard_map/pallas_call | solution.py:44
  3.0 8.6 %all-to-all-start = ((f32[32,16,128]{2,1,0:T(8,128)}), f32[32,16,128]{2,1,0:T(8,128)S(1)}, u32[]{:S(2)}, u32[]{:S(2)}) async-start(f32[32,16,128]{2,1,0:T(8,128)} %get-tuple-element.56), calls=%async_computation | async-start | bytes 524288 | tf_op jit(solution)/shard_map/all_to_all | solution.py:408
  11.6 2.7 %shard_map.121 = (f32[32,128]{1,0:T(8,128)S(1)}, f32[16,128,128]{2,1,0:T(8,128)S(1)}) custom-call(s32[3,2,16]{2,1,0:T(2,128)} %bitcast.34, f32[16,128]{1,0:T(8,128)S(1)} %get-tuple-element.54.refs_1_.refs_7_.v0_ref, f32[32,3,128,128]{3,2,1,0:T(8,128)} %bitcast.8, f32[16,128,128]{2,1,0:T(8,128)} %refs_3_.5), custom_call_target="tpu_custom_call" | custom-call | flops 2097152 | bytes 4194304 | tf_op jit(solution)/shard_map/pallas_call | solution.py:44
  14.8 5.7 %all-to-all-done.refs_3_ = f32[32,16,128]{2,1,0:T(8,128)S(1)} async-done(((f32[32,16,128]{2,1,0:T(8,128)}), f32[32,16,128]{2,1,0:T(8,128)S(1)}, u32[]{:S(2)}, u32[]{:S(2)}) %all-to-all-start) | async-done | bytes 262176 | tf_op jit(solution)/shard_map/all_to_all | solution.py:408
  20.5 3.6 %shard_map.123 = (f32[32,128]{1,0:T(8,128)S(1)}, f32[24,128]{1,0:T(8,128)S(1)}) custom-call(s32[3,2,16]{2,1,0:T(2,128)} %bitcast.35, s32[2,16]{1,0:T(2,128)} %refs_1_.5, f32[32,128]{1,0:T(8,128)S(1)} %get-tuple-element.55.refs_2_, f32[32,16,128]{2,1,0:T(8,128)S(1)} %all-to-all-done.refs_3_, f32[16,128]{1,0:T(8,128)S(1)} %shard_map.122.refs_4_.q0_ref, ...), custom_call_target="tpu_custom_call" | custom-call | flops 3145728 | bytes 4194304 | tf_op jit(solution)/shard_map/pallas_call | solution.py:44
  24.2 7.0 %collective-permute-start = (f32[24,128]{1,0:T(8,128)S(1)}, f32[24,128]{1,0:T(8,128)S(1)}, u32[]{:S(2)}, u32[]{:S(2)}) collective-permute-start(f32[24,128]{1,0:T(8,128)S(1)} %get-tuple-element.60.note_ref), channel_id=1, source_target_pairs={{0,128},{32,160},{64,192},{96,224},{128,0},{160,32},{192,64},{224,... | collective-permute-start | bytes 36872 | tf_op jit(solution)/shard_map/ppermute | solution.py:411
  31.2 3.4 %shard_map.124 = (f32[16,128]{1,0:T(8,128)S(1)}, f32[32,4,128]{2,1,0:T(4,128)}) custom-call(s32[3,2,16]{2,1,0:T(2,128)} %bitcast.36, f32[32,128]{1,0:T(8,128)S(1)} %get-tuple-element.58.refs_1_, f32[16,128]{1,0:T(8,128)S(1)} %bitcast.29, f32[32,3,128,128]{3,2,1,0:T(8,128)S(1)} %bitcast.16), custom_call_target="tpu_custom_call" | custom-call | flops 3145728 | bytes 4194304 | tf_op jit(solution)/shard_map/pallas_call | solution.py:44
  34.6 4.0 %all-to-all-start.1 = ((f32[32,4,128]{2,1,0:T(4,128)}), f32[32,4,128]{2,1,0:T(4,128)S(1)}, u32[]{:S(2)}, u32[]{:S(2)}) async-start(f32[32,4,128]{2,1,0:T(4,128)} %get-tuple-element.62), calls=%async_computation.1 | async-start | bytes 131072 | tf_op jit(solution)/shard_map/all_to_all | solution.py:408
  39.5 2.0 %collective-permute-done.1.came_ref = f32[24,128]{1,0:T(8,128)S(1)} collective-permute-done((f32[24,128]{1,0:T(8,128)S(1)}, f32[24,128]{1,0:T(8,128)S(1)}, u32[]{:S(2)}, u32[]{:S(2)}) %collective-permute-start.1) | collective-permute-done | bytes 12320 | tf_op jit(solution)/shard_map/ppermute | solution.py:411
  41.5 4.6 %all-to-all-done.1.back_ref = f32[32,4,128]{2,1,0:T(4,128)S(1)} async-done(((f32[32,4,128]{2,1,0:T(4,128)}), f32[32,4,128]{2,1,0:T(4,128)S(1)}, u32[]{:S(2)}, u32[]{:S(2)}) %all-to-all-start.1) | async-done | bytes 65568 | tf_op jit(solution)/shard_map/all_to_all | solution.py:408
  46.1 1.6 %shard_map.126 = (f32[24,128]{1,0:T(8,128)S(1)}, f32[16,128]{1,0:T(8,128)S(1)}, f32[16,128]{1,0:T(8,128)S(1)}, f32[32,2,128]{2,1,0:T(2,128)}, f32[2,32,128]{2,1,0:T(8,128)S(1)}) custom-call(f32[16,128]{1,0:T(8,128)S(1)} %get-tuple-element.54.refs_1_.refs_7_.v0_ref, f32[16,128]{1,0:T(8,128)S(1)} %get-tuple-element.59.local_ref, ...), custom_call_target="tpu_custom_call" | custom-call | bytes 4194304 | tf_op jit(solution)/shard_map/pallas_call | solution.py:44
  47.7 3.9 %all-to-all-start.2 = ((f32[32,2,128]{2,1,0:T(2,128)}), f32[32,2,128]{2,1,0:T(2,128)S(1)}, u32[]{:S(2)}, u32[]{:S(2)}) async-start(f32[32,2,128]{2,1,0:T(2,128)} %get-tuple-element.67), calls=%async_computation.2 | async-start | bytes 65536 | tf_op jit(solution)/shard_map/all_to_all | solution.py:408
  51.6 1.5 %collective-permute-start.2 = (f32[24,128]{1,0:T(8,128)S(1)}, f32[24,128]{1,0:T(8,128)S(1)}, u32[]{:S(2)}, u32[]{:S(2)}) collective-permute-start(f32[24,128]{1,0:T(8,128)S(1)} %get-tuple-element.68.half_ref), channel_id=1, source_target_pairs={{0,64},{32,96},{64,0},{96,32},{128,192},{160,224},{192,128},{224,1... | collective-permute-start | bytes 36872 | tf_op jit(solution)/shard_map/ppermute | solution.py:411
  53.0 2.7 %shard_map.127 = (f32[32,128]{1,0:T(8,128)S(1)}, f32[16,128,128]{2,1,0:T(8,128)S(1)}) custom-call(s32[3,2,16]{2,1,0:T(2,128)} %bitcast.37, f32[16,128]{1,0:T(8,128)S(1)} %get-tuple-element.65.refs_1_.v1_ref, f32[32,3,128,128]{3,2,1,0:T(8,128)} %bitcast.10, f32[16,128,128]{2,1,0:T(8,128)} %refs_3_.5), custom_call_target="tpu_custom_call" | custom-call | flops 2097152 | bytes 4194304 | tf_op jit(solution)/shard_map/pallas_call | solution.py:44
  56.2 2.7 %all-to-all-done.2.refs_3_ = f32[32,2,128]{2,1,0:T(2,128)S(1)} async-done(((f32[32,2,128]{2,1,0:T(2,128)}), f32[32,2,128]{2,1,0:T(2,128)S(1)}, u32[]{:S(2)}, u32[]{:S(2)}) %all-to-all-start.2) | async-done | bytes 32800 | tf_op jit(solution)/shard_map/all_to_all | solution.py:408
  58.9 3.6 %shard_map.129 = (f32[32,128]{1,0:T(8,128)S(1)}, f32[24,128]{1,0:T(8,128)S(1)}) custom-call(s32[3,2,16]{2,1,0:T(2,128)} %bitcast.38, s32[2,16]{1,0:T(2,128)} %refs_1_.5, f32[32,128]{1,0:T(8,128)S(1)} %get-tuple-element.66.refs_2_, f32[32,2,128]{2,1,0:T(2,128)S(1)} %all-to-all-done.2.refs_3_, f32[16,128]{1,0:T(8,128)S(1)} %get-tuple-element.70.refs_4_.q1_ref, ...), custom_call_target="tpu_custom_call" | custom-call | flops 3145728 | bytes 4194304 | tf_op jit(solution)/shard_map/pallas_call | solution.py:44
  62.6 3.9 %collective-permute-start.3 = (f32[24,128]{1,0:T(8,128)S(1)}, f32[24,128]{1,0:T(8,128)S(1)}, u32[]{:S(2)}, u32[]{:S(2)}) collective-permute-start(f32[24,128]{1,0:T(8,128)S(1)} %get-tuple-element.74.note_ref), channel_id=1, source_target_pairs={{0,128},{32,160},{64,192},{96,224},{128,0},{160,32},{192,64},{224,... | collective-permute-start | bytes 36872 | tf_op jit(solution)/shard_map/ppermute | solution.py:411
  66.5 3.4 %shard_map.130 = (f32[16,128]{1,0:T(8,128)S(1)}, f32[32,4,128]{2,1,0:T(4,128)}) custom-call(s32[3,2,16]{2,1,0:T(2,128)} %bitcast.39, f32[32,128]{1,0:T(8,128)S(1)} %get-tuple-element.71.refs_1_, f32[8,128]{1,0:T(8,128)S(1)} %get-tuple-element.72.refs_2_, f32[32,3,128,128]{3,2,1,0:T(8,128)S(1)} %bitcast.19), custom_call_target="tpu_custom_call" | custom-call | flops 3145728 | bytes 4194304 | tf_op jit(solution)/shard_map/pallas_call | solution.py:44
  69.9 5.8 %all-to-all-start.3 = ((f32[32,4,128]{2,1,0:T(4,128)}), f32[32,4,128]{2,1,0:T(4,128)S(1)}, u32[]{:S(2)}, u32[]{:S(2)}) async-start(f32[32,4,128]{2,1,0:T(4,128)} %get-tuple-element.76), calls=%async_computation.3 | async-start | bytes 131072 | tf_op jit(solution)/shard_map/all_to_all | solution.py:408
  76.6 2.0 %collective-permute-done.4.came_ref = f32[24,128]{1,0:T(8,128)S(1)} collective-permute-done((f32[24,128]{1,0:T(8,128)S(1)}, f32[24,128]{1,0:T(8,128)S(1)}, u32[]{:S(2)}, u32[]{:S(2)}) %collective-permute-start.4) | collective-permute-done | bytes 12320 | tf_op jit(solution)/shard_map/ppermute | solution.py:411
  78.6 4.5 %all-to-all-done.3.back_ref = f32[32,4,128]{2,1,0:T(4,128)S(1)} async-done(((f32[32,4,128]{2,1,0:T(4,128)}), f32[32,4,128]{2,1,0:T(4,128)S(1)}, u32[]{:S(2)}, u32[]{:S(2)}) %all-to-all-start.3) | async-done | bytes 65568 | tf_op jit(solution)/shard_map/all_to_all | solution.py:408
  83.1 1.2 shard_map.132
  84.3 3.9 %all-to-all-start.4 = ((f32[32,2,128]{2,1,0:T(2,128)}), f32[32,2,128]{2,1,0:T(2,128)S(1)}, u32[]{:S(2)}, u32[]{:S(2)}) async-start(f32[32,2,128]{2,1,0:T(2,128)} %get-tuple-element.85), calls=%async_computation.4 | async-start | bytes 65536 | tf_op jit(solution)/shard_map/all_to_all | solution.py:408
  88.2 1.3 %collective-permute-start.5 = (f32[24,128]{1,0:T(8,128)S(1)}, f32[24,128]{1,0:T(8,128)S(1)}, u32[]{:S(2)}, u32[]{:S(2)}) collective-permute-start(f32[24,128]{1,0:T(8,128)S(1)} %get-tuple-element.87.half_ref), channel_id=1, source_target_pairs={{0,64},{32,96},{64,0},{96,32},{128,192},{160,224},{192,128},{224,1... | collective-permute-start | bytes 36872 | tf_op jit(solution)/shard_map/ppermute | solution.py:411
  89.5 2.5 %shard_map.133 = (f32[32,128]{1,0:T(8,128)S(1)}, f32[16,128,128]{2,1,0:T(8,128)S(1)}) custom-call(s32[3,2,16]{2,1,0:T(2,128)} %bitcast.40, f32[16,128]{1,0:T(8,128)S(1)} %get-tuple-element.83.refs_1_.refs_10_.v2_ref, f32[32,3,128,128]{3,2,1,0:T(8,128)} %bitcast.12, f32[16,128,128]{2,1,0:T(8,128)} %refs_3_.5), custom_call_target="tpu_custom_call" | custom-call | flops 2097152 | bytes 4194304 | tf_op jit(solution)/shard_map/pallas_call | solution.py:44
  92.5 3.0 %all-to-all-done.4.refs_3_ = f32[32,2,128]{2,1,0:T(2,128)S(1)} async-done(((f32[32,2,128]{2,1,0:T(2,128)}), f32[32,2,128]{2,1,0:T(2,128)S(1)}, u32[]{:S(2)}, u32[]{:S(2)}) %all-to-all-start.4) | async-done | bytes 32800 | tf_op jit(solution)/shard_map/all_to_all | solution.py:408
  95.6 4.2 %shard_map.135 = (f32[32,128]{1,0:T(8,128)S(1)}, f32[8,24,128]{2,1,0:T(8,128)}) custom-call(s32[3,2,16]{2,1,0:T(2,128)} %bitcast.41, s32[2,16]{1,0:T(2,128)} %refs_1_.5, f32[32,128]{1,0:T(8,128)S(1)} %get-tuple-element.84.refs_2_, f32[32,2,128]{2,1,0:T(2,128)S(1)} %all-to-all-done.4.refs_3_, f32[16,128]{1,0:T(8,128)S(1)} %get-tuple-element.89.refs_4_.q2_ref, ...), custom_call_target="tpu_custom_call" | custom-call | flops 3145728 | bytes 4194304 | tf_op jit(solution)/shard_map/pallas_call | solution.py:44
  99.8 5.1 %all-to-all-start.5 = ((f32[8,24,128]{2,1,0:T(8,128)}), f32[8,24,128]{2,1,0:T(8,128)S(1)}, u32[]{:S(2)}, u32[]{:S(2)}) async-start(f32[8,24,128]{2,1,0:T(8,128)} %get-tuple-element.93), calls=%async_computation.5 | async-start | bytes 196608 | tf_op jit(solution)/shard_map/all_to_all | solution.py:485
  104.9 2.8 %copy-done = f32[2,16,3,128,128]{4,3,2,1,0:T(8,128)S(1)} copy-done((f32[2,16,3,128,128]{4,3,2,1,0:T(8,128)S(1)}, f32[2,16,3,128,128]{4,3,2,1,0:T(8,128)}, u32[]{:S(2)}) %copy-start) | copy-done | bytes 6291480
  107.7 2.8 %shard_map.136 = (f32[16,128]{1,0:T(8,128)S(1)}, f32[32,4,128]{2,1,0:T(4,128)S(1)}) custom-call(s32[3,2,16]{2,1,0:T(2,128)} %bitcast.42, f32[32,128]{1,0:T(8,128)S(1)} %get-tuple-element.90.refs_1_, f32[8,128]{1,0:T(8,128)S(1)} %get-tuple-element.91.refs_2_.sums_ref, f32[32,3,128,128]{3,2,1,0:T(8,128)S(1)} %bitcast.20), custom_call_target="tpu_custom_call" | custom-call | flops 3145728 | bytes 4194304 | tf_op jit(solution)/shard_map/pallas_call | solution.py:44
  110.5 1.9 %all-to-all-done.5.notes_ref = f32[8,24,128]{2,1,0:T(8,128)S(1)} async-done(((f32[8,24,128]{2,1,0:T(8,128)}), f32[8,24,128]{2,1,0:T(8,128)S(1)}, u32[]{:S(2)}, u32[]{:S(2)}) %all-to-all-start.5) | async-done | bytes 98336 | tf_op jit(solution)/shard_map/all_to_all | solution.py:485
  112.5 14.0 %all_to_all.35.back_ref = f32[32,4,128]{2,1,0:T(4,128)S(1)} all-to-all(f32[32,4,128]{2,1,0:T(4,128)S(1)} %get-tuple-element.95), channel_id=1, replica_groups=mesh['comm'=8,'stn'=16,'tm'=2] {'stn','tm'}, dimensions={0} | all-to-all | bytes 131072 | tf_op jit(solution)/shard_map/all_to_all | solution.py:408
  (32 shorter events, 4.0 us)
Async XLA Ops:
  0.6 19.9 %copy-start.3 = (f32[2,8,128]{2,1,0:T(8,128)S(1)}, f32[2,8,128]{2,1,0:T(8,128)}, u32[]{:S(2)}) copy-start(f32[2,8,128]{2,1,0:T(8,128)} %param.14) | copy-start | bytes 24580
  0.6 13.7 %copy-start.4 = (f32[16,128]{1,0:T(8,128)S(1)}, f32[16,128]{1,0:T(8,128)}, u32[]{:S(2)}) copy-start(f32[16,128]{1,0:T(8,128)} %cap_rhs_ref.5) | copy-start | bytes 24580
  0.7 19.9 %copy-start.2 = (f32[2,16,128]{2,1,0:T(8,128)S(1)}, f32[2,16,128]{2,1,0:T(8,128)}, u32[]{:S(2)}) copy-start(f32[2,16,128]{2,1,0:T(8,128)} %param.13) | copy-start | bytes 49156
  3.0 17.5 %all-to-all-start = ((f32[32,16,128]{2,1,0:T(8,128)}), f32[32,16,128]{2,1,0:T(8,128)S(1)}, u32[]{:S(2)}, u32[]{:S(2)}) async-start(f32[32,16,128]{2,1,0:T(8,128)} %get-tuple-element.56), calls=%async_computation | async-start | bytes 524288 | tf_op jit(solution)/shard_map/all_to_all | solution.py:408
  11.6 19.6 %slice-start = ((s8[6291456]{0:T(1024)(128)(4,1)}), s8[2097152]{0:T(1024)(128)(4,1)S(1)}, s32[]{:S(2)}) async-start(s8[6291456]{0:T(1024)(128)(4,1)} %bitcast.14), calls=%async_computation.7 | async-start | bytes 4194304
  20.5 10.7 %slice-start.1 = ((s8[6291456]{0:T(1024)(128)(4,1)}), s8[4194304]{0:T(1024)(128)(4,1)S(1)}, s32[]{:S(2)}) async-start(s8[6291456]{0:T(1024)(128)(4,1)} %bitcast.14), calls=%async_computation.8 | async-start | bytes 8388608
  20.5 25.6 %copy-start.1 = (f32[2,8,128,128]{3,2,1,0:T(8,128)S(1)}, f32[2,8,128,128]{3,2,1,0:T(8,128)}, u32[]{:S(2)}) copy-start(f32[2,8,128,128]{3,2,1,0:T(8,128)} %param.16) | copy-start | bytes 3145732
  24.2 10.4 %collective-permute-start = (f32[24,128]{1,0:T(8,128)S(1)}, f32[24,128]{1,0:T(8,128)S(1)}, u32[]{:S(2)}, u32[]{:S(2)}) collective-permute-start(f32[24,128]{1,0:T(8,128)S(1)} %get-tuple-element.60.note_ref), channel_id=1, source_target_pairs={{0,128},{32,160},{64,192},{96,224},{128,0},{160,32},{192,64},{224,... | collective-permute-start | bytes 36872 | tf_op jit(solution)/shard_map/ppermute | solution.py:411
  34.6 11.5 %all-to-all-start.1 = ((f32[32,4,128]{2,1,0:T(4,128)}), f32[32,4,128]{2,1,0:T(4,128)S(1)}, u32[]{:S(2)}, u32[]{:S(2)}) async-start(f32[32,4,128]{2,1,0:T(4,128)} %get-tuple-element.62), calls=%async_computation.1 | async-start | bytes 131072 | tf_op jit(solution)/shard_map/all_to_all | solution.py:408
  38.7 2.8 %collective-permute-start.1 = (f32[24,128]{1,0:T(8,128)S(1)}, f32[24,128]{1,0:T(8,128)S(1)}, u32[]{:S(2)}, u32[]{:S(2)}) collective-permute-start(f32[24,128]{1,0:T(8,128)S(1)} %get-tuple-element.63.note_ref), channel_id=1, source_target_pairs={{0,32},{32,0},{64,96},{96,64},{128,160},{160,128},{192,224},{224,1... | collective-permute-start | bytes 36872 | tf_op jit(solution)/shard_map/ppermute | solution.py:411
  47.7 11.3 %all-to-all-start.2 = ((f32[32,2,128]{2,1,0:T(2,128)}), f32[32,2,128]{2,1,0:T(2,128)S(1)}, u32[]{:S(2)}, u32[]{:S(2)}) async-start(f32[32,2,128]{2,1,0:T(2,128)} %get-tuple-element.67), calls=%async_computation.2 | async-start | bytes 65536 | tf_op jit(solution)/shard_map/all_to_all | solution.py:408
  51.6 4.2 %collective-permute-start.2 = (f32[24,128]{1,0:T(8,128)S(1)}, f32[24,128]{1,0:T(8,128)S(1)}, u32[]{:S(2)}, u32[]{:S(2)}) collective-permute-start(f32[24,128]{1,0:T(8,128)S(1)} %get-tuple-element.68.half_ref), channel_id=1, source_target_pairs={{0,64},{32,96},{64,0},{96,32},{128,192},{160,224},{192,128},{224,1... | collective-permute-start | bytes 36872 | tf_op jit(solution)/shard_map/ppermute | solution.py:411
  53.0 13.5 %slice-start.2 = ((s8[6291456]{0:T(1024)(128)(4,1)}), s8[2097152]{0:T(1024)(128)(4,1)S(1)}, s32[]{:S(2)}) async-start(s8[6291456]{0:T(1024)(128)(4,1)} %bitcast.17), calls=%async_computation.9 | async-start | bytes 4194304
  58.9 7.6 %slice-start.3 = ((s8[6291456]{0:T(1024)(128)(4,1)}), s8[4194304]{0:T(1024)(128)(4,1)S(1)}, s32[]{:S(2)}) async-start(s8[6291456]{0:T(1024)(128)(4,1)} %bitcast.17), calls=%async_computation.10 | async-start | bytes 8388608
  62.6 7.4 %collective-permute-start.3 = (f32[24,128]{1,0:T(8,128)S(1)}, f32[24,128]{1,0:T(8,128)S(1)}, u32[]{:S(2)}, u32[]{:S(2)}) collective-permute-start(f32[24,128]{1,0:T(8,128)S(1)} %get-tuple-element.74.note_ref), channel_id=1, source_target_pairs={{0,128},{32,160},{64,192},{96,224},{128,0},{160,32},{192,64},{224,... | collective-permute-start | bytes 36872 | tf_op jit(solution)/shard_map/ppermute | solution.py:411
  69.9 13.1 %all-to-all-start.3 = ((f32[32,4,128]{2,1,0:T(4,128)}), f32[32,4,128]{2,1,0:T(4,128)S(1)}, u32[]{:S(2)}, u32[]{:S(2)}) async-start(f32[32,4,128]{2,1,0:T(4,128)} %get-tuple-element.76), calls=%async_computation.3 | async-start | bytes 131072 | tf_op jit(solution)/shard_map/all_to_all | solution.py:408
  75.8 2.8 %collective-permute-start.4 = (f32[24,128]{1,0:T(8,128)S(1)}, f32[24,128]{1,0:T(8,128)S(1)}, u32[]{:S(2)}, u32[]{:S(2)}) collective-permute-start(f32[24,128]{1,0:T(8,128)S(1)} %get-tuple-element.77.note_ref), channel_id=1, source_target_pairs={{0,32},{32,0},{64,96},{96,64},{128,160},{160,128},{192,224},{224,1... | collective-permute-start | bytes 36872 | tf_op jit(solution)/shard_map/ppermute | solution.py:411
  84.3 11.2 %all-to-all-start.4 = ((f32[32,2,128]{2,1,0:T(2,128)}), f32[32,2,128]{2,1,0:T(2,128)S(1)}, u32[]{:S(2)}, u32[]{:S(2)}) async-start(f32[32,2,128]{2,1,0:T(2,128)} %get-tuple-element.85), calls=%async_computation.4 | async-start | bytes 65536 | tf_op jit(solution)/shard_map/all_to_all | solution.py:408
  88.2 3.8 %collective-permute-start.5 = (f32[24,128]{1,0:T(8,128)S(1)}, f32[24,128]{1,0:T(8,128)S(1)}, u32[]{:S(2)}, u32[]{:S(2)}) collective-permute-start(f32[24,128]{1,0:T(8,128)S(1)} %get-tuple-element.87.half_ref), channel_id=1, source_target_pairs={{0,64},{32,96},{64,0},{96,32},{128,192},{160,224},{192,128},{224,1... | collective-permute-start | bytes 36872 | tf_op jit(solution)/shard_map/ppermute | solution.py:411
  99.8 12.6 %all-to-all-start.5 = ((f32[8,24,128]{2,1,0:T(8,128)}), f32[8,24,128]{2,1,0:T(8,128)S(1)}, u32[]{:S(2)}, u32[]{:S(2)}) async-start(f32[8,24,128]{2,1,0:T(8,128)} %get-tuple-element.93), calls=%async_computation.5 | async-start | bytes 196608 | tf_op jit(solution)/shard_map/all_to_all | solution.py:485
  104.9 2.8 %copy-start = (f32[2,16,3,128,128]{4,3,2,1,0:T(8,128)S(1)}, f32[2,16,3,128,128]{4,3,2,1,0:T(8,128)}, u32[]{:S(2)}) copy-start(f32[2,16,3,128,128]{4,3,2,1,0:T(8,128)} %param.9) | copy-start | bytes 18874372

commit v7 on v6

--- a/solution.py
+++ b/solution.py
@@ -315,9 +315,7 @@
         send_ref[:, c] = row
 
 
-def rows_second_kernel(comms, v0_ref, local_ref, back_ref, note_ref, came_ref, precond_ref, half_ref, y_ref,
-                       v_ref, send_ref, asked_ref):
-    half_ref[...] = note_ref[...] + came_ref[...]
+def rows_second_kernel(comms, v0_ref, local_ref, back_ref, precond_ref, y_ref, v_ref, send_ref, asked_ref):
     asked = [back_ref[:, comms + c] for c in range(comms)]
     for c in range(comms):
         asked_ref[c] = asked[c]
@@ -326,9 +324,8 @@
     pack(comms, v_ref, asked, send_ref)
 
 
-def rows_third_kernel(comms, rhs_ref, v0_ref, y0_ref, v1_ref, local_ref, back_ref, note_ref, came_ref, asked_ref,
-                      precond_ref, half_ref, alpha_ref, z_ref, yz_ref, r_ref, v_ref, send_ref):
-    half_ref[...] = note_ref[...] + came_ref[...]
+def rows_third_kernel(comms, rhs_ref, v0_ref, y0_ref, v1_ref, local_ref, back_ref, asked_ref,
+                      precond_ref, alpha_ref, z_ref, yz_ref, r_ref, v_ref, send_ref):
     asked = [asked_ref[c] for c in range(comms)]
     collect(comms, v1_ref, local_ref, back_ref, asked, yz_ref)
     first = jnp.sum(fold(back_ref[:, comms]), axis=1, keepdims=True)
@@ -429,7 +426,7 @@
         )
 
     def add(note, other, back):
-        return call(add_kernel, [note_shape, back_shape], (note, other, back), aliases={2: 1}, still=(1,))
+        return call(add_kernel, [note_shape, back.shape], (note, other, back), aliases={2: 1}, still=(1,))
 
     v0, send = call(
         first_kernel, [row_shape, (groups, rows, width)], (rhs, precond), 0,
@@ -442,15 +439,17 @@
         functools.partial(up_first_kernel, comms, blocks, caps), [arc_shape, note_shape],
         (index, cap_index, up, got, q0, scale, rhs, v0, tiles, cap_tiles), 2, up_room, flops=3 * unit, hbm=(8, 9),
     )
-    other = across(note, 4)
+    other = across(note, 1)
     local, back = spread(0, scaled, rhs)
     note, back = add(note, other, back)
     back = exchange(back)
-    half, y0, v1, send, asked = call(
+    other = across(note, 4)
+    y0, v1, send, asked = call(
         functools.partial(rows_second_kernel, comms),
-        [note_shape, row_shape, row_shape, send_shape, (comms, groups, width)],
-        (v0, local, back, note, across(note, 1), kept(precond)),
-    )
+        [row_shape, row_shape, send_shape, (comms, groups, width)],
+        (v0, local, back, kept(precond)),
+    )
+    half, send = add(note, other, send)
     got = exchange(send)
     other = across(half, 2)
     up, pre = near(v1)
@@ -461,15 +460,17 @@
         functools.partial(up_second_kernel, comms, blocks), [arc_shape, note_shape],
         (index, cap_index, up, got, q1, scale, tiles, cap_tiles), 2, up_room, flops=3 * unit, hbm=(6, 7),
     )
-    other = across(note, 4)
+    other = across(note, 1)
     local, back = spread(1, scaled, sums)
     note, back = add(note, other, back)
     back = exchange(back)
-    half, alpha, z1, yz, r1, v2, send = call(
+    other = across(note, 4)
+    alpha, z1, yz, r1, v2, send = call(
         functools.partial(rows_third_kernel, comms),
-        [note_shape, small, row_shape, row_shape, row_shape, row_shape, send_shape],
-        (rhs, v0, y0, v1, local, back, note, across(note, 1), asked, kept(precond)),
-    )
+        [small, row_shape, row_shape, row_shape, row_shape, send_shape],
+        (rhs, v0, y0, v1, local, back, asked, kept(precond)),
+    )
+    half, send = add(note, other, send)
     got = exchange(send)
     other = across(half, 2)
     up, pre = near(v2)

time: 128 us -> 126 us (0.984)
  waiting for transfers between devices: 26.4 us -> 14.3 us
  starting transfers between devices: 46.7 us -> 57.3 us
    all_to_all x5, waiting for transfers between devices: 20.5 us -> 12.4 us  [exchange(): return lax.all_to_all(x, GROUP, 0, 0)]
    all_to_all x5, starting transfers between devices: 26.2 us -> 31.8 us  [exchange(): return lax.all_to_all(x, GROUP, 0, 0)]
    ppermute x6, waiting for transfers between devices: 3.97 us -> 0.02 us  [across(): return lax.ppermute(x, 'comm', [(i, i ^ step) for i in range(peers)])]
    ppermute x6, starting transfers between devices: 15.3 us -> 18.8 us  [across(): return lax.ppermute(x, 'comm', [(i, i ^ step) for i in range(peers)])]
    all_to_all x1, starting transfers between devices: 5.14 us -> 6.68 us  [body(): notes = lax.all_to_all(notes, 'comm', 0, 0)]
    pallas_call x19 -> x21, Pallas kernels: 36.5 us -> 36.5 us  [call(): pl.pallas_call(kernel, out_shape=outs, in_specs=[HBM if n in hbm else ANY...]
  transfers between devices with their start and end apart: 12 -> 12, of which waited for: 8 -> 6; matrix products, arithmetic and copies ran while one was open for 0% -> 0% of each run, Pallas kernels for 15% -> 17%
where the time goes in v7:
time: 126 us
  starting transfers between devices  57.3 us (45%)
  Pallas kernels  36.5 us (29%)
  waiting for transfers between devices  14.3 us (11%)
  blocking collectives  14 us (11%)
  local copies, waits for them, and re-layouts  2.81 us (2%)
    pallas_call x21, Pallas kernels, call(): pl.pallas_call(kernel, out_shape=outs, in_specs=[HBM if n in hbm else ANY...  36.5 us
    all_to_all x5, starting transfers between devices, exchange(): return lax.all_to_all(x, GROUP, 0, 0)  31.8 us
    ppermute x6, starting transfers between devices, across(): return lax.ppermute(x, 'comm', [(i, i ^ step) for i in range(peers)])  18.8 us
    all_to_all x1, blocking collectives, exchange(): return lax.all_to_all(x, GROUP, 0, 0)  14 us
    all_to_all x5, waiting for transfers between devices, exchange(): return lax.all_to_all(x, GROUP, 0, 0)  12.4 us
    all_to_all x1, starting transfers between devices, body(): notes = lax.all_to_all(notes, 'comm', 0, 0)  6.68 us
    unnamed x18, local copies, waits for them, and re-layouts  2.81 us
  transfers between devices with their start and end apart: 12, of which 6 were waited for; matrix products, arithmetic and copies ran while one was open for 0% of the time, Pallas kernels for 17%

profile of v7, /device:TPU:1, one launch (start us, length us, event | category | flops | bytes accessed | tf_op | source)
XLA Modules:
  0.0 125.7 jit_solution(17873001207959752489)
XLA Ops:
  0.7 2.3 %shard_map.120 = (f32[16,128]{1,0:T(8,128)S(1)}, f32[32,16,128]{2,1,0:T(8,128)}) custom-call(f32[16,128]{1,0:T(8,128)} %bitcast.27, f32[16,128,128]{2,1,0:T(8,128)} %bitcast.21), custom_call_target="tpu_custom_call" | custom-call | bytes 4194304 | tf_op jit(solution)/shard_map/pallas_call | solution.py:44
  3.0 8.6 %all-to-all-start = ((f32[32,16,128]{2,1,0:T(8,128)}), f32[32,16,128]{2,1,0:T(8,128)S(1)}, u32[]{:S(2)}, u32[]{:S(2)}) async-start(f32[32,16,128]{2,1,0:T(8,128)} %get-tuple-element.58), calls=%async_computation | async-start | bytes 524288 | tf_op jit(solution)/shard_map/all_to_all | solution.py:405
  11.6 2.7 %shard_map.121 = (f32[32,128]{1,0:T(8,128)S(1)}, f32[16,128,128]{2,1,0:T(8,128)S(1)}) custom-call(s32[3,2,16]{2,1,0:T(2,128)} %bitcast.34, f32[16,128]{1,0:T(8,128)S(1)} %get-tuple-element.56.refs_1_.refs_7_.v0_ref, f32[32,3,128,128]{3,2,1,0:T(8,128)} %bitcast.8, f32[16,128,128]{2,1,0:T(8,128)} %refs_3_.5), custom_call_target="tpu_custom_call" | custom-call | flops 2097152 | bytes 4194304 | tf_op jit(solution)/shard_map/pallas_call | solution.py:44
  14.8 5.7 %all-to-all-done.refs_3_ = f32[32,16,128]{2,1,0:T(8,128)S(1)} async-done(((f32[32,16,128]{2,1,0:T(8,128)}), f32[32,16,128]{2,1,0:T(8,128)S(1)}, u32[]{:S(2)}, u32[]{:S(2)}) %all-to-all-start) | async-done | bytes 262176 | tf_op jit(solution)/shard_map/all_to_all | solution.py:405
  20.5 3.6 %shard_map.123 = (f32[32,128]{1,0:T(8,128)S(1)}, f32[24,128]{1,0:T(8,128)S(1)}) custom-call(s32[3,2,16]{2,1,0:T(2,128)} %bitcast.35, s32[2,16]{1,0:T(2,128)} %refs_1_.5, f32[32,128]{1,0:T(8,128)S(1)} %get-tuple-element.57.refs_2_, f32[32,16,128]{2,1,0:T(8,128)S(1)} %all-to-all-done.refs_3_, f32[16,128]{1,0:T(8,128)S(1)} %shard_map.122.refs_4_.q0_ref, ...), custom_call_target="tpu_custom_call" | custom-call | flops 3145728 | bytes 4194304 | tf_op jit(solution)/shard_map/pallas_call | solution.py:44
  24.1 1.7 %collective-permute-start = (f32[24,128]{1,0:T(8,128)S(1)}, f32[24,128]{1,0:T(8,128)S(1)}, u32[]{:S(2)}, u32[]{:S(2)}) collective-permute-start(f32[24,128]{1,0:T(8,128)S(1)} %get-tuple-element.62.note_ref), channel_id=1, source_target_pairs={{0,32},{32,0},{64,96},{96,64},{128,160},{160,128},{192,224},{224,1... | collective-permute-start | bytes 36872 | tf_op jit(solution)/shard_map/ppermute | solution.py:408
  25.9 3.4 %shard_map.124 = (f32[16,128]{1,0:T(8,128)S(1)}, f32[32,4,128]{2,1,0:T(4,128)}) custom-call(s32[3,2,16]{2,1,0:T(2,128)} %bitcast.36, f32[32,128]{1,0:T(8,128)S(1)} %get-tuple-element.60.refs_1_, f32[16,128]{1,0:T(8,128)S(1)} %bitcast.29, f32[32,3,128,128]{3,2,1,0:T(8,128)S(1)} %bitcast.16), custom_call_target="tpu_custom_call" | custom-call | flops 3145728 | bytes 4194304 | tf_op jit(solution)/shard_map/pallas_call | solution.py:44
  29.3 4.0 %all-to-all-start.1 = ((f32[32,4,128]{2,1,0:T(4,128)}), f32[32,4,128]{2,1,0:T(4,128)S(1)}, u32[]{:S(2)}, u32[]{:S(2)}) async-start(f32[32,4,128]{2,1,0:T(4,128)} %get-tuple-element.64), calls=%async_computation.1 | async-start | bytes 131072 | tf_op jit(solution)/shard_map/all_to_all | solution.py:405
  33.4 6.1 %collective-permute-start.1 = (f32[24,128]{1,0:T(8,128)S(1)}, f32[24,128]{1,0:T(8,128)S(1)}, u32[]{:S(2)}, u32[]{:S(2)}) collective-permute-start(f32[24,128]{1,0:T(8,128)S(1)} %get-tuple-element.68.note_ref), channel_id=1, source_target_pairs={{0,128},{32,160},{64,192},{96,224},{128,0},{160,32},{192,64},{224,... | collective-permute-start | bytes 36872 | tf_op jit(solution)/shard_map/ppermute | solution.py:408
  39.5 1.3 %all-to-all-done.1.back_ref = f32[32,4,128]{2,1,0:T(4,128)S(1)} async-done(((f32[32,4,128]{2,1,0:T(4,128)}), f32[32,4,128]{2,1,0:T(4,128)S(1)}, u32[]{:S(2)}, u32[]{:S(2)}) %all-to-all-start.1) | async-done | bytes 65568 | tf_op jit(solution)/shard_map/all_to_all | solution.py:405
  40.8 1.6 %shard_map.126 = (f32[16,128]{1,0:T(8,128)S(1)}, f32[16,128]{1,0:T(8,128)S(1)}, f32[32,2,128]{2,1,0:T(2,128)}, f32[2,32,128]{2,1,0:T(8,128)S(1)}) custom-call(f32[16,128]{1,0:T(8,128)S(1)} %get-tuple-element.56.refs_1_.refs_7_.v0_ref, f32[16,128]{1,0:T(8,128)S(1)} %get-tuple-element.61.local_ref, f32[32,4,128]{2,1,0:T(4,128)S(1)} %all-to-all-done.1.back_ref, ...), custom_call_target="tpu_custom_call" | custom-call | bytes 4194304 | tf_op jit(solution)/shard_map/pallas_call | solution.py:44
  42.4 6.5 %all-to-all-start.2 = ((f32[32,2,128]{2,1,0:T(2,128)}), f32[32,2,128]{2,1,0:T(2,128)S(1)}, u32[]{:S(2)}, u32[]{:S(2)}) async-start(f32[32,2,128]{2,1,0:T(2,128)} %get-tuple-element.70), calls=%async_computation.2 | async-start | bytes 65536 | tf_op jit(solution)/shard_map/all_to_all | solution.py:405
  48.9 2.9 %collective-permute-start.2 = (f32[24,128]{1,0:T(8,128)S(1)}, f32[24,128]{1,0:T(8,128)S(1)}, u32[]{:S(2)}, u32[]{:S(2)}) collective-permute-start(f32[24,128]{1,0:T(8,128)S(1)} %get-tuple-element.71.half_ref), channel_id=1, source_target_pairs={{0,64},{32,96},{64,0},{96,32},{128,192},{160,224},{192,128},{224,1... | collective-permute-start | bytes 36872 | tf_op jit(solution)/shard_map/ppermute | solution.py:408
  51.8 2.7 %shard_map.127 = (f32[32,128]{1,0:T(8,128)S(1)}, f32[16,128,128]{2,1,0:T(8,128)S(1)}) custom-call(s32[3,2,16]{2,1,0:T(2,128)} %bitcast.37, f32[16,128]{1,0:T(8,128)S(1)} %get-tuple-element.66.refs_1_.v1_ref, f32[32,3,128,128]{3,2,1,0:T(8,128)} %bitcast.10, f32[16,128,128]{2,1,0:T(8,128)} %refs_3_.5), custom_call_target="tpu_custom_call" | custom-call | flops 2097152 | bytes 4194304 | tf_op jit(solution)/shard_map/pallas_call | solution.py:44
  55.0 1.1 all-to-all-done.2.refs_3_
  56.2 3.6 %shard_map.130 = (f32[32,128]{1,0:T(8,128)S(1)}, f32[24,128]{1,0:T(8,128)S(1)}) custom-call(s32[3,2,16]{2,1,0:T(2,128)} %bitcast.38, s32[2,16]{1,0:T(2,128)} %refs_1_.5, f32[32,128]{1,0:T(8,128)S(1)} %get-tuple-element.67.refs_2_, f32[32,2,128]{2,1,0:T(2,128)S(1)} %all-to-all-done.2.refs_3_, f32[16,128]{1,0:T(8,128)S(1)} %get-tuple-element.73.refs_4_.q1_ref, ...), custom_call_target="tpu_custom_call" | custom-call | flops 3145728 | bytes 4194304 | tf_op jit(solution)/shard_map/pallas_call | solution.py:44
  59.8 0.8 collective-permute-start.3
  60.6 3.4 %shard_map.131 = (f32[16,128]{1,0:T(8,128)S(1)}, f32[32,4,128]{2,1,0:T(4,128)}) custom-call(s32[3,2,16]{2,1,0:T(2,128)} %bitcast.39, f32[32,128]{1,0:T(8,128)S(1)} %get-tuple-element.74.refs_1_, f32[8,128]{1,0:T(8,128)S(1)} %get-tuple-element.75.refs_2_, f32[32,3,128,128]{3,2,1,0:T(8,128)S(1)} %bitcast.19), custom_call_target="tpu_custom_call" | custom-call | flops 3145728 | bytes 4194304 | tf_op jit(solution)/shard_map/pallas_call | solution.py:44
  64.1 6.1 %all-to-all-start.3 = ((f32[32,4,128]{2,1,0:T(4,128)}), f32[32,4,128]{2,1,0:T(4,128)S(1)}, u32[]{:S(2)}, u32[]{:S(2)}) async-start(f32[32,4,128]{2,1,0:T(4,128)} %get-tuple-element.79), calls=%async_computation.3 | async-start | bytes 131072 | tf_op jit(solution)/shard_map/all_to_all | solution.py:405
  70.1 5.5 %collective-permute-start.4 = (f32[24,128]{1,0:T(8,128)S(1)}, f32[24,128]{1,0:T(8,128)S(1)}, u32[]{:S(2)}, u32[]{:S(2)}) collective-permute-start(f32[24,128]{1,0:T(8,128)S(1)} %get-tuple-element.87.note_ref), channel_id=1, source_target_pairs={{0,128},{32,160},{64,192},{96,224},{128,0},{160,32},{192,64},{224,... | collective-permute-start | bytes 36872 | tf_op jit(solution)/shard_map/ppermute | solution.py:408
  75.6 1.8 %all-to-all-done.3.back_ref = f32[32,4,128]{2,1,0:T(4,128)S(1)} async-done(((f32[32,4,128]{2,1,0:T(4,128)}), f32[32,4,128]{2,1,0:T(4,128)S(1)}, u32[]{:S(2)}, u32[]{:S(2)}) %all-to-all-start.3) | async-done | bytes 65568 | tf_op jit(solution)/shard_map/all_to_all | solution.py:405
  77.5 1.2 shard_map.133
  78.7 6.5 %all-to-all-start.4 = ((f32[32,2,128]{2,1,0:T(2,128)}), f32[32,2,128]{2,1,0:T(2,128)S(1)}, u32[]{:S(2)}, u32[]{:S(2)}) async-start(f32[32,2,128]{2,1,0:T(2,128)} %get-tuple-element.89), calls=%async_computation.4 | async-start | bytes 65536 | tf_op jit(solution)/shard_map/all_to_all | solution.py:405
  85.2 1.8 %collective-permute-start.5 = (f32[24,128]{1,0:T(8,128)S(1)}, f32[24,128]{1,0:T(8,128)S(1)}, u32[]{:S(2)}, u32[]{:S(2)}) collective-permute-start(f32[24,128]{1,0:T(8,128)S(1)} %get-tuple-element.91.half_ref), channel_id=1, source_target_pairs={{0,64},{32,96},{64,0},{96,32},{128,192},{160,224},{192,128},{224,1... | collective-permute-start | bytes 36872 | tf_op jit(solution)/shard_map/ppermute | solution.py:408
  87.0 2.5 %shard_map.134 = (f32[32,128]{1,0:T(8,128)S(1)}, f32[16,128,128]{2,1,0:T(8,128)S(1)}) custom-call(s32[3,2,16]{2,1,0:T(2,128)} %bitcast.40, f32[16,128]{1,0:T(8,128)S(1)} %get-tuple-element.85.refs_1_.refs_10_.v2_ref, f32[32,3,128,128]{3,2,1,0:T(8,128)} %bitcast.12, f32[16,128,128]{2,1,0:T(8,128)} %refs_3_.5), custom_call_target="tpu_custom_call" | custom-call | flops 2097152 | bytes 4194304 | tf_op jit(solution)/shard_map/pallas_call | solution.py:44
  90.1 2.4 %all-to-all-done.4.refs_3_ = f32[32,2,128]{2,1,0:T(2,128)S(1)} async-done(((f32[32,2,128]{2,1,0:T(2,128)}), f32[32,2,128]{2,1,0:T(2,128)S(1)}, u32[]{:S(2)}, u32[]{:S(2)}) %all-to-all-start.4) | async-done | bytes 32800 | tf_op jit(solution)/shard_map/all_to_all | solution.py:405
  92.5 4.2 %shard_map.137 = (f32[32,128]{1,0:T(8,128)S(1)}, f32[8,24,128]{2,1,0:T(8,128)}) custom-call(s32[3,2,16]{2,1,0:T(2,128)} %bitcast.41, s32[2,16]{1,0:T(2,128)} %refs_1_.5, f32[32,128]{1,0:T(8,128)S(1)} %get-tuple-element.86.refs_2_, f32[32,2,128]{2,1,0:T(2,128)S(1)} %all-to-all-done.4.refs_3_, f32[16,128]{1,0:T(8,128)S(1)} %get-tuple-element.93.refs_4_.q2_ref, ...), custom_call_target="tpu_custom_call" | custom-call | flops 3145728 | bytes 4194304 | tf_op jit(solution)/shard_map/pallas_call | solution.py:44
  96.7 6.7 %all-to-all-start.5 = ((f32[8,24,128]{2,1,0:T(8,128)}), f32[8,24,128]{2,1,0:T(8,128)S(1)}, u32[]{:S(2)}, u32[]{:S(2)}) async-start(f32[8,24,128]{2,1,0:T(8,128)} %get-tuple-element.97), calls=%async_computation.5 | async-start | bytes 196608 | tf_op jit(solution)/shard_map/all_to_all | solution.py:486
  103.4 2.8 %copy-done = f32[2,16,3,128,128]{4,3,2,1,0:T(8,128)S(1)} copy-done((f32[2,16,3,128,128]{4,3,2,1,0:T(8,128)S(1)}, f32[2,16,3,128,128]{4,3,2,1,0:T(8,128)}, u32[]{:S(2)}) %copy-start) | copy-done | bytes 6291480
  106.2 2.8 %shard_map.138 = (f32[16,128]{1,0:T(8,128)S(1)}, f32[32,4,128]{2,1,0:T(4,128)S(1)}) custom-call(s32[3,2,16]{2,1,0:T(2,128)} %bitcast.42, f32[32,128]{1,0:T(8,128)S(1)} %get-tuple-element.94.refs_1_, f32[8,128]{1,0:T(8,128)S(1)} %get-tuple-element.95.refs_2_.sums_ref, f32[32,3,128,128]{3,2,1,0:T(8,128)S(1)} %bitcast.20), custom_call_target="tpu_custom_call" | custom-call | flops 3145728 | bytes 4194304 | tf_op jit(solution)/shard_map/pallas_call | solution.py:44
  109.0 1.9 %all-to-all-done.5.notes_ref = f32[8,24,128]{2,1,0:T(8,128)S(1)} async-done(((f32[8,24,128]{2,1,0:T(8,128)}), f32[8,24,128]{2,1,0:T(8,128)S(1)}, u32[]{:S(2)}, u32[]{:S(2)}) %all-to-all-start.5) | async-done | bytes 98336 | tf_op jit(solution)/shard_map/all_to_all | solution.py:486
  111.0 14.0 %all_to_all.35.back_ref = f32[32,4,128]{2,1,0:T(4,128)S(1)} all-to-all(f32[32,4,128]{2,1,0:T(4,128)S(1)} %get-tuple-element.99), channel_id=1, replica_groups=mesh['comm'=8,'stn'=16,'tm'=2] {'stn','tm'}, dimensions={0} | all-to-all | bytes 131072 | tf_op jit(solution)/shard_map/all_to_all | solution.py:405
  (34 shorter events, 2.4 us)
Async XLA Ops:
  0.6 19.9 %copy-start.3 = (f32[2,8,128]{2,1,0:T(8,128)S(1)}, f32[2,8,128]{2,1,0:T(8,128)}, u32[]{:S(2)}) copy-start(f32[2,8,128]{2,1,0:T(8,128)} %param.14) | copy-start | bytes 24580
  0.6 13.7 %copy-start.4 = (f32[16,128]{1,0:T(8,128)S(1)}, f32[16,128]{1,0:T(8,128)}, u32[]{:S(2)}) copy-start(f32[16,128]{1,0:T(8,128)} %cap_rhs_ref.5) | copy-start | bytes 24580
  0.7 19.8 %copy-start.2 = (f32[2,16,128]{2,1,0:T(8,128)S(1)}, f32[2,16,128]{2,1,0:T(8,128)}, u32[]{:S(2)}) copy-start(f32[2,16,128]{2,1,0:T(8,128)} %param.13) | copy-start | bytes 49156
  3.0 17.5 %all-to-all-start = ((f32[32,16,128]{2,1,0:T(8,128)}), f32[32,16,128]{2,1,0:T(8,128)S(1)}, u32[]{:S(2)}, u32[]{:S(2)}) async-start(f32[32,16,128]{2,1,0:T(8,128)} %get-tuple-element.58), calls=%async_computation | async-start | bytes 524288 | tf_op jit(solution)/shard_map/all_to_all | solution.py:405
  11.6 14.3 %slice-start = ((s8[6291456]{0:T(1024)(128)(4,1)}), s8[2097152]{0:T(1024)(128)(4,1)S(1)}, s32[]{:S(2)}) async-start(s8[6291456]{0:T(1024)(128)(4,1)} %bitcast.14), calls=%async_computation.7 | async-start | bytes 4194304
  20.5 5.4 %slice-start.1 = ((s8[6291456]{0:T(1024)(128)(4,1)}), s8[4194304]{0:T(1024)(128)(4,1)S(1)}, s32[]{:S(2)}) async-start(s8[6291456]{0:T(1024)(128)(4,1)} %bitcast.14), calls=%async_computation.8 | async-start | bytes 8388608
  20.5 20.3 %copy-start.1 = (f32[2,8,128,128]{3,2,1,0:T(8,128)S(1)}, f32[2,8,128,128]{3,2,1,0:T(8,128)}, u32[]{:S(2)}) copy-start(f32[2,8,128,128]{3,2,1,0:T(8,128)} %param.16) | copy-start | bytes 3145732
  24.1 5.2 %collective-permute-start = (f32[24,128]{1,0:T(8,128)S(1)}, f32[24,128]{1,0:T(8,128)S(1)}, u32[]{:S(2)}, u32[]{:S(2)}) collective-permute-start(f32[24,128]{1,0:T(8,128)S(1)} %get-tuple-element.62.note_ref), channel_id=1, source_target_pairs={{0,32},{32,0},{64,96},{96,64},{128,160},{160,128},{192,224},{224,1... | collective-permute-start | bytes 36872 | tf_op jit(solution)/shard_map/ppermute | solution.py:408
  29.3 11.5 %all-to-all-start.1 = ((f32[32,4,128]{2,1,0:T(4,128)}), f32[32,4,128]{2,1,0:T(4,128)S(1)}, u32[]{:S(2)}, u32[]{:S(2)}) async-start(f32[32,4,128]{2,1,0:T(4,128)} %get-tuple-element.64), calls=%async_computation.1 | async-start | bytes 131072 | tf_op jit(solution)/shard_map/all_to_all | solution.py:405
  33.4 9.0 %collective-permute-start.1 = (f32[24,128]{1,0:T(8,128)S(1)}, f32[24,128]{1,0:T(8,128)S(1)}, u32[]{:S(2)}, u32[]{:S(2)}) collective-permute-start(f32[24,128]{1,0:T(8,128)S(1)} %get-tuple-element.68.note_ref), channel_id=1, source_target_pairs={{0,128},{32,160},{64,192},{96,224},{128,0},{160,32},{192,64},{224,... | collective-permute-start | bytes 36872 | tf_op jit(solution)/shard_map/ppermute | solution.py:408
  42.4 13.8 %all-to-all-start.2 = ((f32[32,2,128]{2,1,0:T(2,128)}), f32[32,2,128]{2,1,0:T(2,128)S(1)}, u32[]{:S(2)}, u32[]{:S(2)}) async-start(f32[32,2,128]{2,1,0:T(2,128)} %get-tuple-element.70), calls=%async_computation.2 | async-start | bytes 65536 | tf_op jit(solution)/shard_map/all_to_all | solution.py:405
  48.9 5.6 %collective-permute-start.2 = (f32[24,128]{1,0:T(8,128)S(1)}, f32[24,128]{1,0:T(8,128)S(1)}, u32[]{:S(2)}, u32[]{:S(2)}) collective-permute-start(f32[24,128]{1,0:T(8,128)S(1)} %get-tuple-element.71.half_ref), channel_id=1, source_target_pairs={{0,64},{32,96},{64,0},{96,32},{128,192},{160,224},{192,128},{224,1... | collective-permute-start | bytes 36872 | tf_op jit(solution)/shard_map/ppermute | solution.py:408
  51.8 8.8 %slice-start.2 = ((s8[6291456]{0:T(1024)(128)(4,1)}), s8[2097152]{0:T(1024)(128)(4,1)S(1)}, s32[]{:S(2)}) async-start(s8[6291456]{0:T(1024)(128)(4,1)} %bitcast.17), calls=%async_computation.9 | async-start | bytes 4194304
  56.2 4.5 %slice-start.3 = ((s8[6291456]{0:T(1024)(128)(4,1)}), s8[4194304]{0:T(1024)(128)(4,1)S(1)}, s32[]{:S(2)}) async-start(s8[6291456]{0:T(1024)(128)(4,1)} %bitcast.17), calls=%async_computation.10 | async-start | bytes 8388608
  59.8 4.2 %collective-permute-start.3 = (f32[24,128]{1,0:T(8,128)S(1)}, f32[24,128]{1,0:T(8,128)S(1)}, u32[]{:S(2)}, u32[]{:S(2)}) collective-permute-start(f32[24,128]{1,0:T(8,128)S(1)} %get-tuple-element.77.note_ref), channel_id=1, source_target_pairs={{0,32},{32,0},{64,96},{96,64},{128,160},{160,128},{192,224},{224,1... | collective-permute-start | bytes 36872 | tf_op jit(solution)/shard_map/ppermute | solution.py:408
  64.1 13.4 %all-to-all-start.3 = ((f32[32,4,128]{2,1,0:T(4,128)}), f32[32,4,128]{2,1,0:T(4,128)S(1)}, u32[]{:S(2)}, u32[]{:S(2)}) async-start(f32[32,4,128]{2,1,0:T(4,128)} %get-tuple-element.79), calls=%async_computation.3 | async-start | bytes 131072 | tf_op jit(solution)/shard_map/all_to_all | solution.py:405
  70.1 8.5 %collective-permute-start.4 = (f32[24,128]{1,0:T(8,128)S(1)}, f32[24,128]{1,0:T(8,128)S(1)}, u32[]{:S(2)}, u32[]{:S(2)}) collective-permute-start(f32[24,128]{1,0:T(8,128)S(1)} %get-tuple-element.87.note_ref), channel_id=1, source_target_pairs={{0,128},{32,160},{64,192},{96,224},{128,0},{160,32},{192,64},{224,... | collective-permute-start | bytes 36872 | tf_op jit(solution)/shard_map/ppermute | solution.py:408
  78.7 13.8 %all-to-all-start.4 = ((f32[32,2,128]{2,1,0:T(2,128)}), f32[32,2,128]{2,1,0:T(2,128)S(1)}, u32[]{:S(2)}, u32[]{:S(2)}) async-start(f32[32,2,128]{2,1,0:T(2,128)} %get-tuple-element.89), calls=%async_computation.4 | async-start | bytes 65536 | tf_op jit(solution)/shard_map/all_to_all | solution.py:405
  85.2 4.3 %collective-permute-start.5 = (f32[24,128]{1,0:T(8,128)S(1)}, f32[24,128]{1,0:T(8,128)S(1)}, u32[]{:S(2)}, u32[]{:S(2)}) collective-permute-start(f32[24,128]{1,0:T(8,128)S(1)} %get-tuple-element.91.half_ref), channel_id=1, source_target_pairs={{0,64},{32,96},{64,0},{96,32},{128,192},{160,224},{192,128},{224,1... | collective-permute-start | bytes 36872 | tf_op jit(solution)/shard_map/ppermute | solution.py:408
  96.7 14.1 %all-to-all-start.5 = ((f32[8,24,128]{2,1,0:T(8,128)}), f32[8,24,128]{2,1,0:T(8,128)S(1)}, u32[]{:S(2)}, u32[]{:S(2)}) async-start(f32[8,24,128]{2,1,0:T(8,128)} %get-tuple-element.97), calls=%async_computation.5 | async-start | bytes 196608 | tf_op jit(solution)/shard_map/all_to_all | solution.py:486
  103.4 2.8 %copy-start = (f32[2,16,3,128,128]{4,3,2,1,0:T(8,128)S(1)}, f32[2,16,3,128,128]{4,3,2,1,0:T(8,128)}, u32[]{:S(2)}) copy-start(f32[2,16,3,128,128]{4,3,2,1,0:T(8,128)} %param.9) | copy-start | bytes 18874372

commit v8 on v7

--- a/solution.py
+++ b/solution.py
@@ -242,16 +242,22 @@
     notes_ref[...] = jnp.broadcast_to(note_ref[...][None], notes_ref.shape)
 
 
-def down_kernel(comms, blocks, step_number, index_ref, scaled_ref, sums_ref, tiles_ref, local_ref, back_ref, turn_ref, ready):
+def down_kernel(comms, blocks, step_number, index_ref, scaled_ref, sums_ref, tiles_ref, local_ref, back_ref, turn_ref, *room, ready):
     count, touched = tiles_ref.shape[:2]
     width = tiles_ref.shape[3]
     arcs = count // comms
+    copies = []
+    if step_number == 2:
+        tiles_hbm, (tiles_ref, sems) = tiles_ref, room
+        copies = fetch(tiles_hbm, tiles_ref, sems, 0, 2 * PARTS)
     local_ref[...] = jnp.zeros_like(local_ref)
     if step_number == 0:
         back_ref[...] = jnp.full(back_ref.shape, -1.0, F32)
     lane = lax.broadcasted_iota(jnp.int32, (width, width), 1)
     total = jnp.zeros((width, width), F32)
     for i in range(count):
+        if copies and i % (count // len(copies)) == 0:
+            copies[i // (count // len(copies))].wait()
         row = scaled_ref[i : i + 1]
         for k in range(touched):
             total = beside(tiles_ref[i, k], row, lane, k * count + i, total)
@@ -422,7 +428,9 @@
     def spread(step_number, scaled, sums):
         return call(
             functools.partial(down_kernel, comms, blocks, step_number), [row_shape, back_shape],
-            (index, scaled, sums, kept(tiles)), 1, [room(*flat)], flops=3 * unit,
+            (index, scaled, sums, kept(tiles) if step_number < 2 else tiles), 1,
+            [room(*flat)] + ([room(count, touched, *flat), sems(2 * PARTS)] if step_number == 2 else []),
+            flops=3 * unit, hbm=(3,) if step_number == 2 else (),
         )
 
     def add(note, other, back):

time: 126 us -> 126 us (level)
  local copies, waits for them, and re-layouts: 2.81 us -> 0.04 us
  waiting for transfers between devices: 14.3 us -> 15.9 us
    unnamed x18 -> x16, local copies, waits for them, and re-layouts: 2.81 us -> 0.04 us
    all_to_all x1, waiting for transfers between devices: 1.89 us -> 3.48 us  [body(): notes = lax.all_to_all(notes, 'comm', 0, 0)]
  transfers between devices with their start and end apart: 12 -> 12, of which waited for: 6 -> 6; matrix products, arithmetic and copies ran while one was open for 0% -> 0% of each run, Pallas kernels for 17% -> 18%
where the time goes in v8:
time: 126 us
  starting transfers between devices  57.2 us (45%)
  Pallas kernels  37.6 us (30%)
  waiting for transfers between devices  15.9 us (13%)
  blocking collectives  14 us (11%)
    pallas_call x21, Pallas kernels, call(): pl.pallas_call(kernel, out_shape=outs, in_specs=[HBM if n in hbm else ANY...  37.6 us
    all_to_all x5, starting transfers between devices, exchange(): return lax.all_to_all(x, GROUP, 0, 0)  31.8 us
    ppermute x6, starting transfers between devices, across(): return lax.ppermute(x, 'comm', [(i, i ^ step) for i in range(peers)])  18.8 us
    all_to_all x1, blocking collectives, exchange(): return lax.all_to_all(x, GROUP, 0, 0)  14 us
    all_to_all x5, waiting for transfers between devices, exchange(): return lax.all_to_all(x, GROUP, 0, 0)  12.4 us
    all_to_all x1, starting transfers between devices, body(): notes = lax.all_to_all(notes, 'comm', 0, 0)  6.67 us
    all_to_all x1, waiting for transfers between devices, body(): notes = lax.all_to_all(notes, 'comm', 0, 0)  3.48 us
  transfers between devices with their start and end apart: 12, of which 6 were waited for; matrix products, arithmetic and copies ran while one was open for 0% of the time, Pallas kernels for 18%

profile of v8, /device:TPU:1, one launch (start us, length us, event | category | flops | bytes accessed | tf_op | source)
XLA Modules:
  0.0 125.7 jit_solution(6125356101535620975)
XLA Ops:
  0.7 2.3 %shard_map.120 = (f32[16,128]{1,0:T(8,128)S(1)}, f32[32,16,128]{2,1,0:T(8,128)}) custom-call(f32[16,128]{1,0:T(8,128)} %bitcast.27, f32[16,128,128]{2,1,0:T(8,128)} %bitcast.21), custom_call_target="tpu_custom_call" | custom-call | bytes 4194304 | tf_op jit(solution)/shard_map/pallas_call | solution.py:44
  3.0 8.6 %all-to-all-start = ((f32[32,16,128]{2,1,0:T(8,128)}), f32[32,16,128]{2,1,0:T(8,128)S(1)}, u32[]{:S(2)}, u32[]{:S(2)}) async-start(f32[32,16,128]{2,1,0:T(8,128)} %get-tuple-element.58), calls=%async_computation | async-start | bytes 524288 | tf_op jit(solution)/shard_map/all_to_all | solution.py:411
  11.6 2.7 %shard_map.121 = (f32[32,128]{1,0:T(8,128)S(1)}, f32[16,128,128]{2,1,0:T(8,128)S(1)}) custom-call(s32[3,2,16]{2,1,0:T(2,128)} %bitcast.34, f32[16,128]{1,0:T(8,128)S(1)} %get-tuple-element.56.refs_1_.refs_7_.v0_ref, f32[32,3,128,128]{3,2,1,0:T(8,128)} %bitcast.8, f32[16,128,128]{2,1,0:T(8,128)} %refs_3_.5), custom_call_target="tpu_custom_call" | custom-call | flops 2097152 | bytes 4194304 | tf_op jit(solution)/shard_map/pallas_call | solution.py:44
  14.8 5.7 %all-to-all-done.refs_3_ = f32[32,16,128]{2,1,0:T(8,128)S(1)} async-done(((f32[32,16,128]{2,1,0:T(8,128)}), f32[32,16,128]{2,1,0:T(8,128)S(1)}, u32[]{:S(2)}, u32[]{:S(2)}) %all-to-all-start) | async-done | bytes 262176 | tf_op jit(solution)/shard_map/all_to_all | solution.py:411
  20.5 3.6 %shard_map.123 = (f32[32,128]{1,0:T(8,128)S(1)}, f32[24,128]{1,0:T(8,128)S(1)}) custom-call(s32[3,2,16]{2,1,0:T(2,128)} %bitcast.35, s32[2,16]{1,0:T(2,128)} %refs_1_.5, f32[32,128]{1,0:T(8,128)S(1)} %get-tuple-element.57.refs_2_, f32[32,16,128]{2,1,0:T(8,128)S(1)} %all-to-all-done.refs_3_, f32[16,128]{1,0:T(8,128)S(1)} %shard_map.122.refs_4_.q0_ref, ...), custom_call_target="tpu_custom_call" | custom-call | flops 3145728 | bytes 4194304 | tf_op jit(solution)/shard_map/pallas_call | solution.py:44
  24.1 1.7 %collective-permute-start = (f32[24,128]{1,0:T(8,128)S(1)}, f32[24,128]{1,0:T(8,128)S(1)}, u32[]{:S(2)}, u32[]{:S(2)}) collective-permute-start(f32[24,128]{1,0:T(8,128)S(1)} %get-tuple-element.62.note_ref), channel_id=1, source_target_pairs={{0,32},{32,0},{64,96},{96,64},{128,160},{160,128},{192,224},{224,1... | collective-permute-start | bytes 36872 | tf_op jit(solution)/shard_map/ppermute | solution.py:414
  25.9 3.4 %shard_map.124 = (f32[16,128]{1,0:T(8,128)S(1)}, f32[32,4,128]{2,1,0:T(4,128)}) custom-call(s32[3,2,16]{2,1,0:T(2,128)} %bitcast.36, f32[32,128]{1,0:T(8,128)S(1)} %get-tuple-element.60.refs_1_, f32[16,128]{1,0:T(8,128)S(1)} %bitcast.29, f32[32,3,128,128]{3,2,1,0:T(8,128)S(1)} %bitcast.17), custom_call_target="tpu_custom_call" | custom-call | flops 3145728 | bytes 4194304 | tf_op jit(solution)/shard_map/pallas_call | solution.py:44
  29.3 4.0 %all-to-all-start.1 = ((f32[32,4,128]{2,1,0:T(4,128)}), f32[32,4,128]{2,1,0:T(4,128)S(1)}, u32[]{:S(2)}, u32[]{:S(2)}) async-start(f32[32,4,128]{2,1,0:T(4,128)} %get-tuple-element.64), calls=%async_computation.1 | async-start | bytes 131072 | tf_op jit(solution)/shard_map/all_to_all | solution.py:411
  33.4 6.1 %collective-permute-start.1 = (f32[24,128]{1,0:T(8,128)S(1)}, f32[24,128]{1,0:T(8,128)S(1)}, u32[]{:S(2)}, u32[]{:S(2)}) collective-permute-start(f32[24,128]{1,0:T(8,128)S(1)} %get-tuple-element.68.note_ref), channel_id=1, source_target_pairs={{0,128},{32,160},{64,192},{96,224},{128,0},{160,32},{192,64},{224,... | collective-permute-start | bytes 36872 | tf_op jit(solution)/shard_map/ppermute | solution.py:414
  39.5 1.3 %all-to-all-done.1.back_ref = f32[32,4,128]{2,1,0:T(4,128)S(1)} async-done(((f32[32,4,128]{2,1,0:T(4,128)}), f32[32,4,128]{2,1,0:T(4,128)S(1)}, u32[]{:S(2)}, u32[]{:S(2)}) %all-to-all-start.1) | async-done | bytes 65568 | tf_op jit(solution)/shard_map/all_to_all | solution.py:411
  40.8 1.6 %shard_map.126 = (f32[16,128]{1,0:T(8,128)S(1)}, f32[16,128]{1,0:T(8,128)S(1)}, f32[32,2,128]{2,1,0:T(2,128)}, f32[2,32,128]{2,1,0:T(8,128)S(1)}) custom-call(f32[16,128]{1,0:T(8,128)S(1)} %get-tuple-element.56.refs_1_.refs_7_.v0_ref, f32[16,128]{1,0:T(8,128)S(1)} %get-tuple-element.61.local_ref, f32[32,4,128]{2,1,0:T(4,128)S(1)} %all-to-all-done.1.back_ref, ...), custom_call_target="tpu_custom_call" | custom-call | bytes 4194304 | tf_op jit(solution)/shard_map/pallas_call | solution.py:44
  42.4 6.5 %all-to-all-start.2 = ((f32[32,2,128]{2,1,0:T(2,128)}), f32[32,2,128]{2,1,0:T(2,128)S(1)}, u32[]{:S(2)}, u32[]{:S(2)}) async-start(f32[32,2,128]{2,1,0:T(2,128)} %get-tuple-element.70), calls=%async_computation.2 | async-start | bytes 65536 | tf_op jit(solution)/shard_map/all_to_all | solution.py:411
  48.9 2.9 %collective-permute-start.2 = (f32[24,128]{1,0:T(8,128)S(1)}, f32[24,128]{1,0:T(8,128)S(1)}, u32[]{:S(2)}, u32[]{:S(2)}) collective-permute-start(f32[24,128]{1,0:T(8,128)S(1)} %get-tuple-element.71.half_ref), channel_id=1, source_target_pairs={{0,64},{32,96},{64,0},{96,32},{128,192},{160,224},{192,128},{224,1... | collective-permute-start | bytes 36872 | tf_op jit(solution)/shard_map/ppermute | solution.py:414
  51.8 2.7 %shard_map.127 = (f32[32,128]{1,0:T(8,128)S(1)}, f32[16,128,128]{2,1,0:T(8,128)S(1)}) custom-call(s32[3,2,16]{2,1,0:T(2,128)} %bitcast.37, f32[16,128]{1,0:T(8,128)S(1)} %get-tuple-element.66.refs_1_.v1_ref, f32[32,3,128,128]{3,2,1,0:T(8,128)} %bitcast.10, f32[16,128,128]{2,1,0:T(8,128)} %refs_3_.5), custom_call_target="tpu_custom_call" | custom-call | flops 2097152 | bytes 4194304 | tf_op jit(solution)/shard_map/pallas_call | solution.py:44
  55.0 1.1 all-to-all-done.2.refs_3_
  56.2 3.6 %shard_map.130 = (f32[32,128]{1,0:T(8,128)S(1)}, f32[24,128]{1,0:T(8,128)S(1)}) custom-call(s32[3,2,16]{2,1,0:T(2,128)} %bitcast.38, s32[2,16]{1,0:T(2,128)} %refs_1_.5, f32[32,128]{1,0:T(8,128)S(1)} %get-tuple-element.67.refs_2_, f32[32,2,128]{2,1,0:T(2,128)S(1)} %all-to-all-done.2.refs_3_, f32[16,128]{1,0:T(8,128)S(1)} %get-tuple-element.73.refs_4_.q1_ref, ...), custom_call_target="tpu_custom_call" | custom-call | flops 3145728 | bytes 4194304 | tf_op jit(solution)/shard_map/pallas_call | solution.py:44
  59.8 0.8 collective-permute-start.3
  60.6 3.4 %shard_map.131 = (f32[16,128]{1,0:T(8,128)S(1)}, f32[32,4,128]{2,1,0:T(4,128)}) custom-call(s32[3,2,16]{2,1,0:T(2,128)} %bitcast.39, f32[32,128]{1,0:T(8,128)S(1)} %get-tuple-element.74.refs_1_, f32[8,128]{1,0:T(8,128)S(1)} %get-tuple-element.75.refs_2_, f32[32,3,128,128]{3,2,1,0:T(8,128)S(1)} %bitcast.20), custom_call_target="tpu_custom_call" | custom-call | flops 3145728 | bytes 4194304 | tf_op jit(solution)/shard_map/pallas_call | solution.py:44
  64.0 6.1 %all-to-all-start.3 = ((f32[32,4,128]{2,1,0:T(4,128)}), f32[32,4,128]{2,1,0:T(4,128)S(1)}, u32[]{:S(2)}, u32[]{:S(2)}) async-start(f32[32,4,128]{2,1,0:T(4,128)} %get-tuple-element.79), calls=%async_computation.3 | async-start | bytes 131072 | tf_op jit(solution)/shard_map/all_to_all | solution.py:411
  70.1 5.5 %collective-permute-start.4 = (f32[24,128]{1,0:T(8,128)S(1)}, f32[24,128]{1,0:T(8,128)S(1)}, u32[]{:S(2)}, u32[]{:S(2)}) collective-permute-start(f32[24,128]{1,0:T(8,128)S(1)} %get-tuple-element.87.note_ref), channel_id=1, source_target_pairs={{0,128},{32,160},{64,192},{96,224},{128,0},{160,32},{192,64},{224,... | collective-permute-start | bytes 36872 | tf_op jit(solution)/shard_map/ppermute | solution.py:414
  75.6 1.9 %all-to-all-done.3.back_ref = f32[32,4,128]{2,1,0:T(4,128)S(1)} async-done(((f32[32,4,128]{2,1,0:T(4,128)}), f32[32,4,128]{2,1,0:T(4,128)S(1)}, u32[]{:S(2)}, u32[]{:S(2)}) %all-to-all-start.3) | async-done | bytes 65568 | tf_op jit(solution)/shard_map/all_to_all | solution.py:411
  77.4 1.2 shard_map.133
  78.6 6.5 %all-to-all-start.4 = ((f32[32,2,128]{2,1,0:T(2,128)}), f32[32,2,128]{2,1,0:T(2,128)S(1)}, u32[]{:S(2)}, u32[]{:S(2)}) async-start(f32[32,2,128]{2,1,0:T(2,128)} %get-tuple-element.89), calls=%async_computation.4 | async-start | bytes 65536 | tf_op jit(solution)/shard_map/all_to_all | solution.py:411
  85.2 1.8 %collective-permute-start.5 = (f32[24,128]{1,0:T(8,128)S(1)}, f32[24,128]{1,0:T(8,128)S(1)}, u32[]{:S(2)}, u32[]{:S(2)}) collective-permute-start(f32[24,128]{1,0:T(8,128)S(1)} %get-tuple-element.91.half_ref), channel_id=1, source_target_pairs={{0,64},{32,96},{64,0},{96,32},{128,192},{160,224},{192,128},{224,1... | collective-permute-start | bytes 36872 | tf_op jit(solution)/shard_map/ppermute | solution.py:414
  87.0 2.5 %shard_map.134 = (f32[32,128]{1,0:T(8,128)S(1)}, f32[16,128,128]{2,1,0:T(8,128)S(1)}) custom-call(s32[3,2,16]{2,1,0:T(2,128)} %bitcast.40, f32[16,128]{1,0:T(8,128)S(1)} %get-tuple-element.85.refs_1_.refs_10_.v2_ref, f32[32,3,128,128]{3,2,1,0:T(8,128)} %bitcast.12, f32[16,128,128]{2,1,0:T(8,128)} %refs_3_.5), custom_call_target="tpu_custom_call" | custom-call | flops 2097152 | bytes 4194304 | tf_op jit(solution)/shard_map/pallas_call | solution.py:44
  90.0 2.4 %all-to-all-done.4.refs_3_ = f32[32,2,128]{2,1,0:T(2,128)S(1)} async-done(((f32[32,2,128]{2,1,0:T(2,128)}), f32[32,2,128]{2,1,0:T(2,128)S(1)}, u32[]{:S(2)}, u32[]{:S(2)}) %all-to-all-start.4) | async-done | bytes 32800 | tf_op jit(solution)/shard_map/all_to_all | solution.py:411
  92.5 4.2 %shard_map.137 = (f32[32,128]{1,0:T(8,128)S(1)}, f32[8,24,128]{2,1,0:T(8,128)}) custom-call(s32[3,2,16]{2,1,0:T(2,128)} %bitcast.41, s32[2,16]{1,0:T(2,128)} %refs_1_.5, f32[32,128]{1,0:T(8,128)S(1)} %get-tuple-element.86.refs_2_, f32[32,2,128]{2,1,0:T(2,128)S(1)} %all-to-all-done.4.refs_3_, f32[16,128]{1,0:T(8,128)S(1)} %get-tuple-element.93.refs_4_.q2_ref, ...), custom_call_target="tpu_custom_call" | custom-call | flops 3145728 | bytes 4194304 | tf_op jit(solution)/shard_map/pallas_call | solution.py:44
  96.7 6.7 %all-to-all-start.5 = ((f32[8,24,128]{2,1,0:T(8,128)}), f32[8,24,128]{2,1,0:T(8,128)S(1)}, u32[]{:S(2)}, u32[]{:S(2)}) async-start(f32[8,24,128]{2,1,0:T(8,128)} %get-tuple-element.97), calls=%async_computation.5 | async-start | bytes 196608 | tf_op jit(solution)/shard_map/all_to_all | solution.py:494
  103.4 4.0 %shard_map.138 = (f32[16,128]{1,0:T(8,128)S(1)}, f32[32,4,128]{2,1,0:T(4,128)S(1)}) custom-call(s32[3,2,16]{2,1,0:T(2,128)} %bitcast.42, f32[32,128]{1,0:T(8,128)S(1)} %get-tuple-element.94.refs_1_, f32[8,128]{1,0:T(8,128)S(1)} %get-tuple-element.95.refs_2_.sums_ref, f32[32,3,128,128]{3,2,1,0:T(8,128)} %bitcast.14), custom_call_target="tpu_custom_call" | custom-call | flops 3145728 | bytes 4194304 | tf_op jit(solution)/shard_map/pallas_call | solution.py:44
  107.3 3.5 %all-to-all-done.5.notes_ref = f32[8,24,128]{2,1,0:T(8,128)S(1)} async-done(((f32[8,24,128]{2,1,0:T(8,128)}), f32[8,24,128]{2,1,0:T(8,128)S(1)}, u32[]{:S(2)}, u32[]{:S(2)}) %all-to-all-start.5) | async-done | bytes 98336 | tf_op jit(solution)/shard_map/all_to_all | solution.py:494
  110.9 14.0 %all_to_all.35.back_ref = f32[32,4,128]{2,1,0:T(4,128)S(1)} all-to-all(f32[32,4,128]{2,1,0:T(4,128)S(1)} %get-tuple-element.99), channel_id=1, replica_groups=mesh['comm'=8,'stn'=16,'tm'=2] {'stn','tm'}, dimensions={0} | all-to-all | bytes 131072 | tf_op jit(solution)/shard_map/all_to_all | solution.py:411
  124.9 0.7 shard_map.140
  (32 shorter events, 1.6 us)
Async XLA Ops:
  0.6 19.9 %copy-start.2 = (f32[2,8,128]{2,1,0:T(8,128)S(1)}, f32[2,8,128]{2,1,0:T(8,128)}, u32[]{:S(2)}) copy-start(f32[2,8,128]{2,1,0:T(8,128)} %param.14) | copy-start | bytes 24580
  0.6 13.7 %copy-start.3 = (f32[16,128]{1,0:T(8,128)S(1)}, f32[16,128]{1,0:T(8,128)}, u32[]{:S(2)}) copy-start(f32[16,128]{1,0:T(8,128)} %cap_rhs_ref.5) | copy-start | bytes 24580
  0.7 19.8 %copy-start.1 = (f32[2,16,128]{2,1,0:T(8,128)S(1)}, f32[2,16,128]{2,1,0:T(8,128)}, u32[]{:S(2)}) copy-start(f32[2,16,128]{2,1,0:T(8,128)} %param.13) | copy-start | bytes 49156
  3.0 17.5 %all-to-all-start = ((f32[32,16,128]{2,1,0:T(8,128)}), f32[32,16,128]{2,1,0:T(8,128)S(1)}, u32[]{:S(2)}, u32[]{:S(2)}) async-start(f32[32,16,128]{2,1,0:T(8,128)} %get-tuple-element.58), calls=%async_computation | async-start | bytes 524288 | tf_op jit(solution)/shard_map/all_to_all | solution.py:411
  11.6 14.3 %slice-start = ((s8[6291456]{0:T(1024)(128)(4,1)}), s8[2097152]{0:T(1024)(128)(4,1)S(1)}, s32[]{:S(2)}) async-start(s8[6291456]{0:T(1024)(128)(4,1)} %bitcast.15), calls=%async_computation.7 | async-start | bytes 4194304
  20.5 5.4 %slice-start.1 = ((s8[6291456]{0:T(1024)(128)(4,1)}), s8[4194304]{0:T(1024)(128)(4,1)S(1)}, s32[]{:S(2)}) async-start(s8[6291456]{0:T(1024)(128)(4,1)} %bitcast.15), calls=%async_computation.8 | async-start | bytes 8388608
  20.5 20.3 %copy-start = (f32[2,8,128,128]{3,2,1,0:T(8,128)S(1)}, f32[2,8,128,128]{3,2,1,0:T(8,128)}, u32[]{:S(2)}) copy-start(f32[2,8,128,128]{3,2,1,0:T(8,128)} %param.16) | copy-start | bytes 3145732
  24.1 5.2 %collective-permute-start = (f32[24,128]{1,0:T(8,128)S(1)}, f32[24,128]{1,0:T(8,128)S(1)}, u32[]{:S(2)}, u32[]{:S(2)}) collective-permute-start(f32[24,128]{1,0:T(8,128)S(1)} %get-tuple-element.62.note_ref), channel_id=1, source_target_pairs={{0,32},{32,0},{64,96},{96,64},{128,160},{160,128},{192,224},{224,1... | collective-permute-start | bytes 36872 | tf_op jit(solution)/shard_map/ppermute | solution.py:414
  29.3 11.4 %all-to-all-start.1 = ((f32[32,4,128]{2,1,0:T(4,128)}), f32[32,4,128]{2,1,0:T(4,128)S(1)}, u32[]{:S(2)}, u32[]{:S(2)}) async-start(f32[32,4,128]{2,1,0:T(4,128)} %get-tuple-element.64), calls=%async_computation.1 | async-start | bytes 131072 | tf_op jit(solution)/shard_map/all_to_all | solution.py:411
  33.4 9.0 %collective-permute-start.1 = (f32[24,128]{1,0:T(8,128)S(1)}, f32[24,128]{1,0:T(8,128)S(1)}, u32[]{:S(2)}, u32[]{:S(2)}) collective-permute-start(f32[24,128]{1,0:T(8,128)S(1)} %get-tuple-element.68.note_ref), channel_id=1, source_target_pairs={{0,128},{32,160},{64,192},{96,224},{128,0},{160,32},{192,64},{224,... | collective-permute-start | bytes 36872 | tf_op jit(solution)/shard_map/ppermute | solution.py:414
  42.4 13.8 %all-to-all-start.2 = ((f32[32,2,128]{2,1,0:T(2,128)}), f32[32,2,128]{2,1,0:T(2,128)S(1)}, u32[]{:S(2)}, u32[]{:S(2)}) async-start(f32[32,2,128]{2,1,0:T(2,128)} %get-tuple-element.70), calls=%async_computation.2 | async-start | bytes 65536 | tf_op jit(solution)/shard_map/all_to_all | solution.py:411
  48.9 5.6 %collective-permute-start.2 = (f32[24,128]{1,0:T(8,128)S(1)}, f32[24,128]{1,0:T(8,128)S(1)}, u32[]{:S(2)}, u32[]{:S(2)}) collective-permute-start(f32[24,128]{1,0:T(8,128)S(1)} %get-tuple-element.71.half_ref), channel_id=1, source_target_pairs={{0,64},{32,96},{64,0},{96,32},{128,192},{160,224},{192,128},{224,1... | collective-permute-start | bytes 36872 | tf_op jit(solution)/shard_map/ppermute | solution.py:414
  51.8 8.8 %slice-start.2 = ((s8[6291456]{0:T(1024)(128)(4,1)}), s8[2097152]{0:T(1024)(128)(4,1)S(1)}, s32[]{:S(2)}) async-start(s8[6291456]{0:T(1024)(128)(4,1)} %bitcast.18), calls=%async_computation.9 | async-start | bytes 4194304
  56.1 4.5 %slice-start.3 = ((s8[6291456]{0:T(1024)(128)(4,1)}), s8[4194304]{0:T(1024)(128)(4,1)S(1)}, s32[]{:S(2)}) async-start(s8[6291456]{0:T(1024)(128)(4,1)} %bitcast.18), calls=%async_computation.10 | async-start | bytes 8388608
  59.8 4.2 %collective-permute-start.3 = (f32[24,128]{1,0:T(8,128)S(1)}, f32[24,128]{1,0:T(8,128)S(1)}, u32[]{:S(2)}, u32[]{:S(2)}) collective-permute-start(f32[24,128]{1,0:T(8,128)S(1)} %get-tuple-element.77.note_ref), channel_id=1, source_target_pairs={{0,32},{32,0},{64,96},{96,64},{128,160},{160,128},{192,224},{224,1... | collective-permute-start | bytes 36872 | tf_op jit(solution)/shard_map/ppermute | solution.py:414
  64.0 13.4 %all-to-all-start.3 = ((f32[32,4,128]{2,1,0:T(4,128)}), f32[32,4,128]{2,1,0:T(4,128)S(1)}, u32[]{:S(2)}, u32[]{:S(2)}) async-start(f32[32,4,128]{2,1,0:T(4,128)} %get-tuple-element.79), calls=%async_computation.3 | async-start | bytes 131072 | tf_op jit(solution)/shard_map/all_to_all | solution.py:411
  70.1 8.5 %collective-permute-start.4 = (f32[24,128]{1,0:T(8,128)S(1)}, f32[24,128]{1,0:T(8,128)S(1)}, u32[]{:S(2)}, u32[]{:S(2)}) collective-permute-start(f32[24,128]{1,0:T(8,128)S(1)} %get-tuple-element.87.note_ref), channel_id=1, source_target_pairs={{0,128},{32,160},{64,192},{96,224},{128,0},{160,32},{192,64},{224,... | collective-permute-start | bytes 36872 | tf_op jit(solution)/shard_map/ppermute | solution.py:414
  78.6 13.8 %all-to-all-start.4 = ((f32[32,2,128]{2,1,0:T(2,128)}), f32[32,2,128]{2,1,0:T(2,128)S(1)}, u32[]{:S(2)}, u32[]{:S(2)}) async-start(f32[32,2,128]{2,1,0:T(2,128)} %get-tuple-element.89), calls=%async_computation.4 | async-start | bytes 65536 | tf_op jit(solution)/shard_map/all_to_all | solution.py:411
  85.2 4.3 %collective-permute-start.5 = (f32[24,128]{1,0:T(8,128)S(1)}, f32[24,128]{1,0:T(8,128)S(1)}, u32[]{:S(2)}, u32[]{:S(2)}) collective-permute-start(f32[24,128]{1,0:T(8,128)S(1)} %get-tuple-element.91.half_ref), channel_id=1, source_target_pairs={{0,64},{32,96},{64,0},{96,32},{128,192},{160,224},{192,128},{224,1... | collective-permute-start | bytes 36872 | tf_op jit(solution)/shard_map/ppermute | solution.py:414
  96.7 14.1 %all-to-all-start.5 = ((f32[8,24,128]{2,1,0:T(8,128)}), f32[8,24,128]{2,1,0:T(8,128)S(1)}, u32[]{:S(2)}, u32[]{:S(2)}) async-start(f32[8,24,128]{2,1,0:T(8,128)} %get-tuple-element.97), calls=%async_computation.5 | async-start | bytes 196608 | tf_op jit(solution)/shard_map/all_to_all | solution.py:494

commit v9 on v8

--- a/solution.py
+++ b/solution.py
@@ -206,12 +206,8 @@
     turn_ref[...] = total.T
     note_ref[...] = jnp.zeros_like(note_ref)
 
-    def put(i, _):
-        cap = cap_index_ref[lax.div(i, arcs), lax.rem(i, arcs)]
-        note_ref[pl.ds(cap, 1)] += turn_ref[pl.ds(i, 1)]
-        return 0
-
-    lax.fori_loop(0, count, put, 0, unroll=4)
+    for i in range(count):
+        note_ref[pl.ds(cap_index_ref[i // arcs, i % arcs], 1)] += turn_ref[i : i + 1]
     return fold(upward * scaled)
 
 
@@ -264,20 +260,17 @@
     turn_ref[...] = total.T
     ready()
 
-    def put(i, _):
-        c, j = lax.div(i, arcs), lax.rem(i, arcs)
+    for i in range(count):
+        c, j = i // arcs, i % arcs
         for k in range(2):
             b = c * blocks + lax.rem(index_ref[k, c, j], blocks)
-            local_ref[pl.ds(b, 1)] += turn_ref[pl.ds(k * count + i, 1)]
+            local_ref[pl.ds(b, 1)] += turn_ref[k * count + i : k * count + i + 1]
         far = index_ref[2, c, j]
         to = lax.div(far, blocks)
-        back_ref[to, pl.ds(c, 1)] = turn_ref[pl.ds(2 * count + i, 1)]
+        back_ref[to, c : c + 1] = turn_ref[2 * count + i : 2 * count + i + 1]
         if step_number == 0:
             local = lax.rem(far, blocks).astype(F32)
-            back_ref[to, pl.ds(comms + c, 1)] = jnp.full((1, width), local, F32)
-        return 0
-
-    lax.fori_loop(0, count, put, 0, unroll=4)
+            back_ref[to, comms + c : comms + c + 1] = jnp.full((1, width), local, F32)
     if step_number == 1:
         shape = (back_ref.shape[0], 2, width)
         back_ref[:, comms : comms + 2] = jnp.broadcast_to(sums_ref[0:2][None], shape)

time: 126 us -> 125 us (level)
  no operation moved by 1% of the time
where the time goes in v9:
time: 125 us
  starting transfers between devices  57 us (46%)
  Pallas kernels  36.7 us (29%)
  waiting for transfers between devices  16.3 us (13%)
  blocking collectives  14 us (11%)
    pallas_call x21, Pallas kernels, call(): pl.pallas_call(kernel, out_shape=outs, in_specs=[HBM if n in hbm else ANY...  36.7 us
    all_to_all x5, starting transfers between devices, exchange(): return lax.all_to_all(x, GROUP, 0, 0)  32 us
    ppermute x6, starting transfers between devices, across(): return lax.ppermute(x, 'comm', [(i, i ^ step) for i in range(peers)])  18.5 us
    all_to_all x1, blocking collectives, exchange(): return lax.all_to_all(x, GROUP, 0, 0)  14 us
    all_to_all x5, waiting for transfers between devices, exchange(): return lax.all_to_all(x, GROUP, 0, 0)  12.6 us
    all_to_all x1, starting transfers between devices, body(): notes = lax.all_to_all(notes, 'comm', 0, 0)  6.47 us
    all_to_all x1, waiting for transfers between devices, body(): notes = lax.all_to_all(notes, 'comm', 0, 0)  3.64 us
  transfers between devices with their start and end apart: 12, of which 6 were waited for; matrix products, arithmetic and copies ran while one was open for 0% of the time, Pallas kernels for 18%

profile of v9, /device:TPU:1, one launch (start us, length us, event | category | flops | bytes accessed | tf_op | source)
XLA Modules:
  0.0 124.9 jit_solution(583915846966640937)
XLA Ops:
  0.7 2.3 %shard_map.120 = (f32[16,128]{1,0:T(8,128)S(1)}, f32[32,16,128]{2,1,0:T(8,128)}) custom-call(f32[16,128]{1,0:T(8,128)} %bitcast.27, f32[16,128,128]{2,1,0:T(8,128)} %bitcast.21), custom_call_target="tpu_custom_call" | custom-call | bytes 4194304 | tf_op jit(solution)/shard_map/pallas_call | solution.py:44
  3.0 8.6 %all-to-all-start = ((f32[32,16,128]{2,1,0:T(8,128)}), f32[32,16,128]{2,1,0:T(8,128)S(1)}, u32[]{:S(2)}, u32[]{:S(2)}) async-start(f32[32,16,128]{2,1,0:T(8,128)} %get-tuple-element.58), calls=%async_computation | async-start | bytes 524288 | tf_op jit(solution)/shard_map/all_to_all | solution.py:404
  11.6 2.7 %shard_map.121 = (f32[32,128]{1,0:T(8,128)S(1)}, f32[16,128,128]{2,1,0:T(8,128)S(1)}) custom-call(s32[3,2,16]{2,1,0:T(2,128)} %bitcast.34, f32[16,128]{1,0:T(8,128)S(1)} %get-tuple-element.56.refs_1_.refs_7_.v0_ref, f32[32,3,128,128]{3,2,1,0:T(8,128)} %bitcast.8, f32[16,128,128]{2,1,0:T(8,128)} %refs_3_.5), custom_call_target="tpu_custom_call" | custom-call | flops 2097152 | bytes 4194304 | tf_op jit(solution)/shard_map/pallas_call | solution.py:44
  14.8 5.7 %all-to-all-done.refs_3_ = f32[32,16,128]{2,1,0:T(8,128)S(1)} async-done(((f32[32,16,128]{2,1,0:T(8,128)}), f32[32,16,128]{2,1,0:T(8,128)S(1)}, u32[]{:S(2)}, u32[]{:S(2)}) %all-to-all-start) | async-done | bytes 262176 | tf_op jit(solution)/shard_map/all_to_all | solution.py:404
  20.5 3.5 %shard_map.123 = (f32[32,128]{1,0:T(8,128)S(1)}, f32[24,128]{1,0:T(8,128)S(1)}) custom-call(s32[3,2,16]{2,1,0:T(2,128)} %bitcast.35, s32[2,16]{1,0:T(2,128)} %refs_1_.5, f32[32,128]{1,0:T(8,128)S(1)} %get-tuple-element.57.refs_2_, f32[32,16,128]{2,1,0:T(8,128)S(1)} %all-to-all-done.refs_3_, f32[16,128]{1,0:T(8,128)S(1)} %shard_map.122.refs_4_.q0_ref, ...), custom_call_target="tpu_custom_call" | custom-call | flops 3145728 | bytes 4194304 | tf_op jit(solution)/shard_map/pallas_call | solution.py:44
  24.0 1.7 %collective-permute-start = (f32[24,128]{1,0:T(8,128)S(1)}, f32[24,128]{1,0:T(8,128)S(1)}, u32[]{:S(2)}, u32[]{:S(2)}) collective-permute-start(f32[24,128]{1,0:T(8,128)S(1)} %get-tuple-element.62.note_ref), channel_id=1, source_target_pairs={{0,32},{32,0},{64,96},{96,64},{128,160},{160,128},{192,224},{224,1... | collective-permute-start | bytes 36872 | tf_op jit(solution)/shard_map/ppermute | solution.py:407
  25.7 3.2 %shard_map.124 = (f32[16,128]{1,0:T(8,128)S(1)}, f32[32,4,128]{2,1,0:T(4,128)}) custom-call(s32[3,2,16]{2,1,0:T(2,128)} %bitcast.36, f32[32,128]{1,0:T(8,128)S(1)} %get-tuple-element.60.refs_1_, f32[16,128]{1,0:T(8,128)S(1)} %bitcast.29, f32[32,3,128,128]{3,2,1,0:T(8,128)S(1)} %bitcast.17), custom_call_target="tpu_custom_call" | custom-call | flops 3145728 | bytes 4194304 | tf_op jit(solution)/shard_map/pallas_call | solution.py:44
  29.0 4.1 %all-to-all-start.1 = ((f32[32,4,128]{2,1,0:T(4,128)}), f32[32,4,128]{2,1,0:T(4,128)S(1)}, u32[]{:S(2)}, u32[]{:S(2)}) async-start(f32[32,4,128]{2,1,0:T(4,128)} %get-tuple-element.64), calls=%async_computation.1 | async-start | bytes 131072 | tf_op jit(solution)/shard_map/all_to_all | solution.py:404
  33.0 6.1 %collective-permute-start.1 = (f32[24,128]{1,0:T(8,128)S(1)}, f32[24,128]{1,0:T(8,128)S(1)}, u32[]{:S(2)}, u32[]{:S(2)}) collective-permute-start(f32[24,128]{1,0:T(8,128)S(1)} %get-tuple-element.68.note_ref), channel_id=1, source_target_pairs={{0,128},{32,160},{64,192},{96,224},{128,0},{160,32},{192,64},{224,... | collective-permute-start | bytes 36872 | tf_op jit(solution)/shard_map/ppermute | solution.py:407
  39.1 1.3 %all-to-all-done.1.back_ref = f32[32,4,128]{2,1,0:T(4,128)S(1)} async-done(((f32[32,4,128]{2,1,0:T(4,128)}), f32[32,4,128]{2,1,0:T(4,128)S(1)}, u32[]{:S(2)}, u32[]{:S(2)}) %all-to-all-start.1) | async-done | bytes 65568 | tf_op jit(solution)/shard_map/all_to_all | solution.py:404
  40.4 1.6 %shard_map.126 = (f32[16,128]{1,0:T(8,128)S(1)}, f32[16,128]{1,0:T(8,128)S(1)}, f32[32,2,128]{2,1,0:T(2,128)}, f32[2,32,128]{2,1,0:T(8,128)S(1)}) custom-call(f32[16,128]{1,0:T(8,128)S(1)} %get-tuple-element.56.refs_1_.refs_7_.v0_ref, f32[16,128]{1,0:T(8,128)S(1)} %get-tuple-element.61.local_ref, f32[32,4,128]{2,1,0:T(4,128)S(1)} %all-to-all-done.1.back_ref, ...), custom_call_target="tpu_custom_call" | custom-call | bytes 4194304 | tf_op jit(solution)/shard_map/pallas_call | solution.py:44
  42.0 6.5 %all-to-all-start.2 = ((f32[32,2,128]{2,1,0:T(2,128)}), f32[32,2,128]{2,1,0:T(2,128)S(1)}, u32[]{:S(2)}, u32[]{:S(2)}) async-start(f32[32,2,128]{2,1,0:T(2,128)} %get-tuple-element.70), calls=%async_computation.2 | async-start | bytes 65536 | tf_op jit(solution)/shard_map/all_to_all | solution.py:404
  48.5 2.9 %collective-permute-start.2 = (f32[24,128]{1,0:T(8,128)S(1)}, f32[24,128]{1,0:T(8,128)S(1)}, u32[]{:S(2)}, u32[]{:S(2)}) collective-permute-start(f32[24,128]{1,0:T(8,128)S(1)} %get-tuple-element.71.half_ref), channel_id=1, source_target_pairs={{0,64},{32,96},{64,0},{96,32},{128,192},{160,224},{192,128},{224,1... | collective-permute-start | bytes 36872 | tf_op jit(solution)/shard_map/ppermute | solution.py:407
  51.5 2.7 %shard_map.127 = (f32[32,128]{1,0:T(8,128)S(1)}, f32[16,128,128]{2,1,0:T(8,128)S(1)}) custom-call(s32[3,2,16]{2,1,0:T(2,128)} %bitcast.37, f32[16,128]{1,0:T(8,128)S(1)} %get-tuple-element.66.refs_1_.v1_ref, f32[32,3,128,128]{3,2,1,0:T(8,128)} %bitcast.10, f32[16,128,128]{2,1,0:T(8,128)} %refs_3_.5), custom_call_target="tpu_custom_call" | custom-call | flops 2097152 | bytes 4194304 | tf_op jit(solution)/shard_map/pallas_call | solution.py:44
  54.7 1.1 all-to-all-done.2.refs_3_
  55.8 3.5 %shard_map.130 = (f32[32,128]{1,0:T(8,128)S(1)}, f32[24,128]{1,0:T(8,128)S(1)}) custom-call(s32[3,2,16]{2,1,0:T(2,128)} %bitcast.38, s32[2,16]{1,0:T(2,128)} %refs_1_.5, f32[32,128]{1,0:T(8,128)S(1)} %get-tuple-element.67.refs_2_, f32[32,2,128]{2,1,0:T(2,128)S(1)} %all-to-all-done.2.refs_3_, f32[16,128]{1,0:T(8,128)S(1)} %get-tuple-element.73.refs_4_.q1_ref, ...), custom_call_target="tpu_custom_call" | custom-call | flops 3145728 | bytes 4194304 | tf_op jit(solution)/shard_map/pallas_call | solution.py:44
  59.3 0.8 collective-permute-start.3
  60.2 3.2 %shard_map.131 = (f32[16,128]{1,0:T(8,128)S(1)}, f32[32,4,128]{2,1,0:T(4,128)}) custom-call(s32[3,2,16]{2,1,0:T(2,128)} %bitcast.39, f32[32,128]{1,0:T(8,128)S(1)} %get-tuple-element.74.refs_1_, f32[8,128]{1,0:T(8,128)S(1)} %get-tuple-element.75.refs_2_, f32[32,3,128,128]{3,2,1,0:T(8,128)S(1)} %bitcast.20), custom_call_target="tpu_custom_call" | custom-call | flops 3145728 | bytes 4194304 | tf_op jit(solution)/shard_map/pallas_call | solution.py:44
  63.4 6.3 %all-to-all-start.3 = ((f32[32,4,128]{2,1,0:T(4,128)}), f32[32,4,128]{2,1,0:T(4,128)S(1)}, u32[]{:S(2)}, u32[]{:S(2)}) async-start(f32[32,4,128]{2,1,0:T(4,128)} %get-tuple-element.79), calls=%async_computation.3 | async-start | bytes 131072 | tf_op jit(solution)/shard_map/all_to_all | solution.py:404
  69.7 5.3 %collective-permute-start.4 = (f32[24,128]{1,0:T(8,128)S(1)}, f32[24,128]{1,0:T(8,128)S(1)}, u32[]{:S(2)}, u32[]{:S(2)}) collective-permute-start(f32[24,128]{1,0:T(8,128)S(1)} %get-tuple-element.87.note_ref), channel_id=1, source_target_pairs={{0,128},{32,160},{64,192},{96,224},{128,0},{160,32},{192,64},{224,... | collective-permute-start | bytes 36872 | tf_op jit(solution)/shard_map/ppermute | solution.py:407
  74.9 2.0 %all-to-all-done.3.back_ref = f32[32,4,128]{2,1,0:T(4,128)S(1)} async-done(((f32[32,4,128]{2,1,0:T(4,128)}), f32[32,4,128]{2,1,0:T(4,128)S(1)}, u32[]{:S(2)}, u32[]{:S(2)}) %all-to-all-start.3) | async-done | bytes 65568 | tf_op jit(solution)/shard_map/all_to_all | solution.py:404
  77.0 1.2 shard_map.133
  78.2 6.5 %all-to-all-start.4 = ((f32[32,2,128]{2,1,0:T(2,128)}), f32[32,2,128]{2,1,0:T(2,128)S(1)}, u32[]{:S(2)}, u32[]{:S(2)}) async-start(f32[32,2,128]{2,1,0:T(2,128)} %get-tuple-element.89), calls=%async_computation.4 | async-start | bytes 65536 | tf_op jit(solution)/shard_map/all_to_all | solution.py:404
  84.7 1.7 %collective-permute-start.5 = (f32[24,128]{1,0:T(8,128)S(1)}, f32[24,128]{1,0:T(8,128)S(1)}, u32[]{:S(2)}, u32[]{:S(2)}) collective-permute-start(f32[24,128]{1,0:T(8,128)S(1)} %get-tuple-element.91.half_ref), channel_id=1, source_target_pairs={{0,64},{32,96},{64,0},{96,32},{128,192},{160,224},{192,128},{224,1... | collective-permute-start | bytes 36872 | tf_op jit(solution)/shard_map/ppermute | solution.py:407
  86.4 2.5 %shard_map.134 = (f32[32,128]{1,0:T(8,128)S(1)}, f32[16,128,128]{2,1,0:T(8,128)S(1)}) custom-call(s32[3,2,16]{2,1,0:T(2,128)} %bitcast.40, f32[16,128]{1,0:T(8,128)S(1)} %get-tuple-element.85.refs_1_.refs_10_.v2_ref, f32[32,3,128,128]{3,2,1,0:T(8,128)} %bitcast.12, f32[16,128,128]{2,1,0:T(8,128)} %refs_3_.5), custom_call_target="tpu_custom_call" | custom-call | flops 2097152 | bytes 4194304 | tf_op jit(solution)/shard_map/pallas_call | solution.py:44
  89.5 2.5 %all-to-all-done.4.refs_3_ = f32[32,2,128]{2,1,0:T(2,128)S(1)} async-done(((f32[32,2,128]{2,1,0:T(2,128)}), f32[32,2,128]{2,1,0:T(2,128)S(1)}, u32[]{:S(2)}, u32[]{:S(2)}) %all-to-all-start.4) | async-done | bytes 32800 | tf_op jit(solution)/shard_map/all_to_all | solution.py:404
  92.0 4.1 %shard_map.137 = (f32[32,128]{1,0:T(8,128)S(1)}, f32[8,24,128]{2,1,0:T(8,128)}) custom-call(s32[3,2,16]{2,1,0:T(2,128)} %bitcast.41, s32[2,16]{1,0:T(2,128)} %refs_1_.5, f32[32,128]{1,0:T(8,128)S(1)} %get-tuple-element.86.refs_2_, f32[32,2,128]{2,1,0:T(2,128)S(1)} %all-to-all-done.4.refs_3_, f32[16,128]{1,0:T(8,128)S(1)} %get-tuple-element.93.refs_4_.q2_ref, ...), custom_call_target="tpu_custom_call" | custom-call | flops 3145728 | bytes 4194304 | tf_op jit(solution)/shard_map/pallas_call | solution.py:44
  96.1 6.5 %all-to-all-start.5 = ((f32[8,24,128]{2,1,0:T(8,128)}), f32[8,24,128]{2,1,0:T(8,128)S(1)}, u32[]{:S(2)}, u32[]{:S(2)}) async-start(f32[8,24,128]{2,1,0:T(8,128)} %get-tuple-element.97), calls=%async_computation.5 | async-start | bytes 196608 | tf_op jit(solution)/shard_map/all_to_all | solution.py:487
  102.6 3.8 %shard_map.138 = (f32[16,128]{1,0:T(8,128)S(1)}, f32[32,4,128]{2,1,0:T(4,128)S(1)}) custom-call(s32[3,2,16]{2,1,0:T(2,128)} %bitcast.42, f32[32,128]{1,0:T(8,128)S(1)} %get-tuple-element.94.refs_1_, f32[8,128]{1,0:T(8,128)S(1)} %get-tuple-element.95.refs_2_.sums_ref, f32[32,3,128,128]{3,2,1,0:T(8,128)} %bitcast.14), custom_call_target="tpu_custom_call" | custom-call | flops 3145728 | bytes 4194304 | tf_op jit(solution)/shard_map/pallas_call | solution.py:44
  106.4 3.6 %all-to-all-done.5.notes_ref = f32[8,24,128]{2,1,0:T(8,128)S(1)} async-done(((f32[8,24,128]{2,1,0:T(8,128)}), f32[8,24,128]{2,1,0:T(8,128)S(1)}, u32[]{:S(2)}, u32[]{:S(2)}) %all-to-all-start.5) | async-done | bytes 98336 | tf_op jit(solution)/shard_map/all_to_all | solution.py:487
  110.1 14.0 %all_to_all.35.back_ref = f32[32,4,128]{2,1,0:T(4,128)S(1)} all-to-all(f32[32,4,128]{2,1,0:T(4,128)S(1)} %get-tuple-element.99), channel_id=1, replica_groups=mesh['comm'=8,'stn'=16,'tm'=2] {'stn','tm'}, dimensions={0} | all-to-all | bytes 131072 | tf_op jit(solution)/shard_map/all_to_all | solution.py:404
  124.2 0.7 shard_map.140
  (32 shorter events, 1.6 us)
Async XLA Ops:
  0.6 19.9 %copy-start.2 = (f32[2,8,128]{2,1,0:T(8,128)S(1)}, f32[2,8,128]{2,1,0:T(8,128)}, u32[]{:S(2)}) copy-start(f32[2,8,128]{2,1,0:T(8,128)} %param.14) | copy-start | bytes 24580
  0.6 13.7 %copy-start.3 = (f32[16,128]{1,0:T(8,128)S(1)}, f32[16,128]{1,0:T(8,128)}, u32[]{:S(2)}) copy-start(f32[16,128]{1,0:T(8,128)} %cap_rhs_ref.5) | copy-start | bytes 24580
  0.7 19.8 %copy-start.1 = (f32[2,16,128]{2,1,0:T(8,128)S(1)}, f32[2,16,128]{2,1,0:T(8,128)}, u32[]{:S(2)}) copy-start(f32[2,16,128]{2,1,0:T(8,128)} %param.13) | copy-start | bytes 49156
  3.0 17.5 %all-to-all-start = ((f32[32,16,128]{2,1,0:T(8,128)}), f32[32,16,128]{2,1,0:T(8,128)S(1)}, u32[]{:S(2)}, u32[]{:S(2)}) async-start(f32[32,16,128]{2,1,0:T(8,128)} %get-tuple-element.58), calls=%async_computation | async-start | bytes 524288 | tf_op jit(solution)/shard_map/all_to_all | solution.py:404
  11.6 14.1 %slice-start = ((s8[6291456]{0:T(1024)(128)(4,1)}), s8[2097152]{0:T(1024)(128)(4,1)S(1)}, s32[]{:S(2)}) async-start(s8[6291456]{0:T(1024)(128)(4,1)} %bitcast.15), calls=%async_computation.7 | async-start | bytes 4194304
  20.5 5.2 %slice-start.1 = ((s8[6291456]{0:T(1024)(128)(4,1)}), s8[4194304]{0:T(1024)(128)(4,1)S(1)}, s32[]{:S(2)}) async-start(s8[6291456]{0:T(1024)(128)(4,1)} %bitcast.15), calls=%async_computation.8 | async-start | bytes 8388608
  20.5 19.9 %copy-start = (f32[2,8,128,128]{3,2,1,0:T(8,128)S(1)}, f32[2,8,128,128]{3,2,1,0:T(8,128)}, u32[]{:S(2)}) copy-start(f32[2,8,128,128]{3,2,1,0:T(8,128)} %param.16) | copy-start | bytes 3145732
  24.0 4.9 %collective-permute-start = (f32[24,128]{1,0:T(8,128)S(1)}, f32[24,128]{1,0:T(8,128)S(1)}, u32[]{:S(2)}, u32[]{:S(2)}) collective-permute-start(f32[24,128]{1,0:T(8,128)S(1)} %get-tuple-element.62.note_ref), channel_id=1, source_target_pairs={{0,32},{32,0},{64,96},{96,64},{128,160},{160,128},{192,224},{224,1... | collective-permute-start | bytes 36872 | tf_op jit(solution)/shard_map/ppermute | solution.py:407
  29.0 11.5 %all-to-all-start.1 = ((f32[32,4,128]{2,1,0:T(4,128)}), f32[32,4,128]{2,1,0:T(4,128)S(1)}, u32[]{:S(2)}, u32[]{:S(2)}) async-start(f32[32,4,128]{2,1,0:T(4,128)} %get-tuple-element.64), calls=%async_computation.1 | async-start | bytes 131072 | tf_op jit(solution)/shard_map/all_to_all | solution.py:404
  33.0 9.0 %collective-permute-start.1 = (f32[24,128]{1,0:T(8,128)S(1)}, f32[24,128]{1,0:T(8,128)S(1)}, u32[]{:S(2)}, u32[]{:S(2)}) collective-permute-start(f32[24,128]{1,0:T(8,128)S(1)} %get-tuple-element.68.note_ref), channel_id=1, source_target_pairs={{0,128},{32,160},{64,192},{96,224},{128,0},{160,32},{192,64},{224,... | collective-permute-start | bytes 36872 | tf_op jit(solution)/shard_map/ppermute | solution.py:407
  42.0 13.8 %all-to-all-start.2 = ((f32[32,2,128]{2,1,0:T(2,128)}), f32[32,2,128]{2,1,0:T(2,128)S(1)}, u32[]{:S(2)}, u32[]{:S(2)}) async-start(f32[32,2,128]{2,1,0:T(2,128)} %get-tuple-element.70), calls=%async_computation.2 | async-start | bytes 65536 | tf_op jit(solution)/shard_map/all_to_all | solution.py:404
  48.5 5.6 %collective-permute-start.2 = (f32[24,128]{1,0:T(8,128)S(1)}, f32[24,128]{1,0:T(8,128)S(1)}, u32[]{:S(2)}, u32[]{:S(2)}) collective-permute-start(f32[24,128]{1,0:T(8,128)S(1)} %get-tuple-element.71.half_ref), channel_id=1, source_target_pairs={{0,64},{32,96},{64,0},{96,32},{128,192},{160,224},{192,128},{224,1... | collective-permute-start | bytes 36872 | tf_op jit(solution)/shard_map/ppermute | solution.py:407
  51.5 8.7 %slice-start.2 = ((s8[6291456]{0:T(1024)(128)(4,1)}), s8[2097152]{0:T(1024)(128)(4,1)S(1)}, s32[]{:S(2)}) async-start(s8[6291456]{0:T(1024)(128)(4,1)} %bitcast.18), calls=%async_computation.9 | async-start | bytes 4194304
  55.8 4.4 %slice-start.3 = ((s8[6291456]{0:T(1024)(128)(4,1)}), s8[4194304]{0:T(1024)(128)(4,1)S(1)}, s32[]{:S(2)}) async-start(s8[6291456]{0:T(1024)(128)(4,1)} %bitcast.18), calls=%async_computation.10 | async-start | bytes 8388608
  59.3 4.0 %collective-permute-start.3 = (f32[24,128]{1,0:T(8,128)S(1)}, f32[24,128]{1,0:T(8,128)S(1)}, u32[]{:S(2)}, u32[]{:S(2)}) collective-permute-start(f32[24,128]{1,0:T(8,128)S(1)} %get-tuple-element.77.note_ref), channel_id=1, source_target_pairs={{0,32},{32,0},{64,96},{96,64},{128,160},{160,128},{192,224},{224,1... | collective-permute-start | bytes 36872 | tf_op jit(solution)/shard_map/ppermute | solution.py:407
  63.4 13.6 %all-to-all-start.3 = ((f32[32,4,128]{2,1,0:T(4,128)}), f32[32,4,128]{2,1,0:T(4,128)S(1)}, u32[]{:S(2)}, u32[]{:S(2)}) async-start(f32[32,4,128]{2,1,0:T(4,128)} %get-tuple-element.79), calls=%async_computation.3 | async-start | bytes 131072 | tf_op jit(solution)/shard_map/all_to_all | solution.py:404
  69.7 8.5 %collective-permute-start.4 = (f32[24,128]{1,0:T(8,128)S(1)}, f32[24,128]{1,0:T(8,128)S(1)}, u32[]{:S(2)}, u32[]{:S(2)}) collective-permute-start(f32[24,128]{1,0:T(8,128)S(1)} %get-tuple-element.87.note_ref), channel_id=1, source_target_pairs={{0,128},{32,160},{64,192},{96,224},{128,0},{160,32},{192,64},{224,... | collective-permute-start | bytes 36872 | tf_op jit(solution)/shard_map/ppermute | solution.py:407
  78.2 13.8 %all-to-all-start.4 = ((f32[32,2,128]{2,1,0:T(2,128)}), f32[32,2,128]{2,1,0:T(2,128)S(1)}, u32[]{:S(2)}, u32[]{:S(2)}) async-start(f32[32,2,128]{2,1,0:T(2,128)} %get-tuple-element.89), calls=%async_computation.4 | async-start | bytes 65536 | tf_op jit(solution)/shard_map/all_to_all | solution.py:404
  84.7 4.2 %collective-permute-start.5 = (f32[24,128]{1,0:T(8,128)S(1)}, f32[24,128]{1,0:T(8,128)S(1)}, u32[]{:S(2)}, u32[]{:S(2)}) collective-permute-start(f32[24,128]{1,0:T(8,128)S(1)} %get-tuple-element.91.half_ref), channel_id=1, source_target_pairs={{0,64},{32,96},{64,0},{96,32},{128,192},{160,224},{192,128},{224,1... | collective-permute-start | bytes 36872 | tf_op jit(solution)/shard_map/ppermute | solution.py:407
  96.1 13.9 %all-to-all-start.5 = ((f32[8,24,128]{2,1,0:T(8,128)}), f32[8,24,128]{2,1,0:T(8,128)S(1)}, u32[]{:S(2)}, u32[]{:S(2)}) async-start(f32[8,24,128]{2,1,0:T(8,128)} %get-tuple-element.97), calls=%async_computation.5 | async-start | bytes 196608 | tf_op jit(solution)/shard_map/all_to_all | solution.py:487
